TPU v7x, 32 devices: a whole 2x2x4 slice. The times are simulated.
32 devices in a mesh: ctx: 8 (over y, x, core), fsdp: 4 (over z).
Axes of the slice: x: 2, y: 2, z: 4, core: 2. Of those that a mesh axis runs over, the one named last changes fastest.
Arguments:
- hidden_in: bfloat16 [4, 4096, 768], P('fsdp', 'ctx'), may hold values from -6 to 6
- token_ids: int32 [4, 4096], P('fsdp', 'ctx'), may hold values from 0 to 50303, as said below
- hash_table: int32 [50304], replicated, may hold values from 0 to 31, as said below
- deal_order: int32 [8], replicated, may hold values from 0 to 7, each once
- qkv_weight: bfloat16 [768, 2304], P('fsdp'), may hold values from -0.21875 to 0.21875
- out_weight: bfloat16 [768, 768], P('fsdp'), may hold values from -6 to 6
- norm1_gain: bfloat16 [768], P('fsdp'), may hold values from 0.5 to 1.5
- norm1_bias: bfloat16 [768], P('fsdp'), may hold values from -1 to 1
- norm2_gain: bfloat16 [768], P('fsdp'), may hold values from 0.5 to 1.5
- norm2_bias: bfloat16 [768], P('fsdp'), may hold values from -1 to 1
- expert_in: bfloat16 [32, 768, 3072], P('ctx', None, 'fsdp'), may hold values from -0.21875 to 0.21875
- expert_out: bfloat16 [32, 768, 3072], P('ctx', None, 'fsdp'), may hold values from -0.109375 to 0.109375
- out_grad: bfloat16 [4, 4096, 768], P('fsdp', 'ctx'), may hold values from -6 to 6
Outputs:
- layer_out: bfloat16 [4, 4096, 768], P('fsdp', 'ctx')
- grad_hidden: float32 [4, 4096, 768], P('fsdp', 'ctx')
- grad_qkv: float32 [768, 2304], P('fsdp')
- grad_out_weight: float32 [768, 768], P('fsdp')
- grad_norm1_gain: float32 [768], P('fsdp')
- grad_norm1_bias: float32 [768], P('fsdp')
- grad_norm2_gain: float32 [768], P('fsdp')
- grad_norm2_bias: float32 [768], P('fsdp')
- grad_expert_in: float32 [32, 768, 3072], P('ctx', None, 'fsdp')
- grad_expert_out: float32 [32, 768, 3072], P('ctx', None, 'fsdp')
Inputs may be any that keep to these rules, and one draw needn't show every extreme that they name: `token_ids`: in each aligned block of 512 rows of a sequence (the rows of one device), no expert e = hash_table[id] is named by more than 32 tokens, and some expert by exactly 32. `hash_table`: every expert is the value of exactly 1572 token ids.
All inputs are finite; a program needn't handle non-finite values.
Results may differ from a plain program's by a relative error of at most 0.02.
Values may be sent and summed in bfloat16 or wider, within the bound.
No kernel may reach another device: no remote copies, remote signals or barrier semaphores. Data moves between devices by JAX's collectives and lax.ppermute only.
A program may use at most 320 MiB of HBM per device.

v0:
```python
from functools import partial

import jax
import jax.numpy as jnp
from jax import lax
from jax.sharding import PartitionSpec as P

HEADS = 12
HD = 64
BLK = 256
PAIRS = 1
TOK_DEV = 512


epsilon = 1e-05
masked_value = -1e30


def layer_norm(values, norm_gain, norm_bias):
    center = jnp.mean(values, axis=-1, keepdims=True)
    offset = values - center
    spread = jnp.mean(offset * offset, axis=-1, keepdims=True)
    return offset * lax.rsqrt(spread + epsilon) * norm_gain + norm_bias


def block_numbers(deal_order, devices):
    pair_table = deal_order.reshape(devices, PAIRS)
    block_table = jnp.concatenate([pair_table, 2 * PAIRS * devices - 1 - pair_table], axis=1)
    return jnp.repeat(block_table.reshape(-1), BLK)


def block_rows():
    return 512


def block_scores(query_heads, query_ids, key_part, key_ids):
    key_heads = key_part.reshape(key_part.shape[0], HEADS, HD)
    scores = jnp.einsum(
        "qhd,khd->hqk", query_heads, key_heads, preferred_element_type=jnp.float32
    ) * HD ** (-0.5)
    allowed = key_ids[None, None, :] <= query_ids[None, :, None]
    return (scores, allowed)


def block_probs(query_heads, query_ids, log_total, key_rows, key_ids, model_width):
    scores, allowed = block_scores(query_heads, query_ids, key_rows[:, :model_width], key_ids)
    return jnp.where(allowed, jnp.exp(scores - log_total[..., None]), 0.0)


def score_grads(probabilities, grad_heads, value_rows, row_delta):
    value_heads = value_rows.reshape(value_rows.shape[0], HEADS, HD)
    grad_probs = jnp.einsum(
        "qhd,khd->hqk", grad_heads, value_heads, preferred_element_type=jnp.float32
    )
    return (probabilities * (grad_probs - row_delta[..., None])).astype(jnp.bfloat16)


def forward_fold(fold_state, key_piece, query_heads, query_ids, all_ids):
    row_count = key_piece.shape[0]
    step_rows = block_rows()
    model_width = key_piece.shape[1] // 2
    piece_blocks = key_piece.reshape(row_count // step_rows, step_rows, 2 * model_width)
    id_blocks = all_ids.reshape(row_count // step_rows, step_rows)

    def forward_one_block(running, block_item):
        running_max, running_sum, running_acc = running
        key_rows, key_ids = block_item
        scores, allowed = block_scores(query_heads, query_ids, key_rows[:, :model_width], key_ids)
        scores = jnp.where(allowed, scores, masked_value)
        new_max = jnp.maximum(running_max, jnp.max(scores, axis=-1))
        factor = jnp.exp(running_max - new_max)
        weights = jnp.where(allowed, jnp.exp(scores - new_max[..., None]), 0.0)
        value_heads = key_rows[:, model_width:].reshape(step_rows, HEADS, HD)
        update = jnp.einsum(
            "hqk,khd->hqd",
            weights.astype(jnp.bfloat16),
            value_heads,
            preferred_element_type=jnp.float32,
        )
        return (
            (
                new_max,
                running_sum * factor + jnp.sum(weights, axis=-1),
                running_acc * factor[..., None] + update,
            ),
            None,
        )

    fold_state, unused_out = lax.scan(forward_one_block, fold_state, (piece_blocks, id_blocks))
    return fold_state


def query_grads(query_heads, query_ids, grad_heads, log_total, row_delta, key_rows_all, all_ids):
    row_count = key_rows_all.shape[0]
    step_rows = block_rows()
    model_width = key_rows_all.shape[1] // 2
    row_blocks = key_rows_all.reshape(row_count // step_rows, step_rows, 2 * model_width)
    id_blocks = all_ids.reshape(row_count // step_rows, step_rows)

    def query_one_block(running_total, block_item):
        key_rows, key_ids = block_item
        probabilities = block_probs(
            query_heads, query_ids, log_total, key_rows, key_ids, model_width
        )
        grad_scores = score_grads(probabilities, grad_heads, key_rows[:, model_width:], row_delta)
        key_heads = key_rows[:, :model_width].reshape(step_rows, HEADS, HD)
        return (
            running_total
            + jnp.einsum(
                "hqk,khd->qhd", grad_scores, key_heads, preferred_element_type=jnp.float32
            ),
            None,
        )

    start_total = jnp.zeros((query_heads.shape[0], HEADS, HD), jnp.float32)
    running_total, unused_out = lax.scan(query_one_block, start_total, (row_blocks, id_blocks))
    return running_total * HD ** (-0.5)


def key_grads(
    row_count, query_heads, query_ids, grad_heads, log_total, row_delta, key_rows_all, all_ids
):
    model_width = key_rows_all.shape[1] // 2
    step_rows = block_rows()
    row_blocks = key_rows_all.reshape(row_count // step_rows, step_rows, 2 * model_width)
    id_blocks = all_ids.reshape(row_count // step_rows, step_rows)

    def key_one_block(block_item):
        key_rows, key_ids = block_item
        probabilities = block_probs(
            query_heads, query_ids, log_total, key_rows, key_ids, model_width
        )
        grad_values = jnp.einsum(
            "hqk,qhd->khd",
            probabilities.astype(jnp.bfloat16),
            grad_heads,
            preferred_element_type=jnp.float32,
        )
        grad_scores = score_grads(probabilities, grad_heads, key_rows[:, model_width:], row_delta)
        grad_keys = jnp.einsum(
            "hqk,qhd->khd", grad_scores, query_heads, preferred_element_type=jnp.float32
        ) * HD ** (-0.5)
        return jnp.concatenate(
            [
                grad_keys.reshape(step_rows, model_width),
                grad_values.reshape(step_rows, model_width),
            ],
            axis=1,
        )

    stacked = lax.map(key_one_block, (row_blocks, id_blocks))
    return stacked.reshape(row_count, 2 * model_width)


def local(
    hidden_in,
    token_ids,
    hash_table,
    deal_order,
    qkv_weight,
    out_weight,
    norm1_gain,
    norm1_bias,
    norm2_gain,
    norm2_bias,
    expert_in,
    expert_out,
    out_grad,
):
    devices = lax.axis_size("ctx")
    position = lax.axis_index("ctx")
    model_width = hidden_in.shape[2]
    local_experts = expert_in.shape[0]
    experts = local_experts * devices
    capacity = 2 * TOK_DEV // experts
    all_ids = block_numbers(deal_order, devices)
    query_ids = lax.dynamic_slice_in_dim(all_ids, position * TOK_DEV, TOK_DEV)
    qkv_full, out_full, gain_one, bias_one, gain_two, bias_two = (
        lax.all_gather(qkv_weight, "fsdp", axis=0, tiled=True),
        lax.all_gather(out_weight, "fsdp", axis=0, tiled=True),
        lax.all_gather(norm1_gain, "fsdp", axis=0, tiled=True),
        lax.all_gather(norm1_bias, "fsdp", axis=0, tiled=True),
        lax.all_gather(norm2_gain, "fsdp", axis=0, tiled=True),
        lax.all_gather(norm2_bias, "fsdp", axis=0, tiled=True),
    )
    gain_one = gain_one.astype(jnp.float32)
    bias_one = bias_one.astype(jnp.float32)
    gain_two = gain_two.astype(jnp.float32)
    bias_two = bias_two.astype(jnp.float32)
    inputs = hidden_in[0].astype(jnp.float32)
    norm_one_value, norm_one_pull = jax.vjp(layer_norm, inputs, gain_one, bias_one)
    normed_one = norm_one_value.astype(jnp.bfloat16)
    projected = jnp.dot(normed_one, qkv_full, preferred_element_type=jnp.float32).astype(
        jnp.bfloat16
    )
    query_heads = projected[:, :model_width].reshape(TOK_DEV, HEADS, HD)
    key_values = projected[:, model_width:]
    start_state = (
        jnp.full((HEADS, TOK_DEV), masked_value, jnp.float32),
        jnp.zeros((HEADS, TOK_DEV), jnp.float32),
        jnp.zeros((HEADS, TOK_DEV, HD), jnp.float32),
    )
    final_state = forward_fold(
        start_state,
        lax.all_gather(key_values, "ctx", axis=0, tiled=True),
        query_heads,
        query_ids,
        all_ids,
    )
    running_max, running_sum, running_acc = final_state
    log_total = running_max + jnp.log(running_sum)
    attn_heads = jnp.transpose(running_acc / running_sum[..., None], (1, 0, 2))
    attended = attn_heads.reshape(TOK_DEV, model_width).astype(jnp.bfloat16)
    middle = inputs + jnp.dot(attended, out_full, preferred_element_type=jnp.float32)
    norm_two_value, norm_two_pull = jax.vjp(layer_norm, middle, gain_two, bias_two)
    normed_two = norm_two_value.astype(jnp.bfloat16)
    expert_of = hash_table[token_ids[0]]
    expert_range = jnp.arange(experts, dtype=jnp.int32)
    one_hot = (expert_of[:, None] == expert_range[None, :]).astype(jnp.int32)
    earlier = jnp.sum((jnp.cumsum(one_hot, axis=0) - one_hot) * one_hot, axis=1)
    slot_index = expert_of * capacity + earlier
    outgoing = (
        jnp.zeros((experts * capacity, model_width), jnp.bfloat16).at[slot_index].set(normed_two)
    )
    received = lax.all_to_all(
        outgoing.reshape(experts, capacity, model_width),
        "ctx",
        split_axis=0,
        concat_axis=1,
        tiled=True,
    )
    gelu_tanh = partial(jax.nn.gelu, approximate=True)
    first_full, second_full = (
        lax.all_gather(expert_in, "fsdp", axis=2, tiled=True),
        lax.all_gather(expert_out, "fsdp", axis=2, tiled=True),
    )
    pre_act = jnp.einsum("erd,edf->erf", received, first_full, preferred_element_type=jnp.float32)
    gelu_value, gelu_pull = jax.vjp(gelu_tanh, pre_act)
    activated = gelu_value.astype(jnp.bfloat16)
    expert_y = jnp.einsum(
        "erf,edf->erd", activated, second_full, preferred_element_type=jnp.float32
    ).astype(jnp.bfloat16)
    returned = lax.all_to_all(expert_y, "ctx", split_axis=1, concat_axis=0, tiled=True)
    token_y = returned.reshape(experts * capacity, model_width)[slot_index]
    layer_out = (middle + token_y.astype(jnp.float32)).astype(jnp.bfloat16)
    out_cot = out_grad[0]
    grad_outgoing = (
        jnp.zeros((experts * capacity, model_width), jnp.bfloat16).at[slot_index].set(out_cot)
    )
    grad_received = lax.all_to_all(
        grad_outgoing.reshape(experts, capacity, model_width),
        "ctx",
        split_axis=0,
        concat_axis=1,
        tiled=True,
    )
    grad_act = jnp.einsum(
        "erd,edf->erf", grad_received, second_full, preferred_element_type=jnp.float32
    )
    grad_pre = gelu_pull(grad_act)[0].astype(jnp.bfloat16)
    grad_tokens = jnp.einsum(
        "erf,edf->erd", grad_pre, first_full, preferred_element_type=jnp.float32
    ).astype(jnp.bfloat16)
    act_part = lax.slice_in_dim(activated, 0, lax.axis_size("fsdp") * expert_in.shape[2], axis=2)
    grad_first = jnp.einsum("erf,erd->fed", grad_pre, received, preferred_element_type=jnp.float32)
    grad_second = jnp.einsum(
        "erf,erd->fed", act_part, grad_received, preferred_element_type=jnp.float32
    )
    weight_sums = lax.psum_scatter(
        jnp.stack([grad_first, grad_second], axis=2).astype(jnp.bfloat16),
        "fsdp",
        scatter_dimension=0,
        tiled=True,
    ).astype(jnp.float32)
    grad_expert_in = jnp.transpose(weight_sums[:, :, 0, :], (1, 2, 0))
    grad_expert_out = jnp.transpose(weight_sums[:, :, 1, :], (1, 2, 0))
    grad_back = lax.all_to_all(grad_tokens, "ctx", split_axis=1, concat_axis=0, tiled=True)
    grad_normed_two = grad_back.reshape(experts * capacity, model_width)[slot_index].astype(
        jnp.float32
    )
    grad_middle, grad_gain_two, grad_bias_two = norm_two_pull(grad_normed_two)
    grad_middle = grad_middle + out_cot.astype(jnp.float32)
    grad_branch = grad_middle.astype(jnp.bfloat16)
    grad_out_full = jnp.einsum(
        "td,te->de", attended, grad_branch, preferred_element_type=jnp.float32
    )
    grad_attended = jnp.einsum(
        "te,de->td", grad_branch, out_full, preferred_element_type=jnp.float32
    ).astype(jnp.bfloat16)
    grad_heads = grad_attended.reshape(TOK_DEV, HEADS, HD)
    row_delta = jnp.transpose(jnp.sum(grad_heads.astype(jnp.float32) * attn_heads, axis=-1))
    key_rows_all = lax.all_gather(key_values, "ctx", axis=0, tiled=True)
    grad_query = query_grads(
        query_heads, query_ids, grad_heads, log_total, row_delta, key_rows_all, all_ids
    )
    grad_key_values = lax.psum_scatter(
        key_grads(
            lax.axis_size("ctx") * TOK_DEV,
            query_heads,
            query_ids,
            grad_heads,
            log_total,
            row_delta,
            key_rows_all,
            all_ids,
        ).astype(jnp.bfloat16),
        "ctx",
        scatter_dimension=0,
        tiled=True,
    ).astype(jnp.float32)
    grad_projected = jnp.concatenate(
        [grad_query.reshape(TOK_DEV, model_width), grad_key_values], axis=1
    ).astype(jnp.bfloat16)
    grad_qkv_full = jnp.einsum(
        "td,tf->df", normed_one, grad_projected, preferred_element_type=jnp.float32
    )
    grad_normed_one = jnp.einsum(
        "tf,df->td", grad_projected, qkv_full, preferred_element_type=jnp.float32
    )
    grad_inputs, grad_gain_one, grad_bias_one = norm_one_pull(grad_normed_one)
    grad_hidden = (grad_middle + grad_inputs)[None]
    shards = (
        lax.psum_scatter(
            grad_qkv_full.astype(jnp.bfloat16), "fsdp", scatter_dimension=0, tiled=True
        ).astype(jnp.float32),
        lax.psum_scatter(
            grad_out_full.astype(jnp.bfloat16), "fsdp", scatter_dimension=0, tiled=True
        ).astype(jnp.float32),
        lax.psum_scatter(
            grad_gain_one.astype(jnp.bfloat16), "fsdp", scatter_dimension=0, tiled=True
        ).astype(jnp.float32),
        lax.psum_scatter(
            grad_bias_one.astype(jnp.bfloat16), "fsdp", scatter_dimension=0, tiled=True
        ).astype(jnp.float32),
        lax.psum_scatter(
            grad_gain_two.astype(jnp.bfloat16), "fsdp", scatter_dimension=0, tiled=True
        ).astype(jnp.float32),
        lax.psum_scatter(
            grad_bias_two.astype(jnp.bfloat16), "fsdp", scatter_dimension=0, tiled=True
        ).astype(jnp.float32),
    )
    totals = (
        lax.psum(shards[0].astype(jnp.bfloat16), "ctx").astype(jnp.float32),
        lax.psum(shards[1].astype(jnp.bfloat16), "ctx").astype(jnp.float32),
        lax.psum(shards[2].astype(jnp.bfloat16), "ctx").astype(jnp.float32),
        lax.psum(shards[3].astype(jnp.bfloat16), "ctx").astype(jnp.float32),
        lax.psum(shards[4].astype(jnp.bfloat16), "ctx").astype(jnp.float32),
        lax.psum(shards[5].astype(jnp.bfloat16), "ctx").astype(jnp.float32),
    )
    return (
        layer_out[None],
        grad_hidden,
        totals[0],
        totals[1],
        totals[2],
        totals[3],
        totals[4],
        totals[5],
        grad_expert_in,
        grad_expert_out,
    )


def solution(mesh):
    return jax.shard_map(
        local,
        mesh=mesh,
        in_specs=(
            P("fsdp", "ctx", None),
            P("fsdp", "ctx"),
            P(),
            P(),
            P("fsdp", None),
            P("fsdp", None),
            P("fsdp"),
            P("fsdp"),
            P("fsdp"),
            P("fsdp"),
            P("ctx", None, "fsdp"),
            P("ctx", None, "fsdp"),
            P("fsdp", "ctx", None),
        ),
        out_specs=(
            P("fsdp", "ctx", None),
            P("fsdp", "ctx", None),
            P("fsdp", None),
            P("fsdp", None),
            P("fsdp"),
            P("fsdp"),
            P("fsdp"),
            P("fsdp"),
            P("ctx", None, "fsdp"),
            P("ctx", None, "fsdp"),
        ),
        check_vma=False,
    )
```

profile of v0, /device:TPU:0, one launch (start us, length us, event | category | flops | bytes accessed | tf_op | source)
XLA Modules:
  0.0 2081.1 jit_solution(2910632314486827425)
XLA Ops:
  13.3 13.8 all-reduce.11
  30.1 52.4 %all-gather.6.cloned.1.call-done = bf16[768,2304]{1,0:T(8,128)(2,1)} async-done(((bf16[192,2304]{1,0:T(8,128)(2,1)}), bf16[768,2304]{1,0:T(8,128)(2,1)}) %all-gather.6.cloned.1.call-update) | async-done | bytes 3538960 | tf_op jit(solution)/shard_map/all_gather | solution.py:179
  104.1 29.7 %all-to-all-done.2 = bf16[32,32,768]{2,1,0:T(8,128)(2,1)S(1)} async-done(((bf16[32,32,768]{2,1,0:T(8,128)(2,1)}), bf16[32,32,768]{2,1,0:T(8,128)(2,1)S(1)}, u32[]{:S(2)}, u32[]{:S(2)}) %all-to-all-start.2) | async-done | bytes 1572896 | tf_op jit(solution)/shard_map/all_to_all | solution.py:250
  135.4 41.6 %all-gather.8.cloned.1.call-done = bf16[4096,1536]{1,0:T(8,128)(2,1)} async-done(((bf16[512,1536]{1,0:T(8,128)(2,1)}), bf16[4096,1536]{1,0:T(8,128)(2,1)}) %all-gather.8.cloned.1.call-update) | async-done | bytes 12582928 | tf_op jit(solution)/shard_map/all_gather | solution.py:205
  177.0 16.7 copy.85
  193.8 180.2 %while.37 = (s32[]{:T(128)}, f32[12,512]{1,0:T(8,128)S(1)}, f32[12,512]{1,0:T(8,128)S(1)}, f32[12,512,64]{1,2,0:T(8,128)}, s32[8,512]{1,0:T(8,128)S(1)}, /*index...) while((s32[]{:T(128)}, f32[12,512]{1,0:T(8,128)S(1)}, ...), condition=%wide.region_5.6_spmd.clone, body=%wide.region_2.5_spmd.clone.sunk | while | flops 847673344 | bytes 101327000 | solution.py:89
  387.9 144.4 %all-gather.14.cloned.1.call-done = bf16[4,768,3072]{2,1,0:T(8,128)(2,1)} async-done(((bf16[4,768,768]{2,1,0:T(8,128)(2,1)}), bf16[4,768,3072]{2,1,0:T(8,128)(2,1)}) %all-gather.14.cloned.1.call-update) | async-done | bytes 18874384 | tf_op jit(solution)/shard_map/all_gather | solution.py:235
  532.3 15.4 fusion.97
  549.3 305.8 %all-gather.12.cloned.1.call-done = bf16[4,768,3072]{2,1,0:T(8,128)(2,1)} async-done(((bf16[4,768,768]{2,1,0:T(8,128)(2,1)}), bf16[4,768,3072]{2,1,0:T(8,128)(2,1)}) %all-gather.12.cloned.1.call-update) | async-done | bytes 18874384 | tf_op jit(solution)/shard_map/all_gather | solution.py:234
  855.2 22.3 %fusion.46 = (bf16[4,256,3072]{2,1,0:T(8,128)(2,1)}, f32[4,256,3072]{2,1,0:T(8,128)}) fusion(f32[4,256,3072]{2,1,0:T(8,128)} %fusion.97, bf16[4,256,768]{2,1,0:T(8,128)(2,1)S(1)} %bitcast.318, bf16[4,768,3072]{2,1,0:T(8,128)(2,1)} %all-gather.12.cloned.1.call-done), kind=kOutput, calls=%fused_computation.66 | convolution fusion | flops 4894752768 | bytes 51904512 | tf_op jit(solution)/shard_map/erd,edf->erf/dot_general | solution.py:237
  877.4 11.0 convolution_convert_fusion.2
  894.8 14.4 convolution_convert_fusion.3
  926.9 14.1 all-to-all-done.1
  954.7 194.7 %while.36 = (s32[]{:T(128)}, bf16[8,512,1536]{2,1,0:T(8,128)(2,1)}, s32[8,512]{1,0:T(8,128)S(1)}, s32[512]{0:T(512)S(1)}, bf16[8,512,1536]{1,2,0:T(8,128)(2,1)},...) while((s32[]{:T(128)}, bf16[8,512,1536]{2,1,0:T(8,128)(2,1)}, ...), condition=%wide.region_19.20_spmd, body=%wide.region_18.19_spmd.sunk | while | flops 1646264320 | bytes 121454848 | solution.py:151
  966.0 10.9 fusion.170
  1152.7 142.6 %while.38 = (s32[]{:T(128)}, f32[512,12,64]{0,2,1:T(8,128)}, bf16[8,512,1536]{1,2,0:T(8,128)(2,1)}, s32[8,512]{1,0:T(8,128)S(1)}, s32[512]{0:T(512)S(1)}, /*inde...) while((s32[]{:T(128)}, f32[512,12,64]{0,2,1:T(8,128)}, ...), condition=%wide.region_17.18_spmd.clone, body=%wide.region_16.17_spmd.clone.sunk | while | flops 1227882496 | bytes 39116932 | solution.py:116
  1302.8 11.9 convert_bitcast_fusion.1
  1314.7 12.1 convert_bitcast_fusion
  1326.9 40.3 %reduce-scatter.7.cloned.1.call-done = bf16[192,2304]{1,0:T(8,128)(2,1)} async-done(((bf16[768,2304]{1,0:T(8,128)(2,1)}), bf16[192,2304]{1,0:T(8,128)(2,1)}) %reduce-scatter.7.cloned.1.call-update) | async-done | bytes 884752 | tf_op jit(solution)/shard_map/reduce_scatter | solution.py:323
  1367.3 26.0 %pad_maximum_fusion = bf16[3072,4,2,768]{0,3,1,2:T(8,128)(2,1)} fusion(bf16[3072,4,1,768]{0,3,1,2:T(8,128)(2,1)} %convert_bitcast_fusion, bf16[3072,4,1,768]{0,3,1,2:T(8,128)(2,1)} %convert_bitcast_fusion.1), kind=kLoop, calls=%fused_computation.55 | loop fusion | flops 18874368 | bytes 75497472 | tf_op jit(solution)/shard_map/stack | solution.py:270
  1412.3 12.2 all-reduce.8
  1433.5 615.3 %reduce-scatter.11.cloned.1.call-done = bf16[768,4,2,768]{0,3,1,2:T(8,128)(2,1)} async-done(((bf16[3072,4,2,768]{0,3,1,2:T(8,128)(2,1)}), bf16[768,4,2,768]{0,3,1,2:T(8,128)(2,1)}) %reduce-scatter.11.cloned.1.call-update) | async-done | bytes 9437200 | tf_op jit(solution)/shard_map/reduce_scatter | solution.py:269
  2048.8 11.9 convert_element_type.180
  2060.6 13.3 slice_bitcast_fusion
  (503 shorter events, 627.3 us)
Async XLA Ops:
  7.2 83.6 %copy-start = (s32[50304]{0:T(1024)S(1)}, s32[50304]{0:T(1024)}, u32[]{:S(2)}) copy-start(s32[50304]{0:T(1024)} %param.21) | copy-start | bytes 603652
  7.2 75.3 %copy-start.10 = (bf16[1,512,768]{2,1,0:T(8,128)(2,1)S(1)}, bf16[1,512,768]{2,1,0:T(8,128)(2,1)}, u32[]{:S(2)}) copy-start(bf16[1,512,768]{2,1,0:T(8,128)(2,1)} %param.19) | copy-start | bytes 2359300
  7.2 75.3 %all-gather.6.cloned.1.call-start = ((), (), s32[]{:S(2)}) async-start(), calls=%async_computation.8 | async-start | bytes 4423680 | tf_op jit(solution)/shard_map/all_gather | solution.py:179
  7.9 169.1 %all-gather.8.cloned.1.call-start = ((), (), s32[]{:S(2)}) async-start(), calls=%async_computation.9 | async-start | bytes 14155776 | tf_op jit(solution)/shard_map/all_gather | solution.py:205
  27.2 59.4 %copy-start.40 = (f32[768]{0:T(1024)}, f32[768]{0:T(1024)S(1)}, u32[]{:S(2)}) copy-start(f32[768]{0:T(1024)S(1)} %convert_element_type.146) | copy-start | bytes 9220
  27.2 59.4 %copy-start.29 = (f32[768]{0:T(1024)}, f32[768]{0:T(1024)S(1)}, u32[]{:S(2)}) copy-start(f32[768]{0:T(1024)S(1)} %convert_element_type.145) | copy-start | bytes 9220
  28.6 58.1 %copy-start.31 = (f32[512]{0:T(512)}, f32[512]{0:T(512)S(1)}, u32[]{:S(2)}) copy-start(f32[512]{0:T(512)S(1)} %broadcast_multiply_fusion.1) | copy-start | bytes 6148
  30.1 56.6 %copy-start.37 = (f32[512]{0:T(512)}, f32[512]{0:T(512)S(1)}, u32[]{:S(2)}) copy-start(f32[512]{0:T(512)S(1)} %fusion.61) | copy-start | bytes 6148
  30.1 56.6 %copy-start.33 = (f32[512]{0:T(512)}, f32[512]{0:T(512)S(1)}, u32[]{:S(2)}) copy-start(f32[512]{0:T(512)S(1)} %fusion.81) | copy-start | bytes 6148
  89.4 287.1 %all-gather.10.cloned.1.call-start = ((), (), s32[]{:S(2)}) async-start(), calls=%async_computation.10 | async-start | bytes 1474560 | tf_op jit(solution)/shard_map/all_gather | solution.py:180
  90.1 442.1 %all-gather.14.cloned.1.call-start = ((), (), s32[]{:S(2)}) async-start(), calls=%async_computation.12 | async-start | bytes 23592960 | tf_op jit(solution)/shard_map/all_gather | solution.py:235
  99.4 34.4 %all-to-all-start.2 = ((bf16[32,32,768]{2,1,0:T(8,128)(2,1)}), bf16[32,32,768]{2,1,0:T(8,128)(2,1)S(1)}, u32[]{:S(2)}, u32[]{:S(2)}) async-start(bf16[32,32,768]{2,1,0:T(8,128)(2,1)} %bitcast.321), calls=%async_computation.2 | async-start | bytes 3145728 | tf_op jit(solution)/shard_map/all_to_all | solution.py:250
  103.0 752.1 %all-gather.12.cloned.1.call-start = ((), (), s32[]{:S(2)}) async-start(), calls=%async_computation.11 | async-start | bytes 23592960 | tf_op jit(solution)/shard_map/all_gather | solution.py:234
  383.2 149.0 %copy-start.18 = (bf16[4,8,32,768]{3,2,1,0:T(8,128)(2,1)S(1)}, bf16[4,8,32,768]{3,2,1,0:T(8,128)(2,1)}, u32[]{:S(2)}) copy-start(bf16[4,8,32,768]{3,2,1,0:T(8,128)(2,1)} %copy.90) | copy-start | bytes 4718596
  383.2 164.4 %all-to-all-start = ((bf16[32,32,768]{2,1,0:T(8,128)(2,1)}), bf16[32,32,768]{2,1,0:T(8,128)(2,1)}, u32[]{:S(2)}, u32[]{:S(2)}) async-start(bf16[32,32,768]{2,1,0:T(8,128)(2,1)} %bitcast.323), calls=%async_computation | async-start | bytes 3145728 | tf_op jit(solution)/shard_map/all_to_all | solution.py:225
  549.3 328.1 %copy-start.20 = (bf16[4,8,32,768]{3,2,1,0:T(8,128)(2,1)}, bf16[4,8,32,768]{3,2,1,0:T(8,128)(2,1)S(1)}, u32[]{:S(2)}) copy-start(bf16[4,8,32,768]{3,2,1,0:T(8,128)(2,1)S(1)} %copy.87) | copy-start | bytes 4718596
  890.8 25.0 %all-to-all-start.3 = ((bf16[4,256,768]{2,0,1:T(4,128)(2,1)}), bf16[4,256,768]{2,0,1:T(4,128)(2,1)S(1)}, u32[]{:S(2)}, u32[]{:S(2)}) async-start(bf16[4,256,768]{2,0,1:T(4,128)(2,1)} %copy.91), calls=%async_computation.3 | async-start | bytes 3145728 | tf_op jit(solution)/shard_map/all_to_all | solution.py:277
  915.7 25.3 %all-to-all-start.1 = ((bf16[4,256,768]{2,0,1:T(4,128)(2,1)}), bf16[4,256,768]{2,0,1:T(4,128)(2,1)}, u32[]{:S(2)}, u32[]{:S(2)}) async-start(bf16[4,256,768]{2,0,1:T(4,128)(2,1)} %copy.88), calls=%async_computation.1 | async-start | bytes 3145728 | tf_op jit(solution)/shard_map/all_to_all | solution.py:243
  920.0 377.2 %reduce-scatter.5.cloned.1.call-start = ((), (), s32[]{:S(2)}) async-start(), calls=%async_computation.13 | async-start | bytes 14155776 | tf_op jit(solution)/shard_map/reduce_scatter | solution.py:296
  1149.4 177.5 %reduce-scatter.9.cloned.1.call-start = ((), (), s32[]{:S(2)}) async-start(), calls=%async_computation.15 | async-start | bytes 1474560 | tf_op jit(solution)/shard_map/reduce_scatter | solution.py:326
  1152.6 214.6 %reduce-scatter.7.cloned.1.call-start = ((), (), s32[]{:S(2)}) async-start(), calls=%async_computation.14 | async-start | bytes 4423680 | tf_op jit(solution)/shard_map/reduce_scatter | solution.py:323
  1302.8 127.3 %all-reduce.14.cloned.1.call-start = ((), (), s32[]{:S(2)}) async-start(), calls=%async_computation.17 | async-start | bytes 2359296 | tf_op jit(solution)/shard_map/psum | solution.py:343
  1367.2 681.5 %reduce-scatter.11.cloned.1.call-start = ((), (), s32[]{:S(2)}) async-start(), calls=%async_computation.16 | async-start | bytes 47185920 | tf_op jit(solution)/shard_map/reduce_scatter | solution.py:269
  1399.3 27.5 %copy-start.9 = (f32[512,768]{1,0:T(8,128)S(1)}, f32[512,768]{1,0:T(8,128)}, u32[]{:S(2)}) copy-start(f32[512,768]{1,0:T(8,128)} %copy-done.8) | copy-start | bytes 4718596
  (78 other events, 431.3 us)
Sparse Core Ops, SparseCore 0:
  9.6 72.8 all-gather.5
  89.5 87.4 all-gather.7
  178.6 30.4 all-gather.9
  210.5 321.7 all-gather.13
  533.7 321.4 all-gather.11
  1149.5 89.4 reduce-scatter.4
  1241.3 29.1 reduce-scatter.8
  1302.9 64.2 reduce-scatter.6
  1370.4 57.6 all-reduce.13
  1430.4 618.2 reduce-scatter.10
where the time goes:
time: 2090 us; the launch traced here: 2080 us
  waiting for transfers between devices  1250 us (60%)
  matrix products  483 us (23%)
  other arithmetic  139 us (7%)
  local copies, waits for them, and re-layouts  138 us (7%)
  blocking collectives  36.8 us (2%)
    reduce_scatter x1, waiting for transfers between devices, local(): lax.psum_scatter(jnp.stack([grad_first, grad_second], axis=2).astype(jnp....  615 us
    all_gather x1, waiting for transfers between devices, local(): lax.all_gather(expert_in, 'fsdp', axis=2, tiled=True)  306 us
    all_gather x1, waiting for transfers between devices, local(): lax.all_gather(expert_out, 'fsdp', axis=2, tiled=True)  144 us
    dot_general x24, matrix products, block_scores(): jnp.einsum('qhd,khd->hqk', query_heads, key_heads, preferred_element_type...  131 us
    dot_general x8, matrix products, key_one_block(): jnp.einsum('hqk,qhd->khd', grad_scores, query_heads, preferred_element_ty...  87.6 us
    dot_general x8, matrix products, query_one_block(): jnp.einsum('hqk,khd->qhd', grad_scores, key_heads, preferred_element_type...  73.4 us
    reduce_sum x8, other arithmetic, forward_one_block(): jnp.sum(weights, axis=-1)  64.7 us
    all_gather x1, waiting for transfers between devices, local(): lax.all_gather(qkv_weight, 'fsdp', axis=0, tiled=True)  52.4 us
  transfers between devices with their start and end apart: 14, of which 9 were waited for; matrix products, arithmetic and copies ran while one was open for 23% of the time, Pallas kernels for 0%

commit v1 on v0

v1 whole, which is shorter than its diff:
```python
from functools import partial

import jax
import jax.numpy as jnp
from jax import lax
from jax.experimental import pallas as pl
from jax.experimental.pallas import tpu as pltpu
from jax.sharding import PartitionSpec as P
from math import gcd

HEADS = 12
HD = 64
BLK = 256
TOK_DEV = 512
epsilon = 1e-05
masked_value = -1e30
bf16 = jnp.bfloat16
f32 = jnp.float32
NT = (((1,), (1,)), ((), ()))
NN = (((1,), (0,)), ((), ()))
TN = (((0,), (0,)), ((), ()))
VMEM_LIMIT = 56 * 1024 * 1024


def dot(a, b, dims=NN):
    return lax.dot_general(a, b, dims, preferred_element_type=f32)


def swap(value, axis, offset):
    size = lax.axis_size(axis)
    return lax.ppermute(value, axis, [(i, i ^ offset) for i in range(size)])


def in_order(pieces, index):
    count, bit = len(pieces), 1
    while bit < count:
        odd = (index & bit) != 0
        pieces = [jnp.where(odd, pieces[i ^ bit], pieces[i]) for i in range(count)]
        bit *= 2
    return pieces


def norm_stats(values):
    center = jnp.mean(values, axis=-1, keepdims=True)
    offset = values - center
    scale = lax.rsqrt(jnp.mean(offset * offset, axis=-1, keepdims=True) + epsilon)
    return offset * scale, scale


def norm_back(normal, scale, gain, grad):
    inner = grad * gain
    return scale * (
        inner
        - jnp.mean(inner, axis=-1, keepdims=True)
        - normal * jnp.mean(inner * normal, axis=-1, keepdims=True)
    )


def masked_heads(rows, heads):
    lane = lax.broadcasted_iota(jnp.int32, rows.shape, 1) // HD
    return [jnp.where(lane == h, rows, jnp.zeros_like(rows)) for h in range(heads)]


def chunk_places(block, step, place_ref):
    first = step * 2
    second = jnp.minimum(first + 1, block)
    bias = jnp.where(first + 1 <= block, 0.0, masked_value).astype(f32)
    return (
        pl.multiple_of(place_ref[first] * BLK, BLK),
        pl.multiple_of(place_ref[second] * BLK, BLK),
        bias,
    )


def attend_kernel(heads, block_ref, place_ref, q_ref, k_ref, vt_ref, att_ref, att_t_ref, lse_ref, acc_ref):
    block = block_ref[pl.program_id(0)]
    queries = masked_heads(q_ref[...], heads)
    acc_ref[...] = jnp.zeros_like(acc_ref)

    def step(index, state):
        top, total = state
        one, two, bias = chunk_places(block, index, place_ref)
        keys = jnp.concatenate([k_ref[pl.ds(one, BLK), :], k_ref[pl.ds(two, BLK), :]], axis=0)
        values = jnp.concatenate([vt_ref[:, pl.ds(one, BLK)], vt_ref[:, pl.ds(two, BLK)]], axis=1)
        tops, totals = [], []
        for h in range(heads):
            scores = dot(keys, queries[h], NT)
            low, high = scores[:BLK], scores[BLK:] + bias
            new_top = jnp.maximum(
                top[h], jnp.max(jnp.maximum(low, high), axis=0, keepdims=True)
            )
            factor = jnp.exp(top[h] - new_top)
            low, high = jnp.exp(low - new_top), jnp.exp(high - new_top)
            tops.append(new_top)
            totals.append(total[h] * factor + jnp.sum(low + high, axis=0, keepdims=True))
            weights = jnp.concatenate([low.astype(bf16), high.astype(bf16)], axis=0)
            rows = slice(h * HD, (h + 1) * HD)
            acc_ref[rows, :] = acc_ref[rows, :] * factor + dot(values[rows, :], weights)
        return tuple(tops), tuple(totals)

    start = (
        tuple(jnp.full((1, BLK), masked_value, f32) for _ in range(heads)),
        tuple(jnp.zeros((1, BLK), f32) for _ in range(heads)),
    )
    top, total = lax.fori_loop(0, (block + 2) // 2, step, start)
    for h in range(heads):
        rows = slice(h * HD, (h + 1) * HD)
        acc_ref[rows, :] = acc_ref[rows, :] / total[h]
        lse_ref[0, h : h + 1, :] = top[h] + jnp.log(total[h])
    att_t_ref[...] = acc_ref[...]
    att_ref[...] = jnp.transpose(acc_ref[...]).astype(bf16)


def attend(block_of, place_of, queries, keys, values_t):
    rows, width = queries.shape
    heads = width // HD
    blocks = rows // BLK
    whole = lambda shape: pl.BlockSpec(shape, lambda i, *_: (0, 0), pipeline_mode=pl.Buffered(1))
    return pl.pallas_call(
        partial(attend_kernel, heads),
        grid_spec=pltpu.PrefetchScalarGridSpec(
            num_scalar_prefetch=2,
            grid=(blocks,),
            in_specs=[
                pl.BlockSpec((BLK, width), lambda i, *_: (i, 0)),
                whole(keys.shape),
                whole(values_t.shape),
            ],
            out_specs=[
                pl.BlockSpec((BLK, width), lambda i, *_: (i, 0)),
                pl.BlockSpec((width, BLK), lambda i, *_: (0, i)),
                pl.BlockSpec((1, heads, BLK), lambda i, *_: (i, 0, 0)),
            ],
            scratch_shapes=[pltpu.VMEM((width, BLK), f32)],
        ),
        out_shape=[
            jax.ShapeDtypeStruct((rows, width), bf16),
            jax.ShapeDtypeStruct((width, rows), f32),
            jax.ShapeDtypeStruct((blocks, heads, BLK), f32),
        ],
        compiler_params=pltpu.CompilerParams(vmem_limit_bytes=VMEM_LIMIT),
        cost_estimate=pl.CostEstimate(
            flops=16 * rows * keys.shape[0] * width,
            bytes_accessed=8 * keys.shape[0] * width,
            transcendentals=rows * keys.shape[0] * heads // 2,
        ),
        name="attend",
    )(block_of, place_of, queries, keys, values_t)


def attend_back_kernel(
    heads, block_ref, place_ref, q_ref, g_ref, att_t_ref, lse_ref, k_ref, v_ref, kt_ref,
    gq_ref, gk_ref, gv_ref, gqt_ref, gk_acc, gv_acc,
):
    turn = pl.program_id(0)
    block = block_ref[turn]

    @pl.when(turn == 0)
    def _():
        gk_acc[...] = jnp.zeros_like(gk_acc)
        gv_acc[...] = jnp.zeros_like(gv_acc)

    queries = masked_heads(q_ref[...], heads)
    grads = masked_heads(g_ref[...], heads)
    prod = jnp.transpose(g_ref[...].astype(f32)) * att_t_ref[...]
    deltas = [jnp.sum(prod[h * HD : (h + 1) * HD], axis=0, keepdims=True) for h in range(heads)]
    logs = [lse_ref[0, h : h + 1, :] for h in range(heads)]
    gqt_ref[...] = jnp.zeros_like(gqt_ref)

    def step(index, carry):
        one, two, bias = chunk_places(block, index, place_ref)
        keys = jnp.concatenate([k_ref[pl.ds(one, BLK), :], k_ref[pl.ds(two, BLK), :]], axis=0)
        values = jnp.concatenate([v_ref[pl.ds(one, BLK), :], v_ref[pl.ds(two, BLK), :]], axis=0)
        keys_t = jnp.concatenate([kt_ref[:, pl.ds(one, BLK)], kt_ref[:, pl.ds(two, BLK)]], axis=1)
        gk, gv = None, None
        for h in range(heads):
            scores = dot(keys, queries[h], NT)
            low = jnp.exp(scores[:BLK] - logs[h])
            high = jnp.exp(scores[BLK:] + (bias - logs[h]))
            probs = jnp.concatenate([low, high], axis=0)
            grad_scores = (probs * (dot(values, grads[h], NT) - deltas[h])).astype(bf16)
            rows = slice(h * HD, (h + 1) * HD)
            gqt_ref[rows, :] += dot(keys_t[rows, :], grad_scores)
            gv_h = dot(probs.astype(bf16), grads[h])
            gk_h = dot(grad_scores, queries[h])
            gk, gv = (gk_h, gv_h) if h == 0 else (gk + gk_h, gv + gv_h)
        gk_acc[pl.ds(one, BLK), :] += gk[:BLK]
        gv_acc[pl.ds(one, BLK), :] += gv[:BLK]
        gk_acc[pl.ds(two, BLK), :] += gk[BLK:]
        gv_acc[pl.ds(two, BLK), :] += gv[BLK:]
        return carry

    lax.fori_loop(0, (block + 2) // 2, step, 0)
    gq_ref[...] = (jnp.transpose(gqt_ref[...]) * HD ** (-0.5)).astype(bf16)

    @pl.when(turn == pl.num_programs(0) - 1)
    def _():
        gk_ref[...] = gk_acc[...].astype(bf16)
        gv_ref[...] = gv_acc[...].astype(bf16)


def attend_back(block_of, place_of, queries, grads, att_t, logs, keys, values, keys_t):
    rows, width = queries.shape
    heads = width // HD
    blocks = rows // BLK
    whole = lambda shape: pl.BlockSpec(shape, lambda i, *_: (0, 0), pipeline_mode=pl.Buffered(1))
    row_spec = pl.BlockSpec((BLK, width), lambda i, *_: (i, 0))
    return pl.pallas_call(
        partial(attend_back_kernel, heads),
        grid_spec=pltpu.PrefetchScalarGridSpec(
            num_scalar_prefetch=2,
            grid=(blocks,),
            in_specs=[
                row_spec,
                row_spec,
                pl.BlockSpec((width, BLK), lambda i, *_: (0, i)),
                pl.BlockSpec((1, heads, BLK), lambda i, *_: (i, 0, 0)),
                whole(keys.shape),
                whole(values.shape),
                whole(keys_t.shape),
            ],
            out_specs=[row_spec, whole(keys.shape), whole(values.shape)],
            scratch_shapes=[
                pltpu.VMEM((width, BLK), f32),
                pltpu.VMEM(keys.shape, f32),
                pltpu.VMEM(values.shape, f32),
            ],
        ),
        out_shape=[
            jax.ShapeDtypeStruct((rows, width), bf16),
            jax.ShapeDtypeStruct(keys.shape, bf16),
            jax.ShapeDtypeStruct(values.shape, bf16),
        ],
        compiler_params=pltpu.CompilerParams(vmem_limit_bytes=VMEM_LIMIT),
        cost_estimate=pl.CostEstimate(
            flops=40 * rows * keys.shape[0] * width,
            bytes_accessed=16 * keys.shape[0] * width,
            transcendentals=rows * keys.shape[0] * heads // 2,
        ),
        name="attend_back",
    )(block_of, place_of, queries, grads, att_t, logs, keys, values, keys_t)


def expert_kernel(x_ref, gy_ref, first_ref, second_ref, act_ref, gpre_ref, gn_ref, ey_ref):
    flat = lambda ref: ref[...].reshape(-1, ref.shape[-1])
    first, second = first_ref[0], second_ref[0]
    pre = dot(flat(x_ref), first)
    inner = 0.7978845608028654 * (pre + 0.044715 * (pre * pre * pre))
    bend = jnp.tanh(inner)
    half = 0.5 * (1.0 + bend)
    act = (pre * half).astype(bf16)
    slope = half + 0.5 * pre * (1.0 - bend * bend) * (
        0.7978845608028654 * (1.0 + 3 * 0.044715 * (pre * pre))
    )
    gpre = (dot(flat(gy_ref), second) * slope).astype(bf16)
    act_ref[...] = act.reshape(act_ref.shape)
    gpre_ref[...] = gpre.reshape(gpre_ref.shape)
    gn_ref[...] = dot(gpre, first, NT).astype(bf16).reshape(gn_ref.shape)
    ey_ref[...] = dot(act, second, NT).astype(bf16).reshape(ey_ref.shape)


def expert_step(tokens, grads, first, second):
    sources, experts, room, width = tokens.shape
    hidden = first.shape[2]
    token_spec = pl.BlockSpec((sources, 1, room, width), lambda e: (0, e, 0, 0))
    hidden_spec = pl.BlockSpec((sources, 1, room, hidden), lambda e: (0, e, 0, 0))
    weight_spec = pl.BlockSpec((1, width, hidden), lambda e: (e, 0, 0))
    like = lambda last: jax.ShapeDtypeStruct((sources, experts, room, last), bf16)
    return pl.pallas_call(
        expert_kernel,
        grid=(experts,),
        in_specs=[token_spec, token_spec, weight_spec, weight_spec],
        out_specs=[hidden_spec, hidden_spec, token_spec, token_spec],
        out_shape=[like(hidden), like(hidden), like(width), like(width)],
        compiler_params=pltpu.CompilerParams(vmem_limit_bytes=VMEM_LIMIT),
        cost_estimate=pl.CostEstimate(
            flops=8 * sources * experts * room * width * hidden,
            bytes_accessed=4 * first.size + 12 * tokens.size,
            transcendentals=sources * experts * room * hidden,
        ),
        name="expert_step",
    )(tokens, grads, first, second)


def expert_grad_kernel(parts, *refs):
    flat = lambda ref: ref[...].reshape(-1, ref.shape[-1])
    stack = lambda some: jnp.concatenate([flat(r) for r in some], axis=0)
    ins, (gfirst_ref, gsecond_ref) = refs[: 4 * parts], refs[4 * parts :]
    tokens, grads, acts, gpres = (stack(ins[i * parts : (i + 1) * parts]) for i in range(4))
    gfirst_ref[0] = dot(tokens, gpres, TN)
    gsecond_ref[0] = dot(grads, acts, TN)


def expert_grads(tokens, grads, acts, gpres):
    parts = len(tokens)
    sources, experts, room, width = tokens[0].shape
    hidden = acts[0].shape[3]
    spec = lambda last: pl.BlockSpec((sources, 1, room, last), lambda e: (0, e, 0, 0))
    out_spec = pl.BlockSpec((1, width, hidden), lambda e: (e, 0, 0))
    out = jax.ShapeDtypeStruct((experts, width, hidden), f32)
    return pl.pallas_call(
        partial(expert_grad_kernel, parts),
        grid=(experts,),
        in_specs=[spec(width)] * (2 * parts) + [spec(hidden)] * (2 * parts),
        out_specs=[out_spec, out_spec],
        out_shape=[out, out],
        compiler_params=pltpu.CompilerParams(vmem_limit_bytes=VMEM_LIMIT),
        cost_estimate=pl.CostEstimate(
            flops=4 * parts * sources * experts * room * width * hidden,
            bytes_accessed=8 * experts * width * hidden,
            transcendentals=0,
        ),
        name="expert_grads",
    )(*tokens, *grads, *acts, *gpres)


def reduce_stage(parts, index, axis, stride):
    count = parts.shape[0]
    pick = lambda k: lax.dynamic_index_in_dim(parts, index ^ k, 0, keepdims=False)
    total = pick(0)
    for k in range(1, count):
        total = total + swap(pick(k).astype(bf16), axis, k * stride).astype(f32)
    return total


def gather_stage(part, count, index, axis, stride):
    pieces = [part] + [swap(part, axis, k * stride) for k in range(1, count)]
    return in_order(pieces, index)


def local(
    hidden_in, token_ids, hash_table, deal_order, qkv_weight, out_weight,
    norm1_gain, norm1_bias, norm2_gain, norm2_bias, expert_in, expert_out, out_grad,
):
    devices = lax.axis_size("ctx")
    position = lax.axis_index("ctx")
    planes = lax.axis_size("fsdp")
    plane = lax.axis_index("fsdp")
    width = hidden_in.shape[2]
    local_experts = expert_in.shape[0]
    experts = local_experts * devices
    room = 2 * TOK_DEV // experts
    groups = gcd(HEADS, devices)
    cores = devices // groups
    group, core = position // cores, position % cores
    span = width // groups

    own_hidden = hidden_in[0]
    out_cot = out_grad[0]

    hidden = jnp.concatenate(
        [own_hidden] + [swap(own_hidden, "ctx", j * cores) for j in range(1, groups)]
    ).astype(f32)

    cut = lambda part: lax.dynamic_slice_in_dim(qkv_weight, part * width + group * span, span, 1)
    own_cols = jnp.concatenate([cut(0), cut(1), cut(2)], axis=1)
    own_vecs = jnp.stack([norm1_gain, norm1_bias, norm2_gain, norm2_bias])
    cols = jnp.concatenate(gather_stage(own_cols, planes, plane, "fsdp", 1))
    vecs = jnp.concatenate(gather_stage(own_vecs, planes, plane, "fsdp", 1), axis=1).astype(f32)
    out_full = jnp.concatenate(gather_stage(out_weight, planes, plane, "fsdp", 1))
    gain_one, bias_one, gain_two, bias_two = (vecs[i] for i in range(4))
    wq, wk, wv = cols[:, :span], cols[:, span : 2 * span], cols[:, 2 * span :]

    expert_of = hash_table[token_ids[0]]
    same = expert_of[:, None] == expert_of[None, :]
    before = lax.broadcasted_iota(jnp.int32, same.shape, 1) < lax.broadcasted_iota(jnp.int32, same.shape, 0)
    rank = jnp.sum((same & before).astype(jnp.int32), axis=1)
    slot = ((expert_of // local_experts) ^ position) * (local_experts * room) + (
        expert_of % local_experts
    ) * room + rank
    slots = [slot, None] + [swap(slot, "fsdp", k) for k in range(2, planes)]
    all_slots = experts * room
    one_hot = lambda s: (
        lax.broadcasted_iota(jnp.int32, (all_slots, TOK_DEV), 0) == s[None, :]
    ).astype(bf16)
    places = [None if s is None else one_hot(s) for s in slots]

    def exchange(rows):
        pieces = rows.reshape(devices, local_experts * room, width)
        got = [pieces[0]] + [swap(pieces[k], "ctx", k) for k in range(1, devices)]
        return jnp.stack(got)

    def dispatch(rows):
        far = [None, None] + [swap(rows, "fsdp", k) for k in range(2, planes)]
        first = exchange(dot(places[0], rows).astype(bf16))
        got = [first, swap(first, "fsdp", 1)]
        for k in range(2, planes):
            got.append(exchange(dot(places[k], far[k]).astype(bf16)))
        return [g.reshape(devices, local_experts, room, width) for g in got]

    def combine(parts):
        parts = [p.reshape(devices, local_experts * room, width) for p in parts]
        total = None
        for k in range(planes - 1, 1, -1):
            back = dot(places[k], exchange(parts[k]).reshape(all_slots, width), TN).astype(bf16)
            back = swap(back, "fsdp", k).astype(f32)
            total = back if total is None else total + back
        near = (parts[0].astype(f32) + swap(parts[1], "fsdp", 1).astype(f32)).astype(bf16)
        near = dot(places[0], exchange(near).reshape(all_slots, width), TN)
        return near if total is None else near + total

    grads_sent = dispatch(out_cot)

    normal_one, scale_one = norm_stats(hidden)
    normed_one = (normal_one * gain_one + bias_one).astype(bf16)
    queries = (dot(normed_one, wq).astype(bf16) * HD ** (-0.5)).astype(bf16)
    own_keys = dot(normed_one, wk).astype(bf16)
    own_values = dot(normed_one, wv).astype(bf16)
    keys = jnp.concatenate([own_keys] + [swap(own_keys, "ctx", k) for k in range(1, cores)])
    values = jnp.concatenate([own_values] + [swap(own_values, "ctx", k) for k in range(1, cores)])
    keys_t, values_t = keys.T, values.T
    low_of = lambda g, s: deal_order[(group ^ g) * cores + (core ^ s)]
    numbers = []
    for s in range(cores):
        for g in range(groups):
            low = low_of(g, s)
            numbers += [low, 2 * devices - 1 - low]
    numbers = jnp.stack(numbers)
    count = 2 * devices
    place_of = jnp.sum(
        jnp.where(
            numbers[None, :] == jnp.arange(count, dtype=jnp.int32)[:, None],
            jnp.arange(count, dtype=jnp.int32)[None, :],
            0,
        ),
        axis=1,
    ).astype(jnp.int32)
    block_of = numbers[: 2 * groups]
    att, att_t, logs = attend(block_of, place_of, queries, keys, values_t)
    atts = [att[:TOK_DEV]] + [
        swap(att[j * TOK_DEV : (j + 1) * TOK_DEV], "ctx", j * cores) for j in range(1, groups)
    ]
    out_rows = [
        lax.dynamic_slice_in_dim(out_full, (group ^ j) * span, span, 0) for j in range(groups)
    ]
    own_float = own_hidden.astype(f32)
    middle = own_float + sum(dot(a, w) for a, w in zip(atts, out_rows))
    normal_two, scale_two = norm_stats(middle)
    normed_two = (normal_two * gain_two + bias_two).astype(bf16)

    tokens_sent = dispatch(normed_two)
    acts, gpres, gnorms, eys = [], [], [], []
    for k in range(planes):
        act, gpre, gn, ey = expert_step(tokens_sent[k], grads_sent[k], expert_in, expert_out)
        acts.append(act)
        gpres.append(gpre)
        gnorms.append(gn)
        eys.append(ey)
    grad_normed_two = combine(gnorms)
    grad_expert_in, grad_expert_out = expert_grads(tokens_sent, grads_sent, acts, gpres)
    token_y = combine(eys)
    layer_out = (middle + token_y).astype(bf16)

    grad_normed_two = grad_normed_two.astype(bf16).astype(f32)
    grad_gain_two = jnp.sum(grad_normed_two * normal_two, axis=0)
    grad_bias_two = jnp.sum(grad_normed_two, axis=0)
    grad_middle = out_cot.astype(f32) + norm_back(normal_two, scale_two, gain_two, grad_normed_two)
    grad_branch = grad_middle.astype(bf16)
    gatts = [dot(grad_branch, w, NT).astype(bf16) for w in out_rows]
    gatt = jnp.concatenate([gatts[0]] + [swap(gatts[j], "ctx", j * cores) for j in range(1, groups)])
    grad_out_rows = in_order([dot(a, grad_branch, TN) for a in atts], group)
    pad = lambda some: jnp.stack(some + [jnp.zeros_like(some[0])] * (128 - len(some)), axis=1)
    outs = jnp.concatenate(
        [jnp.concatenate(grad_out_rows), pad([grad_gain_two, grad_bias_two])], axis=1
    )

    grad_q, grad_k, grad_v = attend_back(
        block_of, place_of, queries, gatt, att_t, logs, keys, values, keys_t
    )
    half = groups * TOK_DEV

    def meet(some):
        total = some[:half].astype(f32)
        for k in range(1, cores):
            total = total + swap(some[k * half : (k + 1) * half], "ctx", k).astype(f32)
        return total.astype(bf16)

    grad_cols = jnp.concatenate([grad_q, meet(grad_k), meet(grad_v)], axis=1)
    grad_rows = dot(grad_cols, cols, NT)
    pieces = [grad_rows[j * TOK_DEV : (j + 1) * TOK_DEV] for j in range(groups)]
    grad_normed_one = pieces[0] + sum(
        swap(pieces[j].astype(bf16), "ctx", j * cores).astype(f32) for j in range(1, groups)
    )
    grad_hidden = grad_middle + norm_back(
        normal_one[:TOK_DEV], scale_one[:TOK_DEV], gain_one, grad_normed_one
    )
    grad_weights = dot(normed_one, grad_cols, TN)
    grad_gain_one = jnp.sum(grad_rows * normal_one, axis=0)
    grad_bias_one = jnp.sum(grad_rows, axis=0)
    mixed = jnp.concatenate([grad_weights, pad([grad_gain_one, grad_bias_one])], axis=1)

    rows = width // planes
    wide = mixed.shape[1]
    part = reduce_stage(
        jnp.moveaxis(mixed.reshape(planes, cores, rows // cores, wide), 1, 0), core, "ctx", 1
    )
    part = reduce_stage(part, plane, "fsdp", 1).astype(bf16)
    part = jnp.stack(gather_stage(part, groups, group, "ctx", cores))
    part = jnp.concatenate(gather_stage(part, cores, core, "ctx", 1), axis=1).astype(f32)
    grad_qkv = jnp.transpose(
        part[:, :, : 3 * span].reshape(groups, rows, 3, span), (1, 2, 0, 3)
    ).reshape(rows, 3 * width)
    vec_one = jnp.sum(part[:, :, 3 * span : 3 * span + 2], axis=0)

    wide = outs.shape[1]
    part = reduce_stage(
        jnp.moveaxis(outs.reshape(planes, cores, rows // cores, wide), 1, 0), core, "ctx", 1
    )
    part = reduce_stage(
        jnp.moveaxis(part.reshape(planes, groups, rows // devices, wide), 1, 0), group, "ctx", cores
    )
    part = reduce_stage(part, plane, "fsdp", 1).astype(bf16)
    part = jnp.concatenate(gather_stage(part, groups, group, "ctx", cores))
    part = jnp.concatenate(gather_stage(part, cores, core, "ctx", 1)).astype(f32)
    grad_out_weight = part[:, :width]
    vec_two = part[:, width : width + 2]
    return (
        layer_out[None],
        grad_hidden[None],
        grad_qkv,
        grad_out_weight,
        vec_one[:, 0],
        vec_one[:, 1],
        vec_two[:, 0],
        vec_two[:, 1],
        grad_expert_in,
        grad_expert_out,
    )


def solution(mesh):
    return jax.shard_map(
        local,
        mesh=mesh,
        in_specs=(
            P("fsdp", "ctx", None),
            P("fsdp", "ctx"),
            P(),
            P(),
            P("fsdp", None),
            P("fsdp", None),
            P("fsdp"),
            P("fsdp"),
            P("fsdp"),
            P("fsdp"),
            P("ctx", None, "fsdp"),
            P("ctx", None, "fsdp"),
            P("fsdp", "ctx", None),
        ),
        out_specs=(
            P("fsdp", "ctx", None),
            P("fsdp", "ctx", None),
            P("fsdp", None),
            P("fsdp", None),
            P("fsdp"),
            P("fsdp"),
            P("fsdp"),
            P("fsdp"),
            P("ctx", None, "fsdp"),
            P("ctx", None, "fsdp"),
        ),
        check_vma=False,
    )
```

time: 2090 us -> 1030 us (0.49)
  waiting for transfers between devices: 1250 us -> 409 us
  matrix products: 483 us -> 50.8 us
  starting transfers between devices: 17.1 us -> 201 us
  Pallas kernels: 0 us -> 172 us
  other arithmetic: 139 us -> 39.4 us
  blocking collectives: 36.8 us -> 0 us
    reduce_scatter x4 -> x0, waiting for transfers between devices: 656 us -> none  [the longest x1 615 us: local(): lax.psum_scatter(jnp.stack([grad_first, grad_second], axis=2).astype(jnp....]
    all_gather x5 -> x0, waiting for transfers between devices: 544 us -> none  [the longest x1 306 us: local(): lax.all_gather(expert_in, 'fsdp', axis=2, tiled=True)]
    dot_general x68 -> x29, matrix products: 483 us -> 50.8 us  [dot(): return lax.dot_general(a, b, dims, preferred_element_type=f32)]
    ppermute x0 -> x142, waiting for transfers between devices: none -> 409 us  [swap(): return lax.ppermute(value, axis, [(i, i ^ offset) for i in range(size)])]
    ppermute x0 -> x142, starting transfers between devices: none -> 201 us  [swap(): return lax.ppermute(value, axis, [(i, i ^ offset) for i in range(size)])]
    pallas_call x0 -> x7, Pallas kernels: none -> 172 us  [the longest x1 65.7 us: attend_back(): pl.pallas_call(partial(attend_back_kernel, heads), grid_spec=pltpu.Prefet...]
    reduce_sum x17 -> x7, other arithmetic: 76.6 us -> 8.47 us  [the longest x2 4.7 us: norm_stats(): jnp.mean(offset * offset, axis=-1, keepdims=True) + epsilon]
    all_to_all x4 -> x0, waiting for transfers between devices: 46.6 us -> none  [the longest x1 29.7 us: local(): lax.all_to_all(grad_outgoing.reshape(experts, capacity, model_width), 'ct...]
  transfers between devices with their start and end apart: 14 -> 142, of which waited for: 9 -> 69; matrix products, arithmetic and copies ran while one was open for 23% -> 21% of each run, Pallas kernels for 0% -> 17%
where the time goes in v1:
time: 1030 us; the launch traced here: 1020 us
  waiting for transfers between devices  409 us (40%)
  starting transfers between devices  201 us (20%)
  Pallas kernels  172 us (17%)
  local copies, waits for them, and re-layouts  141 us (14%)
  matrix products  50.8 us (5%)
  other arithmetic  39.4 us (4%)
    ppermute x142, waiting for transfers between devices, swap(): return lax.ppermute(value, axis, [(i, i ^ offset) for i in range(size)])  409 us
    ppermute x142, starting transfers between devices, swap(): return lax.ppermute(value, axis, [(i, i ^ offset) for i in range(size)])  201 us
    pallas_call x1, Pallas kernels, attend_back(): pl.pallas_call(partial(attend_back_kernel, heads), grid_spec=pltpu.Prefet...  65.7 us
    dot_general x29, matrix products, dot(): return lax.dot_general(a, b, dims, preferred_element_type=f32)  50.8 us
    pallas_call x1, Pallas kernels, attend(): pl.pallas_call(partial(attend_kernel, heads), grid_spec=pltpu.PrefetchSca...  47.4 us
    unnamed x236, local copies, waits for them, and re-layouts  46.6 us
    pallas_call x4, Pallas kernels, expert_step(): pl.pallas_call(expert_kernel, grid=(experts,), in_specs=[token_spec, toke...  41.1 us
  transfers between devices with their start and end apart: 142, of which 69 were waited for; matrix products, arithmetic and copies ran while one was open for 21% of the time, Pallas kernels for 17%

profile of v1, /device:TPU:0, one launch (start us, length us, event | category | flops | bytes accessed | tf_op | source)
XLA Modules:
  0.0 1021.5 jit_solution(10001194081322476507)
XLA Ops:
  67.9 15.9 %collective-permute-done.30 = bf16[128,768]{1,0:T(8,128)(2,1)S(1)} collective-permute-done((bf16[128,768]{1,0:T(8,128)(2,1)S(1)}, bf16[128,768]{1,0:T(8,128)(2,1)S(1)}, u32[]{:S(2)}, u32[]{:S(2)}) %collective-permute-start.30) | collective-permute-done | bytes 196640 | tf_op jit(solution)/shard_map/ppermute | solution.py:31
  95.7 12.0 %collective-permute-start.13 = (bf16[192,768]{1,0:T(8,128)(2,1)S(1)}, bf16[192,768]{1,0:T(8,128)(2,1)S(1)}, u32[]{:S(2)}, u32[]{:S(2)}) collective-permute-start(bf16[192,768]{1,0:T(8,128)(2,1)S(1)} %copy-done.37), channel_id=1, source_target_pairs={{0,1},{1,0},{2,3},{3,2},{4,5},{5,4},{6,7},{7,6},{8,9},{9,8},{10,11... | collective-permute-start | bytes 884744 | tf_op jit(solution)/shard_map/ppermute | solution.py:31
  139.7 35.2 %collective-permute-done.75 = bf16[512,768]{1,0:T(8,128)(2,1)S(1)} collective-permute-done((bf16[512,768]{1,0:T(8,128)(2,1)S(1)}, bf16[512,768]{1,0:T(8,128)(2,1)S(1)}, u32[]{:S(2)}, u32[]{:S(2)}) %collective-permute-start.75) | collective-permute-done | bytes 786464 | tf_op jit(solution)/shard_map/ppermute | solution.py:31
  197.5 7.4 collective-permute-done.80
  257.5 47.4 %attend.1 = (bf16[2048,192]{1,0:T(8,128)(2,1)}, f32[192,2048]{1,0:T(8,128)}, f32[8,3,256]{2,1,0:T(4,128)}) custom-call(s32[8]{0:T(128)} %stack.379.block_ref, s32[16]{0:T(128)} %select_reduce_fusion.place_ref, bf16[2048,192]{1,0:T(8,128)(2,1)} %fusion.5.q_ref, bf16[4096,192]{1,0:T(8,128)(2,1)} %copy.177.k_ref, bf16[192,4096]{1,0:T(8,128)(2,1)} %copy.178.vt_ref), custom_call_target="tpu_custom_call" | custom-call | flops 25769803776 | bytes 6291456 | tf_op jit(solution)/shard_map/attend/pallas_call | solution.py:119
  310.0 11.3 %collective-permute-done.15 = bf16[512,192]{1,0:T(8,128)(2,1)S(1)} collective-permute-done((bf16[512,192]{1,0:T(8,128)(2,1)S(1)}, bf16[512,192]{1,0:T(8,128)(2,1)S(1)}, u32[]{:S(2)}, u32[]{:S(2)}) %collective-permute-start.15) | collective-permute-done | bytes 196640 | tf_op jit(solution)/shard_map/ppermute | solution.py:31
  323.8 11.6 %collective-permute-start.67 = (bf16[512,768]{1,0:T(8,128)(2,1)S(1)}, bf16[512,768]{1,0:T(8,128)(2,1)}, u32[]{:S(2)}, u32[]{:S(2)}) collective-permute-start(bf16[512,768]{1,0:T(8,128)(2,1)S(1)} %add_convert_fusion.5), channel_id=1, source_target_pairs={{0,2},{1,3},{2,0},{3,1},{4,6},{5,7},{6,4},{7,5},{8,10},{9,11},{10,... | collective-permute-start | bytes 2359304 | tf_op jit(solution)/shard_map/ppermute | solution.py:31
  372.1 10.2 expert_step.4
  405.3 10.1 collective-permute-done.72
  419.7 10.1 expert_step.7
  456.1 10.6 %expert_step.6 = (bf16[8,4,32,768]{3,2,1,0:T(8,128)(2,1)}, bf16[8,4,32,768]{3,2,1,0:T(8,128)(2,1)}, bf16[8,4,32,768]{3,2,1,0:T(8,128)(2,1)}, bf16[8,4,32,768]{3,2,1,0:T(8,128)(2,1)}) custom-call(bf16[8,4,32,768]{3,2,1,0:T(8,128)(2,1)} %constant_dynamic-update-slice_fusion.40.x_ref.refs_3_, bf16[8,4,32,768]{3,2,1,0:T(8,128)(2,1)} %copy-done.63, ...), custom_call_target="tpu_custom_call" | custom-call | flops 4831838208 | bytes 18874368 | tf_op jit(solution)/shard_map/expert_step/pallas_call | solution.py:269
  505.4 7.4 collective-permute-done.113
  550.9 7.2 collective-permute-done.105
  568.9 11.3 %collective-permute-done.87 = bf16[128,768]{1,0:T(8,128)(2,1)S(1)} collective-permute-done((bf16[128,768]{1,0:T(8,128)(2,1)S(1)}, bf16[128,768]{1,0:T(8,128)(2,1)S(1)}, u32[]{:S(2)}, u32[]{:S(2)}) %collective-permute-start.87) | collective-permute-done | bytes 196640 | tf_op jit(solution)/shard_map/ppermute | solution.py:31
  595.3 14.3 %collective-permute-start.114 = (bf16[512,768]{1,0:T(8,128)(2,1)}, bf16[512,768]{1,0:T(8,128)(2,1)}, u32[]{:S(2)}, u32[]{:S(2)}) collective-permute-start(bf16[512,768]{1,0:T(8,128)(2,1)} %fusion.36), channel_id=1, source_target_pairs={{0,2},{1,3},{2,0},{3,1},{4,6},{5,7},{6,4},{7,5},{8,10},{9,11},{10,... | collective-permute-start | bytes 2359304 | tf_op jit(solution)/shard_map/ppermute | solution.py:31
  612.8 10.3 %expert_step.5 = (bf16[8,4,32,768]{3,2,1,0:T(8,128)(2,1)}, bf16[8,4,32,768]{3,2,1,0:T(8,128)(2,1)}, bf16[8,4,32,768]{3,2,1,0:T(8,128)(2,1)}, bf16[8,4,32,768]{3,2,1,0:T(8,128)(2,1)}) custom-call(bf16[8,4,32,768]{3,2,1,0:T(8,128)(2,1)} %bitcast.30.x_ref.refs_1_, bf16[8,4,32,768]{3,2,1,0:T(8,128)(2,1)} %bitcast.39.gy_ref.refs_5_, ...), custom_call_target="tpu_custom_call" | custom-call | flops 4831838208 | bytes 18874368 | tf_op jit(solution)/shard_map/expert_step/pallas_call | solution.py:269
  632.6 17.8 %expert_grads.1 = (f32[4,768,768]{2,1,0:T(8,128)}, f32[4,768,768]{2,1,0:T(8,128)}) custom-call(bf16[8,4,32,768]{3,2,1,0:T(8,128)(2,1)} %constant_dynamic-update-slice_fusion.x_ref.refs_0_, bf16[8,4,32,768]{3,2,1,0:T(8,128)(2,1)} %bitcast.30.x_ref.refs_1_, bf16[8,4,32,768]{3,2,1,0:T(8,128)(2,1)} %constant_dynamic-update-slice_fusion.64.x_ref.refs_2_, ...), custom_call_target="tpu_custom_call" | custom-call | flops 9663676416 | bytes 18874368 | tf_op jit(solution)/shard_map/expert_grads/pallas_call | solution.py:301
  650.4 43.9 %collective-permute-done.91 = bf16[8,128,768]{2,1,0:T(8,128)(2,1)} collective-permute-done((bf16[8,128,768]{2,1,0:T(8,128)(2,1)}, bf16[8,128,768]{2,1,0:T(8,128)(2,1)}, u32[]{:S(2)}, u32[]{:S(2)}) %collective-permute-start.91) | collective-permute-done | bytes 1572896 | tf_op jit(solution)/shard_map/ppermute | solution.py:31
  694.3 32.6 %collective-permute-done.33 = bf16[8,128,768]{2,1,0:T(8,128)(2,1)} collective-permute-done((bf16[8,128,768]{2,1,0:T(8,128)(2,1)}, bf16[8,128,768]{2,1,0:T(8,128)(2,1)}, u32[]{:S(2)}, u32[]{:S(2)}) %collective-permute-start.33) | collective-permute-done | bytes 1572896 | tf_op jit(solution)/shard_map/ppermute | solution.py:31
  733.7 9.2 collective-permute-done.93
  770.3 7.0 collective-permute-done.98
  835.5 65.7 %attend_back.1 = (bf16[2048,192]{1,0:T(8,128)(2,1)}, bf16[4096,192]{1,0:T(8,128)(2,1)}, bf16[4096,192]{1,0:T(8,128)(2,1)}) custom-call(s32[8]{0:T(128)} %stack.379.block_ref, s32[16]{0:T(128)} %select_reduce_fusion.place_ref, bf16[2048,192]{1,0:T(8,128)(2,1)} %fusion.5.q_ref, bf16[2048,192]{1,0:T(8,128)(2,1)} %pad_maximum_fusion.6.g_ref, ...), custom_call_target="tpu_custom_call" | custom-call | flops 64424509440 | bytes 12582912 | tf_op jit(solution)/shard_map/attend_back/pallas_call | solution.py:208
  933.5 9.9 fusion.112
  974.2 18.5 %collective-permute-start.125 = (bf16[96,704]{1,0:T(8,128)(2,1)S(1)}, bf16[96,704]{1,0:T(8,128)(2,1)S(1)}, u32[]{:S(2)}, u32[]{:S(2)}) collective-permute-start(bf16[96,704]{1,0:T(8,128)(2,1)S(1)} %get-tuple-element.193), channel_id=1, source_target_pairs={{0,2},{1,3},{2,0},{3,1},{4,6},{5,7},{6,4},{7,5},{8,10},{9,11},{10,... | collective-permute-start | bytes 405512 | tf_op jit(solution)/shard_map/ppermute | solution.py:31
  (668 shorter events, 576.6 us)
Async XLA Ops:
  10.5 78.5 %collective-permute-start.6 = (bf16[192,576]{1,0:T(8,128)(2,1)S(1)}, bf16[192,576]{1,0:T(8,128)(2,1)S(1)}, u32[]{:S(2)}, u32[]{:S(2)}) collective-permute-start(bf16[192,576]{1,0:T(8,128)(2,1)S(1)} %pad_maximum_fusion.11), channel_id=1, source_target_pairs={{0,3},{1,2},{2,1},{3,0},{4,7},{5,6},{6,5},{7,4},{8,11},{9,10},{10,... | collective-permute-start | bytes 663560 | tf_op jit(solution)/shard_map/ppermute | solution.py:31
  14.3 76.2 %collective-permute-start.7 = (bf16[192,576]{1,0:T(8,128)(2,1)S(1)}, bf16[192,576]{1,0:T(8,128)(2,1)S(1)}, u32[]{:S(2)}, u32[]{:S(2)}) collective-permute-start(bf16[192,576]{1,0:T(8,128)(2,1)S(1)} %pad_maximum_fusion.11), channel_id=1, source_target_pairs={{0,2},{1,3},{2,0},{3,1},{4,6},{5,7},{6,4},{7,5},{8,10},{9,11},{10,... | collective-permute-start | bytes 663560 | tf_op jit(solution)/shard_map/ppermute | solution.py:31
  36.7 55.4 %collective-permute-start.8 = (bf16[192,576]{1,0:T(8,128)(2,1)S(1)}, bf16[192,576]{1,0:T(8,128)(2,1)S(1)}, u32[]{:S(2)}, u32[]{:S(2)}) collective-permute-start(bf16[192,576]{1,0:T(8,128)(2,1)S(1)} %pad_maximum_fusion.11), channel_id=1, source_target_pairs={{0,1},{1,0},{2,3},{3,2},{4,5},{5,4},{6,7},{7,6},{8,9},{9,8},{10,11... | collective-permute-start | bytes 663560 | tf_op jit(solution)/shard_map/ppermute | solution.py:31
  59.8 62.4 %collective-permute-start.2 = (bf16[512,768]{1,0:T(8,128)(2,1)S(1)}, bf16[512,768]{1,0:T(8,128)(2,1)S(1)}, u32[]{:S(2)}, u32[]{:S(2)}) collective-permute-start(bf16[512,768]{1,0:T(8,128)(2,1)S(1)} %bitcast.357), channel_id=1, source_target_pairs={{0,24},{4,28},{8,16},{12,20},{16,8},{20,12},{24,0},{28,4},{1,25},{... | collective-permute-start | bytes 2359304 | tf_op jit(solution)/shard_map/ppermute | solution.py:31
  119.5 61.9 %collective-permute-start.41 = (s32[512]{0:T(512)S(1)}, s32[512]{0:T(512)}, u32[]{:S(2)}, u32[]{:S(2)}) collective-permute-start(s32[512]{0:T(512)S(1)} %fusion.103), channel_id=1, source_target_pairs={{0,3},{1,2},{2,1},{3,0},{4,7},{5,6},{6,5},{7,4},{8,11},{9,10},{10,... | collective-permute-start | bytes 6152 | tf_op jit(solution)/shard_map/ppermute | solution.py:31
  122.3 59.6 %collective-permute-start.50 = (bf16[512,768]{1,0:T(8,128)(2,1)S(1)}, bf16[512,768]{1,0:T(8,128)(2,1)}, u32[]{:S(2)}, u32[]{:S(2)}) collective-permute-start(bf16[512,768]{1,0:T(8,128)(2,1)S(1)} %bitcast.376), channel_id=1, source_target_pairs={{0,3},{1,2},{2,1},{3,0},{4,7},{5,6},{6,5},{7,4},{8,11},{9,10},{10,... | collective-permute-start | bytes 2359304 | tf_op jit(solution)/shard_map/ppermute | solution.py:31
  123.8 487.9 %collective-permute-start.32 = (bf16[8,128,768]{2,1,0:T(8,128)(2,1)}, bf16[8,128,768]{2,1,0:T(8,128)(2,1)}, u32[]{:S(2)}, u32[]{:S(2)}) collective-permute-start(bf16[8,128,768]{2,1,0:T(8,128)(2,1)} %constant_dynamic-update-slice_fusion.24), channel_id=1, source_target_pairs={{0,1},{1,0},{2,3},{3,2},{4,5},{5,4},{6,7},{7,6},{8,9},{9,8},{10,11... | collective-permute-start | bytes 4718600 | tf_op jit(solution)/shard_map/ppermute | solution.py:31
  139.7 102.9 %collective-permute-start.9 = (bf16[2048,192]{0,1:T(8,128)(2,1)S(1)}, bf16[2048,192]{0,1:T(8,128)(2,1)}, u32[]{:S(2)}, u32[]{:S(2)}) collective-permute-start(bf16[2048,192]{0,1:T(8,128)(2,1)S(1)} %convolution_convert_fusion.2), channel_id=1, source_target_pairs={{0,4},{4,0},{8,12},{12,8},{16,20},{20,16},{24,28},{28,24},{1,5},{5... | collective-permute-start | bytes 2359304 | tf_op jit(solution)/shard_map/ppermute | solution.py:31
  175.0 72.7 %collective-permute-start.10 = (bf16[2048,192]{0,1:T(8,128)(2,1)}, bf16[2048,192]{0,1:T(8,128)(2,1)}, u32[]{:S(2)}, u32[]{:S(2)}) collective-permute-start(bf16[2048,192]{0,1:T(8,128)(2,1)} %convolution_convert_fusion.1), channel_id=1, source_target_pairs={{0,4},{4,0},{8,12},{12,8},{16,20},{20,16},{24,28},{28,24},{1,5},{5... | collective-permute-start | bytes 2359304 | tf_op jit(solution)/shard_map/ppermute | solution.py:31
  323.8 63.8 %collective-permute-start.67 = (bf16[512,768]{1,0:T(8,128)(2,1)S(1)}, bf16[512,768]{1,0:T(8,128)(2,1)}, u32[]{:S(2)}, u32[]{:S(2)}) collective-permute-start(bf16[512,768]{1,0:T(8,128)(2,1)S(1)} %add_convert_fusion.5), channel_id=1, source_target_pairs={{0,2},{1,3},{2,0},{3,1},{4,6},{5,7},{6,4},{7,5},{8,10},{9,11},{10,... | collective-permute-start | bytes 2359304 | tf_op jit(solution)/shard_map/ppermute | solution.py:31
  335.4 55.0 %collective-permute-start.42 = (bf16[512,768]{1,0:T(8,128)(2,1)S(1)}, bf16[512,768]{1,0:T(8,128)(2,1)}, u32[]{:S(2)}, u32[]{:S(2)}) collective-permute-start(bf16[512,768]{1,0:T(8,128)(2,1)S(1)} %add_convert_fusion.5), channel_id=1, source_target_pairs={{0,3},{1,2},{2,1},{3,0},{4,7},{5,6},{6,5},{7,4},{8,11},{9,10},{10,... | collective-permute-start | bytes 2359304 | tf_op jit(solution)/shard_map/ppermute | solution.py:31
  367.2 244.4 %collective-permute-start.31 = (bf16[8,128,768]{2,1,0:T(8,128)(2,1)}, bf16[8,128,768]{2,1,0:T(8,128)(2,1)}, u32[]{:S(2)}, u32[]{:S(2)}) collective-permute-start(bf16[8,128,768]{2,1,0:T(8,128)(2,1)} %constant_dynamic-update-slice_fusion.16), channel_id=1, source_target_pairs={{0,1},{1,0},{2,3},{3,2},{4,5},{5,4},{6,7},{7,6},{8,9},{9,8},{10,11... | collective-permute-start | bytes 4718600 | tf_op jit(solution)/shard_map/ppermute | solution.py:31
  449.4 111.6 %collective-permute-start.83 = (bf16[128,768]{1,0:T(8,128)(2,1)S(1)}, bf16[128,768]{1,0:T(8,128)(2,1)}, u32[]{:S(2)}, u32[]{:S(2)}) collective-permute-start(bf16[128,768]{1,0:T(8,128)(2,1)S(1)} %bitcast.407), channel_id=1, source_target_pairs={{0,4},{4,0},{8,12},{12,8},{16,20},{20,16},{24,28},{28,24},{1,5},{5... | collective-permute-start | bytes 589832 | tf_op jit(solution)/shard_map/ppermute | solution.py:31
  454.5 108.5 %collective-permute-start.84 = (bf16[128,768]{1,0:T(8,128)(2,1)S(1)}, bf16[128,768]{1,0:T(8,128)(2,1)}, u32[]{:S(2)}, u32[]{:S(2)}) collective-permute-start(bf16[128,768]{1,0:T(8,128)(2,1)S(1)} %bitcast.405), channel_id=1, source_target_pairs={{0,8},{4,12},{8,0},{12,4},{16,24},{20,28},{24,16},{28,20},{1,9},{5... | collective-permute-start | bytes 589832 | tf_op jit(solution)/shard_map/ppermute | solution.py:31
  595.3 182.1 %collective-permute-start.114 = (bf16[512,768]{1,0:T(8,128)(2,1)}, bf16[512,768]{1,0:T(8,128)(2,1)}, u32[]{:S(2)}, u32[]{:S(2)}) collective-permute-start(bf16[512,768]{1,0:T(8,128)(2,1)} %fusion.36), channel_id=1, source_target_pairs={{0,2},{1,3},{2,0},{3,1},{4,6},{5,7},{6,4},{7,5},{8,10},{9,11},{10,... | collective-permute-start | bytes 2359304 | tf_op jit(solution)/shard_map/ppermute | solution.py:31
  609.6 169.2 %collective-permute-start.106 = (bf16[512,768]{1,0:T(8,128)(2,1)}, bf16[512,768]{1,0:T(8,128)(2,1)}, u32[]{:S(2)}, u32[]{:S(2)}) collective-permute-start(bf16[512,768]{1,0:T(8,128)(2,1)} %fusion.34), channel_id=1, source_target_pairs={{0,3},{1,2},{2,1},{3,0},{4,7},{5,6},{6,5},{7,4},{8,11},{9,10},{10,... | collective-permute-start | bytes 2359304 | tf_op jit(solution)/shard_map/ppermute | solution.py:31
  623.1 71.3 %collective-permute-start.91 = (bf16[8,128,768]{2,1,0:T(8,128)(2,1)}, bf16[8,128,768]{2,1,0:T(8,128)(2,1)}, u32[]{:S(2)}, u32[]{:S(2)}) collective-permute-start(bf16[8,128,768]{2,1,0:T(8,128)(2,1)} %bitcast.461), channel_id=1, source_target_pairs={{0,1},{1,0},{2,3},{3,2},{4,5},{5,4},{6,7},{7,6},{8,9},{9,8},{10,11... | collective-permute-start | bytes 4718600 | tf_op jit(solution)/shard_map/ppermute | solution.py:31
  627.0 99.9 %collective-permute-start.33 = (bf16[8,128,768]{2,1,0:T(8,128)(2,1)}, bf16[8,128,768]{2,1,0:T(8,128)(2,1)}, u32[]{:S(2)}, u32[]{:S(2)}) collective-permute-start(bf16[8,128,768]{2,1,0:T(8,128)(2,1)} %bitcast.460), channel_id=1, source_target_pairs={{0,1},{1,0},{2,3},{3,2},{4,5},{5,4},{6,7},{7,6},{8,9},{9,8},{10,11... | collective-permute-start | bytes 4718600 | tf_op jit(solution)/shard_map/ppermute | solution.py:31
  731.1 74.4 %collective-permute-start.34 = (bf16[128,768]{1,0:T(8,128)(2,1)}, bf16[128,768]{1,0:T(8,128)(2,1)}, u32[]{:S(2)}, u32[]{:S(2)}) collective-permute-start(bf16[128,768]{1,0:T(8,128)(2,1)} %get-tuple-element.120), channel_id=1, source_target_pairs={{0,4},{4,0},{8,12},{12,8},{16,20},{20,16},{24,28},{28,24},{1,5},{5... | collective-permute-start | bytes 589832 | tf_op jit(solution)/shard_map/ppermute | solution.py:31
  731.6 77.1 %collective-permute-start.35 = (bf16[128,768]{1,0:T(8,128)(2,1)}, bf16[128,768]{1,0:T(8,128)(2,1)}, u32[]{:S(2)}, u32[]{:S(2)}) collective-permute-start(bf16[128,768]{1,0:T(8,128)(2,1)} %get-tuple-element.119), channel_id=1, source_target_pairs={{0,8},{4,12},{8,0},{12,4},{16,24},{20,28},{24,16},{28,20},{1,9},{5... | collective-permute-start | bytes 589832 | tf_op jit(solution)/shard_map/ppermute | solution.py:31
  808.7 101.2 %collective-permute-start.40 = (bf16[128,768]{1,0:T(8,128)(2,1)}, bf16[128,768]{1,0:T(8,128)(2,1)}, u32[]{:S(2)}, u32[]{:S(2)}) collective-permute-start(bf16[128,768]{1,0:T(8,128)(2,1)} %get-tuple-element.114), channel_id=1, source_target_pairs={{0,28},{4,24},{8,20},{12,16},{16,12},{20,8},{24,4},{28,0},{1,29},{... | collective-permute-start | bytes 589832 | tf_op jit(solution)/shard_map/ppermute | solution.py:31
  832.1 73.5 %collective-permute-start.134 = (bf16[4,24,896]{2,1,0:T(8,128)(2,1)}, bf16[4,24,896]{2,1,0:T(8,128)(2,1)}, u32[]{:S(2)}, u32[]{:S(2)}) collective-permute-start(bf16[4,24,896]{2,1,0:T(8,128)(2,1)} %get-tuple-element.187), channel_id=1, source_target_pairs={{0,24},{4,28},{8,16},{12,20},{16,8},{20,12},{24,0},{28,4},{1,25},{... | collective-permute-start | bytes 516104 | tf_op jit(solution)/shard_map/ppermute | solution.py:31
  833.7 72.4 %collective-permute-start.133 = (bf16[4,24,896]{2,1,0:T(8,128)(2,1)}, bf16[4,24,896]{2,1,0:T(8,128)(2,1)}, u32[]{:S(2)}, u32[]{:S(2)}) collective-permute-start(bf16[4,24,896]{2,1,0:T(8,128)(2,1)} %get-tuple-element.188), channel_id=1, source_target_pairs={{0,16},{4,20},{8,24},{12,28},{16,0},{20,4},{24,8},{28,12},{1,17},{... | collective-permute-start | bytes 516104 | tf_op jit(solution)/shard_map/ppermute | solution.py:31
  834.4 71.7 %collective-permute-start.132 = (bf16[4,24,896]{2,1,0:T(8,128)(2,1)}, bf16[4,24,896]{2,1,0:T(8,128)(2,1)}, u32[]{:S(2)}, u32[]{:S(2)}) collective-permute-start(bf16[4,24,896]{2,1,0:T(8,128)(2,1)} %get-tuple-element.186), channel_id=1, source_target_pairs={{0,8},{4,12},{8,0},{12,4},{16,24},{20,28},{24,16},{28,20},{1,9},{5... | collective-permute-start | bytes 516104 | tf_op jit(solution)/shard_map/ppermute | solution.py:31
  (189 other events, 3416.1 us)

commit v2 on v1

v2 whole, which is shorter than its diff:
```python
from functools import partial
from math import gcd

import jax
import jax.numpy as jnp
from jax import lax
from jax.experimental import pallas as pl
from jax.experimental.pallas import tpu as pltpu
from jax.sharding import PartitionSpec as P

HEADS = 12
HD = 64
BLK = 256
TOK_DEV = 512
CHUNK = 4
epsilon = 1e-05
masked_value = -1e30
bf16 = jnp.bfloat16
f32 = jnp.float32
NT = (((1,), (1,)), ((), ()))
NN = (((1,), (0,)), ((), ()))
TN = (((0,), (0,)), ((), ()))
PARAMS = pltpu.CompilerParams(vmem_limit_bytes=56 * 1024 * 1024)


def dot(a, b, dims=NN):
    return lax.dot_general(a, b, dims, preferred_element_type=f32)


def swap(value, axis, offset):
    size = lax.axis_size(axis)
    return lax.ppermute(value, axis, [(i, i ^ offset) for i in range(size)])


def trade(parts, axis, groups=None):
    return lax.all_to_all(parts, axis, 0, 0, tiled=True, axis_index_groups=groups)


def share(part, count, axis, groups=None):
    return trade(jnp.broadcast_to(part[None], (count,) + part.shape), axis, groups)


def in_order(pieces, index):
    count, bit = len(pieces), 1
    while bit < count:
        odd = (index & bit) != 0
        pieces = [jnp.where(odd, pieces[i ^ bit], pieces[i]) for i in range(count)]
        bit *= 2
    return pieces


def after(value, *others):
    return lax.optimization_barrier((value,) + others)[0]


def norm_stats(values):
    center = jnp.mean(values, axis=-1, keepdims=True)
    offset = values - center
    scale = lax.rsqrt(jnp.mean(offset * offset, axis=-1, keepdims=True) + epsilon)
    return offset * scale, scale


def norm_back(normal, scale, gain, grad):
    inner = grad * gain
    return scale * (
        inner
        - jnp.mean(inner, axis=-1, keepdims=True)
        - normal * jnp.mean(inner * normal, axis=-1, keepdims=True)
    )


def whole(shape):
    return pl.BlockSpec(shape, lambda i, *_: (0,) * len(shape), pipeline_mode=pl.Buffered(1))


def cost(flops, moved, exps=0):
    return pl.CostEstimate(flops=int(flops), bytes_accessed=int(moved), transcendentals=int(exps))


def project_kernel(hidden_ref, wt_ref, vec_ref, out_ref):
    normal, _ = norm_stats(hidden_ref[0].astype(f32))
    normed = (normal * vec_ref[0:1] + vec_ref[1:2]).astype(bf16)
    got = dot(wt_ref[...], normed, NT).astype(bf16)
    span = got.shape[0] // 3
    out_ref[:span, :] = (got[:span].astype(f32) * HD ** (-0.5)).astype(bf16)
    out_ref[span:, :] = got[span:]


def project(hidden, wt, vecs):
    sources, rows, width = hidden.shape
    wide = wt.shape[0]
    return pl.pallas_call(
        project_kernel,
        grid=(sources,),
        in_specs=[
            pl.BlockSpec((1, rows, width), lambda i: (i, 0, 0)),
            whole(wt.shape),
            whole(vecs.shape),
        ],
        out_specs=pl.BlockSpec((wide, rows), lambda i: (0, i)),
        out_shape=jax.ShapeDtypeStruct((wide, sources * rows), bf16),
        compiler_params=PARAMS,
        cost_estimate=cost(2 * sources * rows * width * wide, 4 * sources * rows * width),
        name="project",
    )(hidden, wt, vecs)


def only_head(block, head):
    heads = block.shape[0] // HD
    zero = jnp.zeros((HD, block.shape[1]), block.dtype)
    return jnp.concatenate(
        [block[h * HD : (h + 1) * HD] if h == head else zero for h in range(heads)], axis=0
    )


def key_blocks(number_ref, span, own_ref, far_ref):
    per = own_ref.shape[1] // BLK
    for s in range(1 + far_ref.shape[0]):
        for i in range(per):
            at = pl.multiple_of(number_ref[s * per + i] * BLK, BLK)
            cut = slice(i * BLK, (i + 1) * BLK)
            yield at, (own_ref[span:, cut] if s == 0 else far_ref[s - 1, :, cut])


def attend_kernel(
    number_ref, q_ref, own_ref, far_ref, att_ref, att_t_ref, lse_ref, acc_ref, k_sorted, v_sorted
):
    turn = pl.program_id(0)
    span = acc_ref.shape[0]
    heads = span // HD
    block = number_ref[turn]
    size = CHUNK * BLK

    @pl.when(turn == 0)
    def _():
        for at, kv in key_blocks(number_ref, span, own_ref, far_ref):
            k_sorted[pl.ds(at, BLK), :] = jnp.transpose(kv[:span])
            v_sorted[:, pl.ds(at, BLK)] = kv[span:]

    queries = [only_head(q_ref[...], h) for h in range(heads)]
    acc_ref[...] = jnp.zeros_like(acc_ref)

    def step(last, index, state):
        top, total = state
        at = pl.multiple_of(index * size, size)
        keys = k_sorted[pl.ds(at, size), :]
        tops, totals = [], []
        scores = [dot(keys, queries[h]) for h in range(heads)]
        if last:
            row = lax.broadcasted_iota(jnp.int32, scores[0].shape, 0)
            limit = (block + 1 - index * CHUNK) * BLK
            scores = [jnp.where(row < limit, s, masked_value) for s in scores]
        for h in range(heads):
            rows = slice(h * HD, (h + 1) * HD)
            new_top = jnp.maximum(top[h], jnp.max(scores[h], axis=0, keepdims=True))
            factor = jnp.exp(top[h] - new_top)
            weights = jnp.exp(scores[h] - new_top)
            tops.append(new_top)
            totals.append(total[h] * factor + jnp.sum(weights, axis=0, keepdims=True))
            update = dot(v_sorted[rows, pl.ds(at, size)], weights.astype(bf16))
            acc_ref[rows, :] = acc_ref[rows, :] * factor + update
        return tuple(tops), tuple(totals)

    start = (
        tuple(jnp.full((1, BLK), masked_value, f32) for _ in range(heads)),
        tuple(jnp.zeros((1, BLK), f32) for _ in range(heads)),
    )
    full = (block + 1) // CHUNK
    state = lax.fori_loop(0, full, partial(step, False), start)
    top, total = lax.fori_loop(full, (block + CHUNK) // CHUNK, partial(step, True), state)
    for h in range(heads):
        rows = slice(h * HD, (h + 1) * HD)
        out = acc_ref[rows, :] / total[h]
        att_t_ref[rows, :] = out
        att_ref[0, rows, :] = out.astype(bf16)
        lse_ref[0, h : h + 1, :] = top[h] + jnp.log(total[h])


def attend(numbers, own, far):
    span, rows = own.shape[0] // 3, own.shape[1]
    blocks = rows // BLK
    keys = rows * (1 + far.shape[0])
    return pl.pallas_call(
        attend_kernel,
        grid_spec=pltpu.PrefetchScalarGridSpec(
            num_scalar_prefetch=1,
            grid=(blocks,),
            in_specs=[
                pl.BlockSpec((span, BLK), lambda i, *_: (0, i)),
                whole(own.shape),
                whole(far.shape),
            ],
            out_specs=[
                pl.BlockSpec((1, span, BLK), lambda i, *_: (i // 2, 0, i % 2)),
                pl.BlockSpec((span, BLK), lambda i, *_: (0, i)),
                pl.BlockSpec((1, 8, BLK), lambda i, *_: (i, 0, 0)),
            ],
            scratch_shapes=[
                pltpu.VMEM((span, BLK), f32),
                pltpu.VMEM((keys, span), bf16),
                pltpu.VMEM((span, keys), bf16),
            ],
        ),
        out_shape=[
            jax.ShapeDtypeStruct((blocks // 2, span, 2 * BLK), bf16),
            jax.ShapeDtypeStruct((span, rows), f32),
            jax.ShapeDtypeStruct((blocks, 8, BLK), f32),
        ],
        compiler_params=PARAMS,
        cost_estimate=cost(12 * rows * keys * span, 8 * keys * span, rows * keys * span // 128),
        name="attend",
    )(numbers, own, own, far)


def attend_back_kernel(
    number_ref, q_ref, g_ref, att_t_ref, lse_ref, own_ref, far_ref, gq_ref, gown_ref, gfar_ref,
    gq_acc, gk_acc, gv_acc, k_sorted, v_sorted, kt_sorted,
):
    turn = pl.program_id(0)
    span = gq_acc.shape[0]
    heads = span // HD
    block = number_ref[turn]
    size = CHUNK * BLK

    @pl.when(turn == 0)
    def _():
        gk_acc[...] = jnp.zeros_like(gk_acc)
        gv_acc[...] = jnp.zeros_like(gv_acc)
        for at, kv in key_blocks(number_ref, span, own_ref, far_ref):
            k_sorted[pl.ds(at, BLK), :] = jnp.transpose(kv[:span])
            v_sorted[pl.ds(at, BLK), :] = jnp.transpose(kv[span:])
            kt_sorted[:, pl.ds(at, BLK)] = kv[:span]

    grads = g_ref[0]
    prod = grads.astype(f32) * att_t_ref[...]
    part = lambda h: slice(h * HD, (h + 1) * HD)
    deltas = [jnp.sum(prod[part(h)], axis=0, keepdims=True) for h in range(heads)]
    logs = [lse_ref[0, h : h + 1, :] for h in range(heads)]
    q_only = [only_head(q_ref[...], h) for h in range(heads)]
    g_only = [only_head(grads, h) for h in range(heads)]
    gq_acc[...] = jnp.zeros_like(gq_acc)

    def step(last, index, carry):
        at = pl.multiple_of(index * size, size)
        keys = k_sorted[pl.ds(at, size), :]
        values = v_sorted[pl.ds(at, size), :]
        if last:
            row = lax.broadcasted_iota(jnp.int32, (size, BLK), 0)
            allowed = row < (block + 1 - index * CHUNK) * BLK
        for h in range(heads):
            rows = part(h)
            probs = jnp.exp(dot(keys, q_only[h]) - logs[h])
            if last:
                probs = jnp.where(allowed, probs, 0.0)
            gs = (probs * (dot(values, g_only[h]) - deltas[h])).astype(bf16)
            gq_acc[rows, :] += dot(kt_sorted[rows, pl.ds(at, size)], gs)
            gv_acc[rows, pl.ds(at, size)] += dot(grads[rows], probs.astype(bf16), NT)
            gk_acc[rows, pl.ds(at, size)] += dot(q_ref[rows, :], gs, NT)
        return carry

    full = (block + 1) // CHUNK
    lax.fori_loop(0, full, partial(step, False), 0)
    lax.fori_loop(full, (block + CHUNK) // CHUNK, partial(step, True), 0)
    gq_ref[...] = (gq_acc[...] * HD ** (-0.5)).astype(bf16)

    @pl.when(turn == pl.num_programs(0) - 1)
    def _():
        per = own_ref.shape[1] // BLK
        for s in range(1 + far_ref.shape[0]):
            for i in range(per):
                at = pl.multiple_of(number_ref[s * per + i] * BLK, BLK)
                cut = slice(i * BLK, (i + 1) * BLK)
                gk = gk_acc[:, pl.ds(at, BLK)].astype(bf16)
                gv = gv_acc[:, pl.ds(at, BLK)].astype(bf16)
                if s == 0:
                    gown_ref[:span, cut], gown_ref[span:, cut] = gk, gv
                else:
                    gfar_ref[s - 1, :span, cut], gfar_ref[s - 1, span:, cut] = gk, gv


def attend_back(numbers, own, far, grads, att_t, logs):
    span, rows = own.shape[0] // 3, own.shape[1]
    blocks = rows // BLK
    keys = rows * (1 + far.shape[0])
    column = pl.BlockSpec((span, BLK), lambda i, *_: (0, i))
    return pl.pallas_call(
        attend_back_kernel,
        grid_spec=pltpu.PrefetchScalarGridSpec(
            num_scalar_prefetch=1,
            grid=(blocks,),
            in_specs=[
                column,
                pl.BlockSpec((1, span, BLK), lambda i, *_: (i // 2, 0, i % 2)),
                column,
                pl.BlockSpec((1, 8, BLK), lambda i, *_: (i, 0, 0)),
                whole(own.shape),
                whole(far.shape),
            ],
            out_specs=[column, whole((2 * span, rows)), whole(far.shape)],
            scratch_shapes=[
                pltpu.VMEM((span, BLK), f32),
                pltpu.VMEM((span, keys), f32),
                pltpu.VMEM((span, keys), f32),
                pltpu.VMEM((keys, span), bf16),
                pltpu.VMEM((keys, span), bf16),
                pltpu.VMEM((span, keys), bf16),
            ],
        ),
        out_shape=[
            jax.ShapeDtypeStruct((span, rows), bf16),
            jax.ShapeDtypeStruct((2 * span, rows), bf16),
            jax.ShapeDtypeStruct(far.shape, bf16),
        ],
        compiler_params=PARAMS,
        cost_estimate=cost(30 * rows * keys * span, 16 * keys * span, rows * keys * span // 128),
        name="attend_back",
    )(numbers, own, grads, att_t, logs, own, far)


def middle_kernel(att_ref, x_ref, w_ref, vec_ref, slot_ref, mid_ref, normed_ref, send_ref):
    middle = x_ref[...].astype(f32) + dot(att_ref[...], w_ref[...], TN)
    normal, _ = norm_stats(middle)
    normed = (normal * vec_ref[2:3] + vec_ref[3:4]).astype(bf16)
    mid_ref[...] = middle
    normed_ref[...] = normed
    slots = lax.broadcasted_iota(jnp.int32, (send_ref.shape[0], x_ref.shape[0]), 0)
    place = (slots == slot_ref[...]).astype(f32).astype(bf16)
    send_ref[...] = dot(place, normed).astype(bf16)


def middle_step(att_t, rows, weight, vecs, slot, all_slots):
    count, width = rows.shape
    return pl.pallas_call(
        middle_kernel,
        out_shape=[
            jax.ShapeDtypeStruct((count, width), f32),
            jax.ShapeDtypeStruct((count, width), bf16),
            jax.ShapeDtypeStruct((all_slots, width), bf16),
        ],
        compiler_params=PARAMS,
        cost_estimate=cost(2 * count * width * (width + all_slots), 10 * count * width),
        name="middle",
    )(att_t, rows, weight, vecs, slot[None, :])


def turn_kernel(
    got_ref, far_ref, slot_ref, mid_ref, cot_ref, w_ref, vec_ref, gmid_ref, gbr_ref, gatt_ref, sum_ref
):
    slots = lax.broadcasted_iota(jnp.int32, (mid_ref.shape[0], got_ref.shape[0]), 1)
    place = (slots == slot_ref[...]).astype(f32).astype(bf16)
    grad = (dot(place, got_ref[...]) + far_ref[...].astype(f32)).astype(bf16).astype(f32)
    normal, scale = norm_stats(mid_ref[...])
    middle = cot_ref[...].astype(f32) + norm_back(normal, scale, vec_ref[2:3], grad)
    branch = middle.astype(bf16)
    gmid_ref[...] = middle
    gbr_ref[...] = branch
    gatt_ref[...] = dot(w_ref[...], branch, NT).astype(bf16)
    sum_ref[...] = jnp.zeros_like(sum_ref)
    sum_ref[0:1] = jnp.sum(grad * normal, axis=0, keepdims=True)
    sum_ref[1:2] = jnp.sum(grad, axis=0, keepdims=True)


def turn_step(got, far, slot, middle, cot, weight, vecs):
    count, width = middle.shape
    return pl.pallas_call(
        turn_kernel,
        out_shape=[
            jax.ShapeDtypeStruct((count, width), f32),
            jax.ShapeDtypeStruct((count, width), bf16),
            jax.ShapeDtypeStruct((weight.shape[0], count), bf16),
            jax.ShapeDtypeStruct((128, width), f32),
        ],
        compiler_params=PARAMS,
        cost_estimate=cost(2 * count * width * (width + got.shape[0]), 12 * count * width),
        name="turn",
    )(got, far, slot[:, None], middle, cot, weight, vecs)


def out_grad_kernel(att_ref, gbr_ref, sum_ref, out_ref):
    width = gbr_ref.shape[1]
    out_ref[:, :width] = dot(att_ref[...], gbr_ref[...]).astype(bf16)
    out_ref[:, width:] = jnp.transpose(sum_ref[...]).astype(bf16)


def out_grad_step(att_t, gbr, sums):
    return pl.pallas_call(
        out_grad_kernel,
        out_shape=jax.ShapeDtypeStruct((att_t.shape[0], gbr.shape[1] + 128), bf16),
        compiler_params=PARAMS,
        cost_estimate=cost(2 * att_t.size * gbr.shape[1], 6 * gbr.size),
        name="out_grad",
    )(att_t, gbr, sums)


def tail_kernel(
    gq_ref, gown_ref, got_ref, hidden_ref, wt_ref, vec_ref, rows_ref, mixed_ref, gw_acc, sum_acc
):
    turn = pl.program_id(0)

    @pl.when(turn == 0)
    def _():
        gw_acc[...] = jnp.zeros_like(gw_acc)
        sum_acc[...] = jnp.zeros_like(sum_acc)

    gkv = gown_ref[...].astype(f32)
    for k in range(got_ref.shape[0]):
        gkv = gkv + got_ref[k].astype(f32)
    columns = jnp.concatenate([gq_ref[...], gkv.astype(bf16)], axis=0)
    rows = dot(columns, wt_ref[...], TN)
    rows_ref[0] = rows.astype(bf16)
    normal, _ = norm_stats(hidden_ref[0].astype(f32))
    normed = (normal * vec_ref[0:1] + vec_ref[1:2]).astype(bf16)
    sum_acc[0:1] += jnp.sum(rows * normal, axis=0, keepdims=True)
    sum_acc[1:2] += jnp.sum(rows, axis=0, keepdims=True)
    gw_acc[...] += dot(columns, normed)

    @pl.when(turn == pl.num_programs(0) - 1)
    def _():
        cores, planes, count, _ = mixed_ref.shape
        wide = gw_acc.shape[0]
        weights = jnp.transpose(gw_acc[...]).astype(bf16)
        sums = jnp.transpose(sum_acc[...]).astype(bf16)
        for z in range(planes):
            for s in range(cores):
                at = (z * cores + s) * count
                mixed_ref[s, z, :, :wide] = weights[at : at + count]
                mixed_ref[s, z, :, wide:] = sums[at : at + count]


def tail_step(gq, gown, got, hidden, wt, vecs, cores, planes):
    sources, rows, width = hidden.shape
    wide = wt.shape[0]
    count = width // (cores * planes)
    return pl.pallas_call(
        tail_kernel,
        grid=(sources,),
        in_specs=[
            pl.BlockSpec((gq.shape[0], rows), lambda i: (0, i)),
            pl.BlockSpec((gown.shape[0], rows), lambda i: (0, i)),
            pl.BlockSpec((got.shape[0], gown.shape[0], rows), lambda i: (0, 0, i)),
            pl.BlockSpec((1, rows, width), lambda i: (i, 0, 0)),
            whole(wt.shape),
            whole(vecs.shape),
        ],
        out_specs=[
            pl.BlockSpec((1, rows, width), lambda i: (i, 0, 0)),
            whole((cores, planes, count, wide + 128)),
        ],
        out_shape=[
            jax.ShapeDtypeStruct((sources, rows, width), bf16),
            jax.ShapeDtypeStruct((cores, planes, count, wide + 128), bf16),
        ],
        scratch_shapes=[pltpu.VMEM((wide, width), f32), pltpu.VMEM((128, width), f32)],
        compiler_params=PARAMS,
        cost_estimate=cost(4 * sources * rows * width * wide, 6 * sources * rows * width),
        name="tail",
    )(gq, gown, got, hidden, wt, vecs)


def assemble_kernel(span, groups, part_ref, out_ref, sum_ref):
    count, rows, _ = part_ref.shape
    cores = count // groups
    for s in range(cores):
        at = slice(s * rows, (s + 1) * rows)
        pieces = [part_ref[g * cores + s].astype(f32) for g in range(groups)]
        out_ref[at, :] = jnp.concatenate(
            [p[:, t * span : (t + 1) * span] for t in range(3) for p in pieces], axis=1
        )
        sum_ref[at, :] = sum(p[:, 3 * span :] for p in pieces)


def assemble(part, span, groups):
    count, rows, wide = part.shape
    total = rows * (count // groups)
    return pl.pallas_call(
        partial(assemble_kernel, span, groups),
        out_shape=[
            jax.ShapeDtypeStruct((total, 3 * span * groups), f32),
            jax.ShapeDtypeStruct((total, wide - 3 * span), f32),
        ],
        compiler_params=PARAMS,
        cost_estimate=cost(part.size, 6 * part.size),
        name="assemble",
    )(part)


def expert_kernel(x_ref, gy_ref, first_ref, second_ref, act_ref, gpre_ref, gn_ref, ey_ref):
    flat = lambda ref: ref[...].reshape(-1, ref.shape[-1])
    first, second = first_ref[0], second_ref[0]
    pre = dot(flat(x_ref), first)
    inner = 0.7978845608028654 * (pre + 0.044715 * (pre * pre * pre))
    bend = jnp.tanh(inner)
    half = 0.5 * (1.0 + bend)
    act = (pre * half).astype(bf16)
    slope = half + 0.5 * pre * (1.0 - bend * bend) * (
        0.7978845608028654 * (1.0 + 3 * 0.044715 * (pre * pre))
    )
    gpre = (dot(flat(gy_ref), second) * slope).astype(bf16)
    act_ref[...] = act.reshape(act_ref.shape)
    gpre_ref[...] = gpre.reshape(gpre_ref.shape)
    gn_ref[...] = dot(gpre, first, NT).astype(bf16).reshape(gn_ref.shape)
    ey_ref[...] = dot(act, second, NT).astype(bf16).reshape(ey_ref.shape)


def expert_step(tokens, grads, first, second):
    sources, experts, room, width = tokens.shape
    hidden = first.shape[2]
    token_spec = pl.BlockSpec((sources, 1, room, width), lambda e: (0, e, 0, 0))
    hidden_spec = pl.BlockSpec((sources, 1, room, hidden), lambda e: (0, e, 0, 0))
    weight_spec = pl.BlockSpec((1, width, hidden), lambda e: (e, 0, 0))
    like = lambda last: jax.ShapeDtypeStruct((sources, experts, room, last), bf16)
    return pl.pallas_call(
        expert_kernel,
        grid=(experts,),
        in_specs=[token_spec, token_spec, weight_spec, weight_spec],
        out_specs=[hidden_spec, hidden_spec, token_spec, token_spec],
        out_shape=[like(hidden), like(hidden), like(width), like(width)],
        compiler_params=PARAMS,
        cost_estimate=pl.CostEstimate(
            flops=8 * sources * experts * room * width * hidden,
            bytes_accessed=4 * first.size + 12 * tokens.size,
            transcendentals=sources * experts * room * hidden,
        ),
        name="expert_step",
    )(tokens, grads, first, second)


def expert_grad_kernel(parts, *refs):
    flat = lambda ref: ref[...].reshape(-1, ref.shape[-1])
    stack = lambda some: jnp.concatenate([flat(r) for r in some], axis=0)
    ins, (gfirst_ref, gsecond_ref) = refs[: 4 * parts], refs[4 * parts :]
    tokens, grads, acts, gpres = (stack(ins[i * parts : (i + 1) * parts]) for i in range(4))
    gfirst_ref[0] = dot(tokens, gpres, TN)
    gsecond_ref[0] = dot(grads, acts, TN)


def expert_grads(tokens, grads, acts, gpres):
    parts = len(tokens)
    sources, experts, room, width = tokens[0].shape
    hidden = acts[0].shape[3]
    spec = lambda last: pl.BlockSpec((sources, 1, room, last), lambda e: (0, e, 0, 0))
    out_spec = pl.BlockSpec((1, width, hidden), lambda e: (e, 0, 0))
    out = jax.ShapeDtypeStruct((experts, width, hidden), f32)
    return pl.pallas_call(
        partial(expert_grad_kernel, parts),
        grid=(experts,),
        in_specs=[spec(width)] * (2 * parts) + [spec(hidden)] * (2 * parts),
        out_specs=[out_spec, out_spec],
        out_shape=[out, out],
        compiler_params=PARAMS,
        cost_estimate=pl.CostEstimate(
            flops=4 * parts * sources * experts * room * width * hidden,
            bytes_accessed=8 * experts * width * hidden,
            transcendentals=0,
        ),
        name="expert_grads",
    )(*tokens, *grads, *acts, *gpres)


def local(
    hidden_in, token_ids, hash_table, deal_order, qkv_weight, out_weight,
    norm1_gain, norm1_bias, norm2_gain, norm2_bias, expert_in, expert_out, out_grad,
):
    devices = lax.axis_size("ctx")
    position = lax.axis_index("ctx")
    planes = lax.axis_size("fsdp")
    plane = lax.axis_index("fsdp")
    width = hidden_in.shape[2]
    local_experts = expert_in.shape[0]
    experts = local_experts * devices
    room = 2 * TOK_DEV // experts
    all_slots = experts * room
    groups = gcd(HEADS, devices)
    cores = devices // groups
    group, core = position // cores, position % cores
    span = width // groups
    across = [[g * cores + c for g in range(groups)] for c in range(cores)]

    own_hidden = hidden_in[0]
    out_cot = out_grad[0]

    hidden = share(own_hidden, groups, "ctx", across).reshape(groups, TOK_DEV, width)
    cut = lambda part: lax.dynamic_slice_in_dim(qkv_weight, part * width + group * span, span, 1)
    vecs = jnp.stack([norm1_gain, norm1_bias, norm2_gain, norm2_bias], axis=1)
    own_cols = jnp.concatenate(
        [cut(0), cut(1), cut(2), jnp.pad(vecs, ((0, 0), (0, 60))), out_weight], axis=1
    )
    full = lax.all_gather(own_cols, "fsdp", axis=0, tiled=True)
    wt, out_full = full[:, : 3 * span].T, full[:, 3 * span + 64 :]
    vecs = full[:, 3 * span : 3 * span + 4].T.astype(f32)

    expert_of = hash_table[token_ids[0]]
    same = expert_of[:, None] == expert_of[None, :]
    shape = (TOK_DEV, TOK_DEV)
    before = lax.broadcasted_iota(jnp.int32, shape, 1) < lax.broadcasted_iota(jnp.int32, shape, 0)
    slot = expert_of * room + jnp.sum((same & before).astype(jnp.int32), axis=1)

    def spread(value):
        far = [None, None]
        for k in range(2, planes):
            far.append(swap(far[k - 1], "fsdp", 1) if k % 2 else swap(value, "fsdp", k))
        return far

    far_slots = spread(slot)
    counter = lambda axis: lax.broadcasted_iota(
        jnp.int32, (all_slots, TOK_DEV) if axis == 0 else (TOK_DEV, all_slots), axis
    )
    place = lambda s, rows: dot((counter(0) == s[None, :]).astype(bf16), rows).astype(bf16)
    fetch = lambda s, rows: dot((counter(1) == s[:, None]).astype(bf16), rows)
    shaped = (devices, local_experts, room, width)
    exchange = lambda rows: trade(
        rows.reshape(devices, local_experts * room, width), "ctx"
    ).reshape(shaped)

    evens = range(2, planes, 2)
    far_cots = {k: swap(out_cot, "fsdp", k) for k in evens}
    gys = [exchange(after(place(slot, out_cot), hidden))]
    gys.append(swap(gys[0], "fsdp", 1))
    for k in evens:
        gys.append(exchange(place(far_slots[k], far_cots[k])))
        gys.append(swap(gys[k], "fsdp", 1))

    own = project(hidden, wt, vecs)
    far = jnp.stack([swap(own[span:], "ctx", k) for k in range(1, cores)])
    order = deal_order.reshape(groups, cores)
    low = jnp.stack([lax.dynamic_index_in_dim(order, core ^ s, 1, False) for s in range(cores)])
    numbers = jnp.stack([low, 2 * devices - 1 - low], axis=2).reshape(-1)
    att, att_f, logs = attend(numbers, own, far)
    att_t = trade(att, "ctx", across).reshape(width, TOK_DEV)
    middle, normed, sent = middle_step(att_t, own_hidden, out_full, vecs, slot, all_slots)

    far_rows = spread(normed)
    tokens = [exchange(sent)]
    tokens.append(swap(tokens[0], "fsdp", 1))
    for k in range(2, planes):
        tokens.append(exchange(place(far_slots[k], far_rows[k])))
    acts, gpres, gns, eys = [], [], [], []
    for k in range(planes):
        act, gpre, gn, ey = expert_step(tokens[k], gys[k], expert_in, expert_out)
        acts.append(act)
        gpres.append(gpre)
        gns.append(gn)
        eys.append(ey)

    far_grad = jnp.zeros((TOK_DEV, width), f32)
    for k in evens:
        last = fetch(far_slots[k + 1], exchange(gns[k + 1]).reshape(all_slots, width)).astype(bf16)
        back = fetch(far_slots[k], exchange(gns[k]).reshape(all_slots, width))
        back = (back + swap(last, "fsdp", 1).astype(f32)).astype(bf16)
        far_grad = far_grad + swap(back, "fsdp", k).astype(f32)
    near = (gns[0].astype(f32) + swap(gns[1], "fsdp", 1).astype(f32)).astype(bf16)
    near = exchange(near).reshape(all_slots, width)
    grad_middle, branch, gatt, sums_two = turn_step(
        near, far_grad.astype(bf16), slot, middle, out_cot, out_full, vecs
    )
    gatt = trade(gatt.reshape(groups, span, TOK_DEV), "ctx", across)
    outs = out_grad_step(att_t, branch, sums_two)
    grad_expert_in, grad_expert_out = expert_grads(tokens, gys, acts, gpres)

    total_y = eys[0].astype(f32) + swap(eys[1], "fsdp", 1).astype(f32)
    for k in evens:
        back = (eys[k].astype(f32) + swap(eys[k + 1], "fsdp", 1).astype(f32)).astype(bf16)
        total_y = total_y + swap(back, "fsdp", k).astype(f32)
    token_y = fetch(slot, exchange(total_y.astype(bf16)).reshape(all_slots, width))
    layer_out = (middle + token_y).astype(bf16)

    gq, gown, gfar = attend_back(numbers, own, far, gatt, att_f, logs)
    got = jnp.stack([swap(gfar[k - 1], "ctx", k) for k in range(1, cores)])
    grad_rows, mixed = tail_step(gq, gown, got, hidden, wt, vecs, cores, planes)
    grad_rows = trade(grad_rows, "ctx", across)
    grad_normed = jnp.sum(grad_rows.astype(f32), axis=0)
    own_normal, own_scale = norm_stats(own_hidden.astype(f32))
    grad_hidden = grad_middle + norm_back(own_normal, own_scale, vecs[0], grad_normed)

    def keep(parts, index, axis, stride):
        pick = lambda k: lax.dynamic_index_in_dim(parts, index ^ k, 0, False)
        total = pick(0).astype(f32)
        for k in range(1, parts.shape[0]):
            total = total + swap(pick(k), axis, k * stride).astype(f32)
        return total.astype(bf16)

    def collect(part):
        pieces = [part] + [swap(part, "ctx", j * cores) for j in range(1, groups)]
        mine = jnp.stack(in_order(pieces, group))
        sides = in_order([mine] + [swap(mine, "ctx", k) for k in range(1, cores)], core)
        return jnp.stack(sides, axis=1).reshape((devices,) + part.shape)

    part = keep(keep(mixed, core, "ctx", 1), plane, "fsdp", 1)
    grad_qkv, vec_one = assemble(collect(part), span, groups)

    rows = width // planes
    wide = outs.shape[1]
    part = jnp.moveaxis(outs.reshape(planes, devices, rows // devices, wide), 1, 0)
    part = jnp.sum(trade(part, "ctx").astype(f32), axis=0).astype(bf16)
    part = keep(part, plane, "fsdp", 1)
    part = share(part, devices, "ctx").reshape(rows, wide).astype(f32)
    return (
        layer_out[None],
        grad_hidden[None],
        grad_qkv,
        part[:, :width],
        vec_one[:, 0],
        vec_one[:, 1],
        part[:, width],
        part[:, width + 1],
        grad_expert_in,
        grad_expert_out,
    )


def solution(mesh):
    return jax.shard_map(
        local,
        mesh=mesh,
        in_specs=(
            P("fsdp", "ctx", None),
            P("fsdp", "ctx"),
            P(),
            P(),
            P("fsdp", None),
            P("fsdp", None),
            P("fsdp"),
            P("fsdp"),
            P("fsdp"),
            P("fsdp"),
            P("ctx", None, "fsdp"),
            P("ctx", None, "fsdp"),
            P("fsdp", "ctx", None),
        ),
        out_specs=(
            P("fsdp", "ctx", None),
            P("fsdp", "ctx", None),
            P("fsdp", None),
            P("fsdp", None),
            P("fsdp"),
            P("fsdp"),
            P("fsdp"),
            P("fsdp"),
            P("ctx", None, "fsdp"),
            P("ctx", None, "fsdp"),
        ),
        check_vma=False,
    )
```

time: 1030 us -> 661 us (0.64)
  waiting for transfers between devices: 409 us -> 293 us
  starting transfers between devices: 201 us -> 90.1 us
  local copies, waits for them, and re-layouts: 141 us -> 36.8 us
  matrix products: 50.8 us -> 17.2 us
  other arithmetic: 39.4 us -> 21.9 us
    ppermute x142 -> x27, waiting for transfers between devices: 409 us -> 196 us  [swap(): return lax.ppermute(value, axis, [(i, i ^ offset) for i in range(size)])]
    ppermute x142 -> x27, starting transfers between devices: 201 us -> 27.6 us  [swap(): return lax.ppermute(value, axis, [(i, i ^ offset) for i in range(size)])]
    all_to_all x0 -> x15, starting transfers between devices: none -> 62.5 us  [trade(): lax.all_to_all(parts, axis, 0, 0, tiled=True, axis_index_groups=groups)]
    all_to_all x0 -> x15, waiting for transfers between devices: none -> 54.2 us  [trade(): lax.all_to_all(parts, axis, 0, 0, tiled=True, axis_index_groups=groups)]
    all_gather x0 -> x1, waiting for transfers between devices: none -> 43.1 us  [local(): full = lax.all_gather(own_cols, 'fsdp', axis=0, tiled=True)]
    unnamed x236 -> x57, local copies, waits for them, and re-layouts: 46.6 us -> 7.98 us
    dot_general x29 -> x7, matrix products: 50.8 us -> 17.2 us  [dot(): return lax.dot_general(a, b, dims, preferred_element_type=f32)]
    concatenate x22 -> x1, local copies, waits for them, and re-layouts: 25 us -> 1.86 us  [local(): jnp.concatenate([cut(0), cut(1), cut(2), jnp.pad(vecs, ((0, 0), (0, 60)))...]
  transfers between devices with their start and end apart: 142 -> 43, of which waited for: 69 -> 18; matrix products, arithmetic and copies ran while one was open for 21% -> 8% of each run, Pallas kernels for 17% -> 26%
where the time goes in v2:
time: 661 us; the launch traced here: 650 us
  waiting for transfers between devices  293 us (44%)
  Pallas kernels  176 us (27%)
  starting transfers between devices  90.1 us (14%)
  local copies, waits for them, and re-layouts  36.8 us (6%)
  other arithmetic  21.9 us (3%)
  matrix products  17.2 us (3%)
  between operations  14.8 us (2%)
    ppermute x27, waiting for transfers between devices, swap(): return lax.ppermute(value, axis, [(i, i ^ offset) for i in range(size)])  196 us
    all_to_all x15, starting transfers between devices, trade(): lax.all_to_all(parts, axis, 0, 0, tiled=True, axis_index_groups=groups)  62.5 us
    all_to_all x15, waiting for transfers between devices, trade(): lax.all_to_all(parts, axis, 0, 0, tiled=True, axis_index_groups=groups)  54.2 us
    pallas_call x1, Pallas kernels, attend_back(): pl.pallas_call(attend_back_kernel, grid_spec=pltpu.PrefetchScalarGridSpec...  49.9 us
    all_gather x1, waiting for transfers between devices, local(): full = lax.all_gather(own_cols, 'fsdp', axis=0, tiled=True)  43.1 us
    pallas_call x4, Pallas kernels, expert_step(): pl.pallas_call(expert_kernel, grid=(experts,), in_specs=[token_spec, toke...  40.7 us
    pallas_call x1, Pallas kernels, attend(): pl.pallas_call(attend_kernel, grid_spec=pltpu.PrefetchScalarGridSpec(num_...  32.9 us
    ppermute x27, starting transfers between devices, swap(): return lax.ppermute(value, axis, [(i, i ^ offset) for i in range(size)])  27.6 us
  transfers between devices with their start and end apart: 43, of which 18 were waited for; matrix products, arithmetic and copies ran while one was open for 8% of the time, Pallas kernels for 26%

profile of v2, /device:TPU:0, one launch (start us, length us, event | category | flops | bytes accessed | tf_op | source)
XLA Modules:
  0.0 650.0 jit_solution(933540602957293948)
XLA Ops:
  20.3 43.1 %all-gather.2.cloned.1.call-done = bf16[768,1408]{1,0:T(8,128)(2,1)} async-done(((bf16[192,1408]{1,0:T(8,128)(2,1)}), bf16[768,1408]{1,0:T(8,128)(2,1)}) %all-gather.2.cloned.1.call-update) | async-done | bytes 2162704 | tf_op jit(solution)/shard_map/all_gather | solution.py:588
  67.4 6.8 %project.1.q_ref.own_ref = bf16[576,2048]{1,0:T(8,128)(2,1)} custom-call(bf16[4,512,768]{2,1,0:T(8,128)(2,1)} %all-to-all-done.hidden_ref, bf16[576,768]{1,0:T(8,128)(2,1)} %bitcast.123, f32[4,768]{1,0:T(4,128)} %bitcast.128), custom_call_target="tpu_custom_call" | custom-call | flops 1811939328 | bytes 6291456 | tf_op jit(solution)/shard_map/project/pallas_call | solution.py:92
  84.6 29.4 %collective-permute-done.4 = s32[512]{0:T(512)S(1)} collective-permute-done((s32[512]{0:T(512)S(1)}, s32[512]{0:T(512)S(1)}, u32[]{:S(2)}, u32[]{:S(2)}) %collective-permute-start.4) | collective-permute-done | bytes 2080 | tf_op jit(solution)/shard_map/ppermute | solution.py:32
  121.6 32.9 %attend.1 = (bf16[4,192,512]{2,1,0:T(8,128)(2,1)}, f32[192,2048]{1,0:T(8,128)}, f32[8,8,256]{2,1,0:T(8,128)}) custom-call(s32[16]{0:T(128)} %reshape.212.number_ref, bf16[576,2048]{1,0:T(8,128)(2,1)} %project.1.q_ref.own_ref, bf16[576,2048]{1,0:T(8,128)(2,1)} %project.1.q_ref.own_ref, bf16[1,384,2048]{2,1,0:T(8,128)(2,1)} %bitcast.6.far_ref), custom_call_target="tpu_custom_call" | custom-call | flops 19327352832 | bytes 6291456 | tf_op jit(solution)/shard_map/attend/pallas_call | solution.py:183
  161.9 7.6 %all-to-all-done.1 = bf16[4,192,512]{2,1,0:T(8,128)(2,1)S(1)} async-done(((bf16[4,192,512]{2,1,0:T(8,128)(2,1)}), bf16[4,192,512]{2,1,0:T(8,128)(2,1)S(1)}, u32[]{:S(2)}, u32[]{:S(2)}) %all-to-all-start.1) | async-done | bytes 786464 | tf_op jit(solution)/shard_map/all_to_all | solution.py:36
  181.2 14.5 %all-to-all-done.3 = bf16[8,128,768]{2,1,0:T(8,128)(2,1)} async-done(((bf16[8,128,768]{2,1,0:T(8,128)(2,1)}), bf16[8,128,768]{2,1,0:T(8,128)(2,1)}, u32[]{:S(2)}, u32[]{:S(2)}) %all-to-all-start.3) | async-done | bytes 1572896 | tf_op jit(solution)/shard_map/all_to_all | solution.py:36
  199.6 18.6 %collective-permute-done.5 = bf16[512,768]{1,0:T(8,128)(2,1)S(1)} collective-permute-done((bf16[512,768]{1,0:T(8,128)(2,1)}, bf16[512,768]{1,0:T(8,128)(2,1)S(1)}, u32[]{:S(2)}, u32[]{:S(2)}) %collective-permute-start.5) | collective-permute-done | bytes 786464 | tf_op jit(solution)/shard_map/ppermute | solution.py:32
  220.2 17.5 %collective-permute-done.7 = s32[512]{0:T(512)S(1)} collective-permute-done((s32[512]{0:T(512)S(1)}, s32[512]{0:T(512)S(1)}, u32[]{:S(2)}, u32[]{:S(2)}) %collective-permute-start.7) | collective-permute-done | bytes 2080 | tf_op jit(solution)/shard_map/ppermute | solution.py:32
  247.4 17.4 %all-to-all-done.6 = bf16[8,128,768]{2,1,0:T(8,128)(2,1)S(1)} async-done(((bf16[8,128,768]{2,1,0:T(8,128)(2,1)}), bf16[8,128,768]{2,1,0:T(8,128)(2,1)S(1)}, u32[]{:S(2)}, u32[]{:S(2)}) %all-to-all-start.6) | async-done | bytes 1572896 | tf_op jit(solution)/shard_map/all_to_all | solution.py:36
  272.4 8.9 %collective-permute-done.9.gy_ref.refs_7_ = bf16[8,4,32,768]{3,2,1,0:T(8,128)(2,1)} collective-permute-done((bf16[8,4,32,768]{3,2,1,0:T(8,128)(2,1)}, bf16[8,4,32,768]{3,2,1,0:T(8,128)(2,1)}, u32[]{:S(2)}, u32[]{:S(2)}) %collective-permute-start.9) | collective-permute-done | bytes 1572896 | tf_op jit(solution)/shard_map/ppermute | solution.py:32
  281.3 10.2 %expert_step.7 = (bf16[8,4,32,768]{3,2,1,0:T(8,128)(2,1)}, bf16[8,4,32,768]{3,2,1,0:T(8,128)(2,1)}, bf16[8,4,32,768]{3,2,1,0:T(8,128)(2,1)}, bf16[8,4,32,768]{3,2,1,0:T(8,128)(2,1)}) custom-call(bf16[8,4,32,768]{3,2,1,0:T(8,128)(2,1)} %bitcast.111, bf16[8,4,32,768]{3,2,1,0:T(8,128)(2,1)} %collective-permute-done.9.gy_ref.refs_7_, ...), custom_call_target="tpu_custom_call" | custom-call | flops 4831838208 | bytes 18874368 | tf_op jit(solution)/shard_map/expert_step/pallas_call | solution.py:512
  295.7 19.3 %collective-permute-done.2.gy_ref.refs_5_ = bf16[8,4,32,768]{3,2,1,0:T(8,128)(2,1)} collective-permute-done((bf16[8,4,32,768]{3,2,1,0:T(8,128)(2,1)}, bf16[8,4,32,768]{3,2,1,0:T(8,128)(2,1)}, u32[]{:S(2)}, u32[]{:S(2)}) %collective-permute-start.2) | collective-permute-done | bytes 1572896 | tf_op jit(solution)/shard_map/ppermute | solution.py:32
  315.0 33.3 %collective-permute-done.1.x_ref.refs_1_ = bf16[8,4,32,768]{3,2,1,0:T(8,128)(2,1)} collective-permute-done((bf16[8,4,32,768]{3,2,1,0:T(8,128)(2,1)S(1)}, bf16[8,4,32,768]{3,2,1,0:T(8,128)(2,1)}, u32[]{:S(2)}, u32[]{:S(2)}) %collective-permute-start.1) | collective-permute-done | bytes 1572896 | tf_op jit(solution)/shard_map/ppermute | solution.py:32
  348.3 10.2 %expert_step.5 = (bf16[8,4,32,768]{3,2,1,0:T(8,128)(2,1)}, bf16[8,4,32,768]{3,2,1,0:T(8,128)(2,1)}, bf16[8,4,32,768]{3,2,1,0:T(8,128)(2,1)}, bf16[8,4,32,768]{3,2,1,0:T(8,128)(2,1)}) custom-call(bf16[8,4,32,768]{3,2,1,0:T(8,128)(2,1)} %collective-permute-done.1.x_ref.refs_1_, bf16[8,4,32,768]{3,2,1,0:T(8,128)(2,1)} %collective-permute-done.2.gy_ref.refs_5_, ...), custom_call_target="tpu_custom_call" | custom-call | flops 4831838208 | bytes 18874368 | tf_op jit(solution)/shard_map/expert_step/pallas_call | solution.py:512
  358.8 10.2 %expert_step.6 = (bf16[8,4,32,768]{3,2,1,0:T(8,128)(2,1)}, bf16[8,4,32,768]{3,2,1,0:T(8,128)(2,1)}, bf16[8,4,32,768]{3,2,1,0:T(8,128)(2,1)}, bf16[8,4,32,768]{3,2,1,0:T(8,128)(2,1)}) custom-call(bf16[8,4,32,768]{3,2,1,0:T(8,128)(2,1)} %bitcast.17.x_ref.refs_2_, bf16[8,4,32,768]{3,2,1,0:T(8,128)(2,1)} %bitcast.19.gy_ref.refs_6_, ...), custom_call_target="tpu_custom_call" | custom-call | flops 4831838208 | bytes 18874368 | tf_op jit(solution)/shard_map/expert_step/pallas_call | solution.py:512
  376.5 10.2 %expert_step.4 = (bf16[8,4,32,768]{3,2,1,0:T(8,128)(2,1)}, bf16[8,4,32,768]{3,2,1,0:T(8,128)(2,1)}, bf16[8,4,32,768]{3,2,1,0:T(8,128)(2,1)}, bf16[8,4,32,768]{3,2,1,0:T(8,128)(2,1)}) custom-call(bf16[8,4,32,768]{3,2,1,0:T(8,128)(2,1)} %bitcast.109, bf16[8,4,32,768]{3,2,1,0:T(8,128)(2,1)} %bitcast.15.gy_ref.refs_4_, bf16[4,768,768]{2,1,0:T(8,128)(2,1)} %first_ref.7, ...), custom_call_target="tpu_custom_call" | custom-call | flops 4831838208 | bytes 18874368 | tf_op jit(solution)/shard_map/expert_step/pallas_call | solution.py:512
  387.0 9.1 %collective-permute-done.12 = bf16[8,4,32,768]{3,2,1,0:T(8,128)(2,1)} collective-permute-done((bf16[8,4,32,768]{3,2,1,0:T(8,128)(2,1)}, bf16[8,4,32,768]{3,2,1,0:T(8,128)(2,1)}, u32[]{:S(2)}, u32[]{:S(2)}) %collective-permute-start.12) | collective-permute-done | bytes 1572896 | tf_op jit(solution)/shard_map/ppermute | solution.py:32
  404.7 8.3 %collective-permute-done.13 = bf16[512,768]{1,0:T(8,128)(2,1)} collective-permute-done((bf16[512,768]{1,0:T(8,128)(2,1)}, bf16[512,768]{1,0:T(8,128)(2,1)}, u32[]{:S(2)}, u32[]{:S(2)}) %collective-permute-start.13) | collective-permute-done | bytes 786464 | tf_op jit(solution)/shard_map/ppermute | solution.py:32
  416.0 8.6 %all-to-all-done.8 = bf16[8,128,768]{2,1,0:T(8,128)(2,1)S(1)} async-done(((bf16[8,128,768]{2,1,0:T(8,128)(2,1)}), bf16[8,128,768]{2,1,0:T(8,128)(2,1)S(1)}, u32[]{:S(2)}, u32[]{:S(2)}) %all-to-all-start.8) | async-done | bytes 1572896 | tf_op jit(solution)/shard_map/all_to_all | solution.py:36
  424.6 35.3 %collective-permute-done.14.far_ref = bf16[512,768]{1,0:T(8,128)(2,1)S(1)} collective-permute-done((bf16[512,768]{1,0:T(8,128)(2,1)S(1)}, bf16[512,768]{1,0:T(8,128)(2,1)S(1)}, u32[]{:S(2)}, u32[]{:S(2)}) %collective-permute-start.14) | collective-permute-done | bytes 786464 | tf_op jit(solution)/shard_map/ppermute | solution.py:32
  487.8 49.9 %attend_back.1 = (bf16[192,2048]{1,0:T(8,128)(2,1)}, bf16[384,2048]{1,0:T(8,128)(2,1)}, bf16[1,384,2048]{2,1,0:T(8,128)(2,1)}) custom-call(s32[16]{0:T(128)} %reshape.212.number_ref, bf16[576,2048]{1,0:T(8,128)(2,1)} %project.1.q_ref.own_ref, bf16[4,192,512]{2,1,0:T(8,128)(2,1)} %copy-done.14, f32[192,2048]{1,0:T(8,128)} %get-tuple-element.61.att_t_ref, ...), custom_call_target="tpu_custom_call" | custom-call | flops 48318382080 | bytes 12582912 | tf_op jit(solution)/shard_map/attend_back/pallas_call | solution.py:286
  542.9 6.9 %collective-permute-done.11 = bf16[8,4,32,768]{3,2,1,0:T(8,128)(2,1)} collective-permute-done((bf16[8,4,32,768]{3,2,1,0:T(8,128)(2,1)}, bf16[8,4,32,768]{3,2,1,0:T(8,128)(2,1)}, u32[]{:S(2)}, u32[]{:S(2)}) %collective-permute-start.11) | collective-permute-done | bytes 1572896 | tf_op jit(solution)/shard_map/ppermute | solution.py:32
  558.2 10.0 %tail.1 = (bf16[4,512,768]{2,1,0:T(8,128)(2,1)}, bf16[2,4,96,704]{3,2,1,0:T(8,128)(2,1)}) custom-call(bf16[192,2048]{1,0:T(8,128)(2,1)} %get-tuple-element.63.gq_ref, bf16[384,2048]{1,0:T(8,128)(2,1)} %get-tuple-element.64.gown_ref, bf16[1,384,2048]{2,1,0:T(8,128)(2,1)} %bitcast.34.got_ref, bf16[4,512,768]{2,1,0:T(8,128)(2,1)} %all-to-all-done.hidden_ref, ...), custom_call_target="tpu_custom_call" | custom-call | flops 3623878656 | bytes 9437184 | tf_op jit(solution)/shard_map/tail/pallas_call | solution.py:434
  601.5 17.5 %expert_grads.1 = (f32[4,768,768]{2,1,0:T(8,128)}, f32[4,768,768]{2,1,0:T(8,128)}) custom-call(bf16[8,4,32,768]{3,2,1,0:T(8,128)(2,1)} %bitcast.110, bf16[8,4,32,768]{3,2,1,0:T(8,128)(2,1)} %collective-permute-done.1.x_ref.refs_1_, bf16[8,4,32,768]{3,2,1,0:T(8,128)(2,1)} %bitcast.17.x_ref.refs_2_, bf16[8,4,32,768]{3,2,1,0:T(8,128)(2,1)} %bitcast.112, ...), custom_call_target="tpu_custom_call" | custom-call | flops 9663676416 | bytes 18874368 | tf_op jit(solution)/shard_map/expert_grads/pallas_call | solution.py:544
  (198 shorter events, 199.8 us)
Async XLA Ops:
  7.2 56.2 %all-gather.2.cloned.1.call-start = ((), (), s32[]{:S(2)}) async-start(), calls=%async_computation.15 | async-start | bytes 2703360 | tf_op jit(solution)/shard_map/all_gather | solution.py:588
  15.2 52.2 %all-to-all-start = ((bf16[4,512,768]{2,1,0:T(8,128)(2,1)}), bf16[4,512,768]{2,1,0:T(8,128)(2,1)}, u32[]{:S(2)}, u32[]{:S(2)}) async-start(bf16[4,512,768]{2,1,0:T(8,128)(2,1)} %broadcast_in_dim.11), calls=%async_computation | async-start | bytes 6291456 | tf_op jit(solution)/shard_map/all_to_all | solution.py:36
  77.0 44.5 %collective-permute-start = (bf16[384,2048]{1,0:T(8,128)(2,1)}, bf16[384,2048]{1,0:T(8,128)(2,1)}, u32[]{:S(2)}, u32[]{:S(2)}) collective-permute-start(bf16[384,2048]{1,0:T(8,128)(2,1)} %slice.44), channel_id=1, source_target_pairs={{0,4},{4,0},{8,12},{12,8},{16,20},{20,16},{24,28},{28,24},{1,5},{5... | collective-permute-start | bytes 4718600 | tf_op jit(solution)/shard_map/ppermute | solution.py:32
  77.0 36.9 %collective-permute-start.6 = (bf16[512,768]{1,0:T(8,128)(2,1)S(1)}, bf16[512,768]{1,0:T(8,128)(2,1)}, u32[]{:S(2)}, u32[]{:S(2)}) collective-permute-start(bf16[512,768]{1,0:T(8,128)(2,1)S(1)} %bitcast.127), channel_id=1, source_target_pairs={{0,2},{1,3},{2,0},{3,1},{4,6},{5,7},{6,4},{7,5},{8,10},{9,11},{10,... | collective-permute-start | bytes 2359304 | tf_op jit(solution)/shard_map/ppermute | solution.py:32
  81.3 32.6 %collective-permute-start.4 = (s32[512]{0:T(512)S(1)}, s32[512]{0:T(512)S(1)}, u32[]{:S(2)}, u32[]{:S(2)}) collective-permute-start(s32[512]{0:T(512)S(1)} %multiply_add_fusion), channel_id=1, source_target_pairs={{0,2},{1,3},{2,0},{3,1},{4,6},{5,7},{6,4},{7,5},{8,10},{9,11},{10,... | collective-permute-start | bytes 6152 | tf_op jit(solution)/shard_map/ppermute | solution.py:32
  117.2 37.2 %all-to-all-start.5 = ((bf16[8,128,768]{2,1,0:T(8,128)(2,1)}), bf16[8,128,768]{2,1,0:T(8,128)(2,1)}, u32[]{:S(2)}, u32[]{:S(2)}) async-start(bf16[8,128,768]{2,1,0:T(8,128)(2,1)} %bitcast.122), calls=%async_computation.5 | async-start | bytes 3145728 | tf_op jit(solution)/shard_map/all_to_all | solution.py:36
  181.2 37.0 %collective-permute-start.5 = (bf16[512,768]{1,0:T(8,128)(2,1)}, bf16[512,768]{1,0:T(8,128)(2,1)S(1)}, u32[]{:S(2)}, u32[]{:S(2)}) collective-permute-start(bf16[512,768]{1,0:T(8,128)(2,1)} %get-tuple-element.52), channel_id=1, source_target_pairs={{0,2},{1,3},{2,0},{3,1},{4,6},{5,7},{6,4},{7,5},{8,10},{9,11},{10,... | collective-permute-start | bytes 2359304 | tf_op jit(solution)/shard_map/ppermute | solution.py:32
  195.7 44.3 %all-to-all-start.2 = ((bf16[8,128,768]{2,1,0:T(8,128)(2,1)}), bf16[8,128,768]{2,1,0:T(8,128)(2,1)S(1)}, u32[]{:S(2)}, u32[]{:S(2)}) async-start(bf16[8,128,768]{2,1,0:T(8,128)(2,1)} %bitcast.116), calls=%async_computation.2 | async-start | bytes 3145728 | tf_op jit(solution)/shard_map/all_to_all | solution.py:36
  243.8 37.5 %collective-permute-start.9 = (bf16[8,4,32,768]{3,2,1,0:T(8,128)(2,1)}, bf16[8,4,32,768]{3,2,1,0:T(8,128)(2,1)}, u32[]{:S(2)}, u32[]{:S(2)}) collective-permute-start(bf16[8,4,32,768]{3,2,1,0:T(8,128)(2,1)} %bitcast.19.gy_ref.refs_6_), channel_id=1, source_target_pairs={{0,1},{1,0},{2,3},{3,2},{4,5},{5,4},{6,7},{7,6},{8,9},{9,8},{10,11... | collective-permute-start | bytes 4718600 | tf_op jit(solution)/shard_map/ppermute | solution.py:32
  266.0 25.5 %all-to-all-start.4 = ((bf16[8,128,768]{2,1,0:T(8,128)(2,1)}), bf16[8,128,768]{2,1,0:T(8,128)(2,1)}, u32[]{:S(2)}, u32[]{:S(2)}) async-start(bf16[8,128,768]{2,1,0:T(8,128)(2,1)} %bitcast.119), calls=%async_computation.4 | async-start | bytes 3145728 | tf_op jit(solution)/shard_map/all_to_all | solution.py:36
  270.3 44.7 %collective-permute-start.2 = (bf16[8,4,32,768]{3,2,1,0:T(8,128)(2,1)}, bf16[8,4,32,768]{3,2,1,0:T(8,128)(2,1)}, u32[]{:S(2)}, u32[]{:S(2)}) collective-permute-start(bf16[8,4,32,768]{3,2,1,0:T(8,128)(2,1)} %bitcast.15.gy_ref.refs_4_), channel_id=1, source_target_pairs={{0,1},{1,0},{2,3},{3,2},{4,5},{5,4},{6,7},{7,6},{8,9},{9,8},{10,11... | collective-permute-start | bytes 4718600 | tf_op jit(solution)/shard_map/ppermute | solution.py:32
  270.6 77.7 %collective-permute-start.1 = (bf16[8,4,32,768]{3,2,1,0:T(8,128)(2,1)S(1)}, bf16[8,4,32,768]{3,2,1,0:T(8,128)(2,1)}, u32[]{:S(2)}, u32[]{:S(2)}) collective-permute-start(bf16[8,4,32,768]{3,2,1,0:T(8,128)(2,1)S(1)} %bitcast.108), channel_id=1, source_target_pairs={{0,1},{1,0},{2,3},{3,2},{4,5},{5,4},{6,7},{7,6},{8,9},{9,8},{10,11... | collective-permute-start | bytes 4718600 | tf_op jit(solution)/shard_map/ppermute | solution.py:32
  291.4 77.5 %all-to-all-start.10 = ((bf16[8,128,768]{2,1,0:T(8,128)(2,1)}), bf16[8,128,768]{2,1,0:T(8,128)(2,1)S(1)}, u32[]{:S(2)}, u32[]{:S(2)}) async-start(bf16[8,128,768]{2,1,0:T(8,128)(2,1)} %bitcast.118), calls=%async_computation.10 | async-start | bytes 3145728 | tf_op jit(solution)/shard_map/all_to_all | solution.py:36
  358.5 37.6 %collective-permute-start.12 = (bf16[8,4,32,768]{3,2,1,0:T(8,128)(2,1)}, bf16[8,4,32,768]{3,2,1,0:T(8,128)(2,1)}, u32[]{:S(2)}, u32[]{:S(2)}) collective-permute-start(bf16[8,4,32,768]{3,2,1,0:T(8,128)(2,1)} %get-tuple-element.56), channel_id=1, source_target_pairs={{0,1},{1,0},{2,3},{3,2},{4,5},{5,4},{6,7},{7,6},{8,9},{9,8},{10,11... | collective-permute-start | bytes 4718600 | tf_op jit(solution)/shard_map/ppermute | solution.py:32
  369.0 30.8 %all-to-all-start.9 = ((bf16[8,128,768]{2,1,0:T(8,128)(2,1)}), bf16[8,128,768]{2,1,0:T(8,128)(2,1)S(1)}, u32[]{:S(2)}, u32[]{:S(2)}) async-start(bf16[8,128,768]{2,1,0:T(8,128)(2,1)} %bitcast.115), calls=%async_computation.9 | async-start | bytes 3145728 | tf_op jit(solution)/shard_map/all_to_all | solution.py:36
  374.8 38.2 %collective-permute-start.13 = (bf16[512,768]{1,0:T(8,128)(2,1)}, bf16[512,768]{1,0:T(8,128)(2,1)}, u32[]{:S(2)}, u32[]{:S(2)}) collective-permute-start(bf16[512,768]{1,0:T(8,128)(2,1)} %fusion.21), channel_id=1, source_target_pairs={{0,1},{1,0},{2,3},{3,2},{4,5},{5,4},{6,7},{7,6},{8,9},{9,8},{10,11... | collective-permute-start | bytes 2359304 | tf_op jit(solution)/shard_map/ppermute | solution.py:32
  386.7 87.3 %collective-permute-start.10 = (bf16[8,4,32,768]{3,2,1,0:T(8,128)(2,1)}, bf16[8,4,32,768]{3,2,1,0:T(8,128)(2,1)}, u32[]{:S(2)}, u32[]{:S(2)}) collective-permute-start(bf16[8,4,32,768]{3,2,1,0:T(8,128)(2,1)} %get-tuple-element.54), channel_id=1, source_target_pairs={{0,1},{1,0},{2,3},{3,2},{4,5},{5,4},{6,7},{7,6},{8,9},{9,8},{10,11... | collective-permute-start | bytes 4718600 | tf_op jit(solution)/shard_map/ppermute | solution.py:32
  414.3 45.7 %collective-permute-start.14 = (bf16[512,768]{1,0:T(8,128)(2,1)S(1)}, bf16[512,768]{1,0:T(8,128)(2,1)S(1)}, u32[]{:S(2)}, u32[]{:S(2)}) collective-permute-start(bf16[512,768]{1,0:T(8,128)(2,1)S(1)} %add_convert_fusion.3), channel_id=1, source_target_pairs={{0,2},{1,3},{2,0},{3,1},{4,6},{5,7},{6,4},{7,5},{8,10},{9,11},{10,... | collective-permute-start | bytes 2359304 | tf_op jit(solution)/shard_map/ppermute | solution.py:32
  471.0 71.0 %collective-permute-start.3 = (bf16[8,4,32,768]{3,2,1,0:T(8,128)(2,1)}, bf16[8,4,32,768]{3,2,1,0:T(8,128)(2,1)}, u32[]{:S(2)}, u32[]{:S(2)}) collective-permute-start(bf16[8,4,32,768]{3,2,1,0:T(8,128)(2,1)} %get-tuple-element.51), channel_id=1, source_target_pairs={{0,1},{1,0},{2,3},{3,2},{4,5},{5,4},{6,7},{7,6},{8,9},{9,8},{10,11... | collective-permute-start | bytes 4718600 | tf_op jit(solution)/shard_map/ppermute | solution.py:32
  477.2 72.6 %collective-permute-start.11 = (bf16[8,4,32,768]{3,2,1,0:T(8,128)(2,1)}, bf16[8,4,32,768]{3,2,1,0:T(8,128)(2,1)}, u32[]{:S(2)}, u32[]{:S(2)}) collective-permute-start(bf16[8,4,32,768]{3,2,1,0:T(8,128)(2,1)} %add_convert_fusion.2), channel_id=1, source_target_pairs={{0,2},{1,3},{2,0},{3,1},{4,6},{5,7},{6,4},{7,5},{8,10},{9,11},{10,... | collective-permute-start | bytes 4718600 | tf_op jit(solution)/shard_map/ppermute | solution.py:32
  483.5 54.7 %all-to-all-start.13 = ((bf16[8,4,24,896]{3,2,1,0:T(8,128)(2,1)}), bf16[8,4,24,896]{3,2,1,0:T(8,128)(2,1)S(1)}, u32[]{:S(2)}, u32[]{:S(2)}) async-start(bf16[8,4,24,896]{3,2,1,0:T(8,128)(2,1)} %bitcast.100), calls=%async_computation.13 | async-start | bytes 2752512 | tf_op jit(solution)/shard_map/all_to_all | solution.py:36
  569.9 26.7 %all-to-all-start.7 = ((bf16[8,128,768]{2,1,0:T(8,128)(2,1)}), bf16[8,128,768]{2,1,0:T(8,128)(2,1)S(1)}, u32[]{:S(2)}, u32[]{:S(2)}) async-start(bf16[8,128,768]{2,1,0:T(8,128)(2,1)} %bitcast.22), calls=%async_computation.7 | async-start | bytes 3145728 | tf_op jit(solution)/shard_map/all_to_all | solution.py:36
  593.1 26.0 %collective-permute-start.20 = (bf16[96,704]{1,0:T(8,128)(2,1)S(1)}, bf16[96,704]{1,0:T(8,128)(2,1)S(1)}, u32[]{:S(2)}, u32[]{:S(2)}) collective-permute-start(bf16[96,704]{1,0:T(8,128)(2,1)S(1)} %fusion.34), channel_id=1, source_target_pairs={{0,24},{4,28},{8,16},{12,20},{16,8},{20,12},{24,0},{28,4},{1,25},{... | collective-permute-start | bytes 405512 | tf_op jit(solution)/shard_map/ppermute | solution.py:32
  596.6 40.7 %all-to-all-start.12 = ((bf16[4,512,768]{2,1,0:T(8,128)(2,1)}), bf16[4,512,768]{2,1,0:T(8,128)(2,1)}, u32[]{:S(2)}, u32[]{:S(2)}) async-start(bf16[4,512,768]{2,1,0:T(8,128)(2,1)} %get-tuple-element.66), calls=%async_computation.12 | async-start | bytes 6291456 | tf_op jit(solution)/shard_map/all_to_all | solution.py:36
  (47 other events, 649.3 us)
Sparse Core Ops, SparseCore 0:
  13.4 49.9 all-gather.1

commit v3 on v2

--- a/solution.py
+++ b/solution.py
@@ -78,7 +78,7 @@
 
 
 def project_kernel(hidden_ref, wt_ref, vec_ref, out_ref):
-    normal, _ = norm_stats(hidden_ref[0].astype(f32))
+    normal, _ = norm_stats(hidden_ref[...].astype(f32))
     normed = (normal * vec_ref[0:1] + vec_ref[1:2]).astype(bf16)
     got = dot(wt_ref[...], normed, NT).astype(bf16)
     span = got.shape[0] // 3
@@ -87,20 +87,13 @@
 
 
 def project(hidden, wt, vecs):
-    sources, rows, width = hidden.shape
+    rows, width = hidden.shape
     wide = wt.shape[0]
     return pl.pallas_call(
         project_kernel,
-        grid=(sources,),
-        in_specs=[
-            pl.BlockSpec((1, rows, width), lambda i: (i, 0, 0)),
-            whole(wt.shape),
-            whole(vecs.shape),
-        ],
-        out_specs=pl.BlockSpec((wide, rows), lambda i: (0, i)),
-        out_shape=jax.ShapeDtypeStruct((wide, sources * rows), bf16),
-        compiler_params=PARAMS,
-        cost_estimate=cost(2 * sources * rows * width * wide, 4 * sources * rows * width),
+        out_shape=jax.ShapeDtypeStruct((wide, rows), bf16),
+        compiler_params=PARAMS,
+        cost_estimate=cost(2 * rows * width * wide, 4 * rows * width),
         name="project",
     )(hidden, wt, vecs)
 
@@ -113,18 +106,19 @@
     )
 
 
-def key_blocks(number_ref, span, own_ref, far_ref):
-    per = own_ref.shape[1] // BLK
-    for s in range(1 + far_ref.shape[0]):
+def key_blocks(number_ref, own_refs, far_refs):
+    span = own_refs[0].shape[0] // 3
+    per = own_refs[0].shape[1] // BLK
+    for p, ref in enumerate(own_refs + far_refs):
         for i in range(per):
-            at = pl.multiple_of(number_ref[s * per + i] * BLK, BLK)
+            at = pl.multiple_of(number_ref[p * per + i] * BLK, BLK)
             cut = slice(i * BLK, (i + 1) * BLK)
-            yield at, (own_ref[span:, cut] if s == 0 else far_ref[s - 1, :, cut])
-
-
-def attend_kernel(
-    number_ref, q_ref, own_ref, far_ref, att_ref, att_t_ref, lse_ref, acc_ref, k_sorted, v_sorted
-):
+            yield at, (ref[span:, cut] if p < len(own_refs) else ref[:, cut])
+
+
+def attend_kernel(pieces, sides, number_ref, order_ref, *refs):
+    own_refs, far_refs = refs[:pieces], refs[pieces : pieces * sides]
+    att_ref, att_t_ref, lse_ref, acc_ref, q_all, k_sorted, v_sorted = refs[pieces * sides :]
     turn = pl.program_id(0)
     span = acc_ref.shape[0]
     heads = span // HD
@@ -133,11 +127,15 @@
 
     @pl.when(turn == 0)
     def _():
-        for at, kv in key_blocks(number_ref, span, own_ref, far_ref):
+        for p, ref in enumerate(own_refs):
+            rows = ref.shape[1]
+            q_all[:, p * rows : (p + 1) * rows] = ref[:span, :]
+        for at, kv in key_blocks(number_ref, own_refs, far_refs):
             k_sorted[pl.ds(at, BLK), :] = jnp.transpose(kv[:span])
             v_sorted[:, pl.ds(at, BLK)] = kv[span:]
 
-    queries = [only_head(q_ref[...], h) for h in range(heads)]
+    own_queries = q_all[:, pl.ds(pl.multiple_of(turn * BLK, BLK), BLK)]
+    queries = [only_head(own_queries, h) for h in range(heads)]
     acc_ref[...] = jnp.zeros_like(acc_ref)
 
     def step(last, index, state):
@@ -176,46 +174,45 @@
         lse_ref[0, h : h + 1, :] = top[h] + jnp.log(total[h])
 
 
-def attend(numbers, own, far):
-    span, rows = own.shape[0] // 3, own.shape[1]
+def attend(numbers, order, own, far):
+    pieces, sides = len(own), 1 + len(far) // len(own)
+    span, piece = own[0].shape[0] // 3, own[0].shape[1]
+    rows = pieces * piece
     blocks = rows // BLK
-    keys = rows * (1 + far.shape[0])
-    return pl.pallas_call(
-        attend_kernel,
+    keys = rows * sides
+    return pl.pallas_call(
+        partial(attend_kernel, pieces, sides),
         grid_spec=pltpu.PrefetchScalarGridSpec(
-            num_scalar_prefetch=1,
+            num_scalar_prefetch=2,
             grid=(blocks,),
-            in_specs=[
-                pl.BlockSpec((span, BLK), lambda i, *_: (0, i)),
-                whole(own.shape),
-                whole(far.shape),
-            ],
+            in_specs=[whole(a.shape) for a in own + far],
             out_specs=[
-                pl.BlockSpec((1, span, BLK), lambda i, *_: (i // 2, 0, i % 2)),
+                pl.BlockSpec((1, span, BLK), lambda i, n, o: (o[i // 2], 0, i % 2)),
                 pl.BlockSpec((span, BLK), lambda i, *_: (0, i)),
                 pl.BlockSpec((1, 8, BLK), lambda i, *_: (i, 0, 0)),
             ],
             scratch_shapes=[
                 pltpu.VMEM((span, BLK), f32),
+                pltpu.VMEM((span, rows), bf16),
                 pltpu.VMEM((keys, span), bf16),
                 pltpu.VMEM((span, keys), bf16),
             ],
         ),
         out_shape=[
-            jax.ShapeDtypeStruct((blocks // 2, span, 2 * BLK), bf16),
+            jax.ShapeDtypeStruct((pieces, span, piece), bf16),
             jax.ShapeDtypeStruct((span, rows), f32),
             jax.ShapeDtypeStruct((blocks, 8, BLK), f32),
         ],
         compiler_params=PARAMS,
         cost_estimate=cost(12 * rows * keys * span, 8 * keys * span, rows * keys * span // 128),
         name="attend",
-    )(numbers, own, own, far)
-
-
-def attend_back_kernel(
-    number_ref, q_ref, g_ref, att_t_ref, lse_ref, own_ref, far_ref, gq_ref, gown_ref, gfar_ref,
-    gq_acc, gk_acc, gv_acc, k_sorted, v_sorted, kt_sorted,
-):
+    )(numbers, order, *own, *far)
+
+
+def attend_back_kernel(pieces, sides, number_ref, order_ref, g_ref, att_t_ref, lse_ref, *refs):
+    own_refs, far_refs = refs[:pieces], refs[pieces : pieces * sides]
+    gq_ref, gown_ref, gfar_ref = refs[pieces * sides : pieces * sides + 3]
+    gq_acc, gk_acc, gv_acc, q_all, k_sorted, v_sorted, kt_sorted = refs[pieces * sides + 3 :]
     turn = pl.program_id(0)
     span = gq_acc.shape[0]
     heads = span // HD
@@ -226,17 +223,21 @@
     def _():
         gk_acc[...] = jnp.zeros_like(gk_acc)
         gv_acc[...] = jnp.zeros_like(gv_acc)
-        for at, kv in key_blocks(number_ref, span, own_ref, far_ref):
+        for p, ref in enumerate(own_refs):
+            rows = ref.shape[1]
+            q_all[:, p * rows : (p + 1) * rows] = ref[:span, :]
+        for at, kv in key_blocks(number_ref, own_refs, far_refs):
             k_sorted[pl.ds(at, BLK), :] = jnp.transpose(kv[:span])
             v_sorted[pl.ds(at, BLK), :] = jnp.transpose(kv[span:])
             kt_sorted[:, pl.ds(at, BLK)] = kv[:span]
 
     grads = g_ref[0]
+    queries = q_all[:, pl.ds(pl.multiple_of(turn * BLK, BLK), BLK)]
     prod = grads.astype(f32) * att_t_ref[...]
     part = lambda h: slice(h * HD, (h + 1) * HD)
     deltas = [jnp.sum(prod[part(h)], axis=0, keepdims=True) for h in range(heads)]
     logs = [lse_ref[0, h : h + 1, :] for h in range(heads)]
-    q_only = [only_head(q_ref[...], h) for h in range(heads)]
+    q_only = [only_head(queries, h) for h in range(heads)]
     g_only = [only_head(grads, h) for h in range(heads)]
     gq_acc[...] = jnp.zeros_like(gq_acc)
 
@@ -255,7 +256,7 @@
             gs = (probs * (dot(values, g_only[h]) - deltas[h])).astype(bf16)
             gq_acc[rows, :] += dot(kt_sorted[rows, pl.ds(at, size)], gs)
             gv_acc[rows, pl.ds(at, size)] += dot(grads[rows], probs.astype(bf16), NT)
-            gk_acc[rows, pl.ds(at, size)] += dot(q_ref[rows, :], gs, NT)
+            gk_acc[rows, pl.ds(at, size)] += dot(queries[rows], gs, NT)
         return carry
 
     full = (block + 1) // CHUNK
@@ -265,8 +266,8 @@
 
     @pl.when(turn == pl.num_programs(0) - 1)
     def _():
-        per = own_ref.shape[1] // BLK
-        for s in range(1 + far_ref.shape[0]):
+        per = gown_ref.shape[1] // BLK
+        for s in range(sides):
             for i in range(per):
                 at = pl.multiple_of(number_ref[s * per + i] * BLK, BLK)
                 cut = slice(i * BLK, (i + 1) * BLK)
@@ -278,29 +279,30 @@
                     gfar_ref[s - 1, :span, cut], gfar_ref[s - 1, span:, cut] = gk, gv
 
 
-def attend_back(numbers, own, far, grads, att_t, logs):
-    span, rows = own.shape[0] // 3, own.shape[1]
+def attend_back(numbers, order, own, far, grads, att_t, logs):
+    pieces, sides = len(own), 1 + len(far) // len(own)
+    span, piece = own[0].shape[0] // 3, own[0].shape[1]
+    rows = pieces * piece
     blocks = rows // BLK
-    keys = rows * (1 + far.shape[0])
+    keys = rows * sides
     column = pl.BlockSpec((span, BLK), lambda i, *_: (0, i))
     return pl.pallas_call(
-        attend_back_kernel,
+        partial(attend_back_kernel, pieces, sides),
         grid_spec=pltpu.PrefetchScalarGridSpec(
-            num_scalar_prefetch=1,
+            num_scalar_prefetch=2,
             grid=(blocks,),
             in_specs=[
-                column,
-                pl.BlockSpec((1, span, BLK), lambda i, *_: (i // 2, 0, i % 2)),
+                pl.BlockSpec((1, span, BLK), lambda i, n, o: (o[i // 2], 0, i % 2)),
                 column,
                 pl.BlockSpec((1, 8, BLK), lambda i, *_: (i, 0, 0)),
-                whole(own.shape),
-                whole(far.shape),
-            ],
-            out_specs=[column, whole((2 * span, rows)), whole(far.shape)],
+            ]
+            + [whole(a.shape) for a in own + far],
+            out_specs=[column, whole((2 * span, rows)), whole((sides - 1, 2 * span, rows))],
             scratch_shapes=[
                 pltpu.VMEM((span, BLK), f32),
                 pltpu.VMEM((span, keys), f32),
                 pltpu.VMEM((span, keys), f32),
+                pltpu.VMEM((span, rows), bf16),
                 pltpu.VMEM((keys, span), bf16),
                 pltpu.VMEM((keys, span), bf16),
                 pltpu.VMEM((span, keys), bf16),
@@ -309,12 +311,12 @@
         out_shape=[
             jax.ShapeDtypeStruct((span, rows), bf16),
             jax.ShapeDtypeStruct((2 * span, rows), bf16),
-            jax.ShapeDtypeStruct(far.shape, bf16),
+            jax.ShapeDtypeStruct((sides - 1, 2 * span, rows), bf16),
         ],
         compiler_params=PARAMS,
         cost_estimate=cost(30 * rows * keys * span, 16 * keys * span, rows * keys * span // 128),
         name="attend_back",
-    )(numbers, own, grads, att_t, logs, own, far)
+    )(numbers, order, grads, att_t, logs, *own, *far)
 
 
 def middle_kernel(att_ref, x_ref, w_ref, vec_ref, slot_ref, mid_ref, normed_ref, send_ref):
@@ -392,69 +394,76 @@
     )(att_t, gbr, sums)
 
 
-def tail_kernel(
-    gq_ref, gown_ref, got_ref, hidden_ref, wt_ref, vec_ref, rows_ref, mixed_ref, gw_acc, sum_acc
-):
-    turn = pl.program_id(0)
-
-    @pl.when(turn == 0)
-    def _():
-        gw_acc[...] = jnp.zeros_like(gw_acc)
-        sum_acc[...] = jnp.zeros_like(sum_acc)
-
+def rows_kernel(gq_ref, gown_ref, got_ref, wt_ref, rows_ref, cols_ref):
     gkv = gown_ref[...].astype(f32)
     for k in range(got_ref.shape[0]):
         gkv = gkv + got_ref[k].astype(f32)
     columns = jnp.concatenate([gq_ref[...], gkv.astype(bf16)], axis=0)
-    rows = dot(columns, wt_ref[...], TN)
-    rows_ref[0] = rows.astype(bf16)
-    normal, _ = norm_stats(hidden_ref[0].astype(f32))
-    normed = (normal * vec_ref[0:1] + vec_ref[1:2]).astype(bf16)
-    sum_acc[0:1] += jnp.sum(rows * normal, axis=0, keepdims=True)
-    sum_acc[1:2] += jnp.sum(rows, axis=0, keepdims=True)
-    gw_acc[...] += dot(columns, normed)
-
-    @pl.when(turn == pl.num_programs(0) - 1)
-    def _():
-        cores, planes, count, _ = mixed_ref.shape
-        wide = gw_acc.shape[0]
-        weights = jnp.transpose(gw_acc[...]).astype(bf16)
-        sums = jnp.transpose(sum_acc[...]).astype(bf16)
-        for z in range(planes):
-            for s in range(cores):
-                at = (z * cores + s) * count
-                mixed_ref[s, z, :, :wide] = weights[at : at + count]
-                mixed_ref[s, z, :, wide:] = sums[at : at + count]
-
-
-def tail_step(gq, gown, got, hidden, wt, vecs, cores, planes):
-    sources, rows, width = hidden.shape
-    wide = wt.shape[0]
-    count = width // (cores * planes)
-    return pl.pallas_call(
-        tail_kernel,
+    cols_ref[...] = columns
+    rows_ref[0] = dot(columns, wt_ref[...], TN).astype(bf16)
+
+
+def rows_step(gq, gown, got, wt, rows):
+    sources = gq.shape[1] // rows
+    wide, width = wt.shape
+    return pl.pallas_call(
+        rows_kernel,
         grid=(sources,),
         in_specs=[
             pl.BlockSpec((gq.shape[0], rows), lambda i: (0, i)),
             pl.BlockSpec((gown.shape[0], rows), lambda i: (0, i)),
             pl.BlockSpec((got.shape[0], gown.shape[0], rows), lambda i: (0, 0, i)),
-            pl.BlockSpec((1, rows, width), lambda i: (i, 0, 0)),
             whole(wt.shape),
-            whole(vecs.shape),
         ],
         out_specs=[
             pl.BlockSpec((1, rows, width), lambda i: (i, 0, 0)),
-            whole((cores, planes, count, wide + 128)),
+            pl.BlockSpec((wide, rows), lambda i: (0, i)),
         ],
         out_shape=[
             jax.ShapeDtypeStruct((sources, rows, width), bf16),
-            jax.ShapeDtypeStruct((cores, planes, count, wide + 128), bf16),
+            jax.ShapeDtypeStruct((wide, sources * rows), bf16),
         ],
-        scratch_shapes=[pltpu.VMEM((wide, width), f32), pltpu.VMEM((128, width), f32)],
-        compiler_params=PARAMS,
-        cost_estimate=cost(4 * sources * rows * width * wide, 6 * sources * rows * width),
-        name="tail",
-    )(gq, gown, got, hidden, wt, vecs)
+        compiler_params=PARAMS,
+        cost_estimate=cost(2 * sources * rows * width * wide, 4 * sources * rows * width),
+        name="rows",
+    )(gq, gown, got, wt)
+
+
+def weights_kernel(cols_ref, rows_ref, vec_ref, *refs):
+    sources = rows_ref.shape[0]
+    hidden_refs, mixed_ref = refs[:sources], refs[sources]
+    piece = rows_ref.shape[1]
+    total, gains, biases = None, 0.0, 0.0
+    for j, ref in enumerate(hidden_refs):
+        normal, _ = norm_stats(ref[...].astype(f32))
+        normed = (normal * vec_ref[0:1] + vec_ref[1:2]).astype(bf16)
+        rows = rows_ref[j].astype(f32)
+        gains += jnp.sum(rows * normal, axis=0, keepdims=True)
+        biases += jnp.sum(rows, axis=0, keepdims=True)
+        part = dot(cols_ref[:, j * piece : (j + 1) * piece], normed)
+        total = part if total is None else total + part
+    cores, planes, count, _ = mixed_ref.shape
+    wide = total.shape[0]
+    weights = jnp.transpose(total).astype(bf16)
+    zeros = jnp.zeros((126, total.shape[1]), f32)
+    sums = jnp.transpose(jnp.concatenate([gains, biases, zeros], axis=0)).astype(bf16)
+    for z in range(planes):
+        for s in range(cores):
+            at = (z * cores + s) * count
+            mixed_ref[s, z, :, :wide] = weights[at : at + count]
+            mixed_ref[s, z, :, wide:] = sums[at : at + count]
+
+
+def weights_step(cols, rows, vecs, hidden, cores, planes):
+    wide, width = cols.shape[0], rows.shape[2]
+    shape = (cores, planes, width // (cores * planes), wide + 128)
+    return pl.pallas_call(
+        weights_kernel,
+        out_shape=jax.ShapeDtypeStruct(shape, bf16),
+        compiler_params=PARAMS,
+        cost_estimate=cost(2 * cols.size * width, 4 * rows.size),
+        name="weights",
+    )(cols, rows, vecs, *hidden)
 
 
 def assemble_kernel(span, groups, part_ref, out_ref, sum_ref):
@@ -579,16 +588,6 @@
     own_hidden = hidden_in[0]
     out_cot = out_grad[0]
 
-    hidden = share(own_hidden, groups, "ctx", across).reshape(groups, TOK_DEV, width)
-    cut = lambda part: lax.dynamic_slice_in_dim(qkv_weight, part * width + group * span, span, 1)
-    vecs = jnp.stack([norm1_gain, norm1_bias, norm2_gain, norm2_bias], axis=1)
-    own_cols = jnp.concatenate(
-        [cut(0), cut(1), cut(2), jnp.pad(vecs, ((0, 0), (0, 60))), out_weight], axis=1
-    )
-    full = lax.all_gather(own_cols, "fsdp", axis=0, tiled=True)
-    wt, out_full = full[:, : 3 * span].T, full[:, 3 * span + 64 :]
-    vecs = full[:, 3 * span : 3 * span + 4].T.astype(f32)
-
     expert_of = hash_table[token_ids[0]]
     same = expert_of[:, None] == expert_of[None, :]
     shape = (TOK_DEV, TOK_DEV)
@@ -601,39 +600,59 @@
             far.append(swap(far[k - 1], "fsdp", 1) if k % 2 else swap(value, "fsdp", k))
         return far
 
-    far_slots = spread(slot)
     counter = lambda axis: lax.broadcasted_iota(
         jnp.int32, (all_slots, TOK_DEV) if axis == 0 else (TOK_DEV, all_slots), axis
     )
     place = lambda s, rows: dot((counter(0) == s[None, :]).astype(bf16), rows).astype(bf16)
     fetch = lambda s, rows: dot((counter(1) == s[:, None]).astype(bf16), rows)
+    packed = (devices, local_experts * room, width)
     shaped = (devices, local_experts, room, width)
-    exchange = lambda rows: trade(
-        rows.reshape(devices, local_experts * room, width), "ctx"
-    ).reshape(shaped)
-
+    exchange = lambda rows: trade(rows.reshape(packed), "ctx").reshape(shaped)
     evens = range(2, planes, 2)
+
+    cut = lambda part: lax.dynamic_slice_in_dim(qkv_weight, part * width + group * span, span, 1)
+    vecs = jnp.stack([norm1_gain, norm1_bias, norm2_gain, norm2_bias], axis=1)
+    own_cols = jnp.concatenate(
+        [cut(0), cut(1), cut(2), jnp.pad(vecs, ((0, 0), (0, 60)))], axis=1
+    )
+    full = lax.all_gather(own_cols, "fsdp", axis=0, tiled=True)
+    wt, vecs = full[:, : 3 * span].T, full[:, 3 * span : 3 * span + 4].T.astype(f32)
+    hidden = [own_hidden] + [swap(own_hidden, "ctx", j * cores) for j in range(1, groups)]
     far_cots = {k: swap(out_cot, "fsdp", k) for k in evens}
-    gys = [exchange(after(place(slot, out_cot), hidden))]
-    gys.append(swap(gys[0], "fsdp", 1))
-    for k in evens:
-        gys.append(exchange(place(far_slots[k], far_cots[k])))
-        gys.append(swap(gys[k], "fsdp", 1))
-
-    own = project(hidden, wt, vecs)
-    far = jnp.stack([swap(own[span:], "ctx", k) for k in range(1, cores)])
-    order = deal_order.reshape(groups, cores)
-    low = jnp.stack([lax.dynamic_index_in_dim(order, core ^ s, 1, False) for s in range(cores)])
+    far_slots = spread(slot)
+
+    near_first = [place(slot, out_cot)] + [place(far_slots[k], far_cots[k]) for k in evens]
+    sides = len(near_first)
+    stacked = after(jnp.stack([p.reshape(packed) for p in near_first], axis=1), *hidden)
+    got_near = trade(stacked, "ctx")
+    got_far = swap(got_near, "fsdp", 1)
+    gys = [None] * planes
+    for i, k in enumerate([0, *evens]):
+        gys[k] = got_near[:, i].reshape(shaped)
+        gys[k + 1] = got_far[:, i].reshape(shaped)
+
+    own = [project(h, wt, vecs) for h in hidden]
+    far = [swap(o[span:], "ctx", k) for k in range(1, cores) for o in own]
+    out_full = lax.all_gather(out_weight, "fsdp", axis=0, tiled=True)
+    table = deal_order.reshape(groups, cores)
+    order = group ^ jnp.arange(groups, dtype=jnp.int32)
+    low = jnp.stack(
+        [lax.dynamic_index_in_dim(table, core ^ s, 1, False)[order] for s in range(cores)]
+    )
     numbers = jnp.stack([low, 2 * devices - 1 - low], axis=2).reshape(-1)
-    att, att_f, logs = attend(numbers, own, far)
+    att, att_f, logs = attend(numbers, order, own, far)
+    att = after(att, got_near)
     att_t = trade(att, "ctx", across).reshape(width, TOK_DEV)
     middle, normed, sent = middle_step(att_t, own_hidden, out_full, vecs, slot, all_slots)
 
-    far_rows = spread(normed)
     tokens = [exchange(sent)]
     tokens.append(swap(tokens[0], "fsdp", 1))
-    for k in range(2, planes):
-        tokens.append(exchange(place(far_slots[k], far_rows[k])))
+    for k in evens:
+        rows = swap(normed, "fsdp", k)
+        send = place(far_slots[k], after(rows, got_far))
+        tokens.append(exchange(send))
+        rows = swap(after(rows, send), "fsdp", 1)
+        tokens.append(exchange(place(far_slots[k + 1], rows)))
     acts, gpres, gns, eys = [], [], [], []
     for k in range(planes):
         act, gpre, gn, ey = expert_step(tokens[k], gys[k], expert_in, expert_out)
@@ -641,6 +660,7 @@
         gpres.append(gpre)
         gns.append(gn)
         eys.append(ey)
+    grad_expert_in, grad_expert_out = expert_grads(tokens, gys, acts, gpres)
 
     far_grad = jnp.zeros((TOK_DEV, width), f32)
     for k in evens:
@@ -650,12 +670,12 @@
         far_grad = far_grad + swap(back, "fsdp", k).astype(f32)
     near = (gns[0].astype(f32) + swap(gns[1], "fsdp", 1).astype(f32)).astype(bf16)
     near = exchange(near).reshape(all_slots, width)
+    far_grad = after(far_grad.astype(bf16), near, grad_expert_in)
     grad_middle, branch, gatt, sums_two = turn_step(
-        near, far_grad.astype(bf16), slot, middle, out_cot, out_full, vecs
+        near, far_grad, slot, middle, out_cot, out_full, vecs
     )
     gatt = trade(gatt.reshape(groups, span, TOK_DEV), "ctx", across)
     outs = out_grad_step(att_t, branch, sums_two)
-    grad_expert_in, grad_expert_out = expert_grads(tokens, gys, acts, gpres)
 
     total_y = eys[0].astype(f32) + swap(eys[1], "fsdp", 1).astype(f32)
     for k in evens:
@@ -664,11 +684,13 @@
     token_y = fetch(slot, exchange(total_y.astype(bf16)).reshape(all_slots, width))
     layer_out = (middle + token_y).astype(bf16)
 
-    gq, gown, gfar = attend_back(numbers, own, far, gatt, att_f, logs)
+    gq, gown, gfar = attend_back(numbers, order, own, far, gatt, att_f, logs)
     got = jnp.stack([swap(gfar[k - 1], "ctx", k) for k in range(1, cores)])
-    grad_rows, mixed = tail_step(gq, gown, got, hidden, wt, vecs, cores, planes)
-    grad_rows = trade(grad_rows, "ctx", across)
-    grad_normed = jnp.sum(grad_rows.astype(f32), axis=0)
+    grad_rows, grad_cols = rows_step(gq, gown, got, wt, TOK_DEV)
+    grad_normed = grad_rows[0].astype(f32)
+    for j in range(1, groups):
+        grad_normed = grad_normed + swap(grad_rows[j], "ctx", j * cores).astype(f32)
+    mixed = weights_step(grad_cols, grad_rows, vecs, hidden, cores, planes)
     own_normal, own_scale = norm_stats(own_hidden.astype(f32))
     grad_hidden = grad_middle + norm_back(own_normal, own_scale, vecs[0], grad_normed)
 
@@ -679,14 +701,8 @@
             total = total + swap(pick(k), axis, k * stride).astype(f32)
         return total.astype(bf16)
 
-    def collect(part):
-        pieces = [part] + [swap(part, "ctx", j * cores) for j in range(1, groups)]
-        mine = jnp.stack(in_order(pieces, group))
-        sides = in_order([mine] + [swap(mine, "ctx", k) for k in range(1, cores)], core)
-        return jnp.stack(sides, axis=1).reshape((devices,) + part.shape)
-
     part = keep(keep(mixed, core, "ctx", 1), plane, "fsdp", 1)
-    grad_qkv, vec_one = assemble(collect(part), span, groups)
+    grad_qkv, vec_one = assemble(share(part, devices, "ctx"), span, groups)
 
     rows = width // planes
     wide = outs.shape[1]

time: 661 us -> 609 us (0.921)
  waiting for transfers between devices: 293 us -> 200 us
  blocking collectives: 0 us -> 22.5 us
  Pallas kernels: 176 us -> 188 us
    ppermute x27 -> x31, waiting for transfers between devices: 196 us -> 152 us  [swap(): return lax.ppermute(value, axis, [(i, i ^ offset) for i in range(size)])]
    all_gather x1, waiting for transfers between devices: 43.1 us -> 0.02 us  [local(): out_full = lax.all_gather(out_weight, 'fsdp', axis=0, tiled=True)]
    all_gather x0 -> x1, blocking collectives: none -> 22.5 us  [local(): full = lax.all_gather(own_cols, 'fsdp', axis=0, tiled=True)]
    ppermute x27 -> x31, starting transfers between devices: 27.6 us -> 40.6 us  [swap(): return lax.ppermute(value, axis, [(i, i ^ offset) for i in range(size)])]
    pallas_call x4 -> x8, Pallas kernels: 99.6 us -> 112 us  [the longest x1 50.3 us: attend_back(): pl.pallas_call(partial(attend_back_kernel, pieces, sides), grid_spec=pltp...]
    all_to_all x15 -> x13, starting transfers between devices: 62.5 us -> 54.7 us  [trade(): lax.all_to_all(parts, axis, 0, 0, tiled=True, axis_index_groups=groups)]
    slice x4 -> x6, local copies, waits for them, and re-layouts: 5.73 us -> 12.8 us  [the longest x4 7.08 us: local(): far = [swap(o[span:], 'ctx', k) for k in range(1, cores) for o in own]]
    all_to_all x15 -> x13, waiting for transfers between devices: 54.2 us -> 47.5 us  [trade(): lax.all_to_all(parts, axis, 0, 0, tiled=True, axis_index_groups=groups)]
  transfers between devices with their start and end apart: 43 -> 45, of which waited for: 18 -> 17; matrix products, arithmetic and copies ran while one was open for 8% -> 13% of each run, Pallas kernels for 26% -> 31%
where the time goes in v3:
time: 609 us; the launch traced here: 603 us
  waiting for transfers between devices  200 us (33%)
  Pallas kernels  188 us (31%)
  starting transfers between devices  95.3 us (16%)
  local copies, waits for them, and re-layouts  41.1 us (7%)
  other arithmetic  24.5 us (4%)
  blocking collectives  22.5 us (4%)
  matrix products  16.6 us (3%)
  between operations  14.9 us (2%)
    ppermute x31, waiting for transfers between devices, swap(): return lax.ppermute(value, axis, [(i, i ^ offset) for i in range(size)])  152 us
    all_to_all x13, starting transfers between devices, trade(): lax.all_to_all(parts, axis, 0, 0, tiled=True, axis_index_groups=groups)  54.7 us
    pallas_call x1, Pallas kernels, attend_back(): pl.pallas_call(partial(attend_back_kernel, pieces, sides), grid_spec=pltp...  50.3 us
    all_to_all x13, waiting for transfers between devices, trade(): lax.all_to_all(parts, axis, 0, 0, tiled=True, axis_index_groups=groups)  47.5 us
    pallas_call x4, Pallas kernels, expert_step(): pl.pallas_call(expert_kernel, grid=(experts,), in_specs=[token_spec, toke...  40.7 us
    ppermute x31, starting transfers between devices, swap(): return lax.ppermute(value, axis, [(i, i ^ offset) for i in range(size)])  40.6 us
    pallas_call x1, Pallas kernels, attend(): pl.pallas_call(partial(attend_kernel, pieces, sides), grid_spec=pltpu.Pre...  32.8 us
    all_gather x1, blocking collectives, local(): full = lax.all_gather(own_cols, 'fsdp', axis=0, tiled=True)  22.5 us
  transfers between devices with their start and end apart: 45, of which 17 were waited for; matrix products, arithmetic and copies ran while one was open for 13% of the time, Pallas kernels for 31%

profile of v3, /device:TPU:0, one launch (start us, length us, event | category | flops | bytes accessed | tf_op | source)
XLA Modules:
  0.0 603.3 jit_solution(9745157766095607072)
XLA Ops:
  20.1 28.7 %collective-permute-done.7 = s32[512]{0:T(512)S(1)} collective-permute-done((s32[512]{0:T(512)S(1)}, s32[512]{0:T(512)S(1)}, u32[]{:S(2)}, u32[]{:S(2)}) %collective-permute-start.7) | collective-permute-done | bytes 2080 | tf_op jit(solution)/shard_map/ppermute | solution.py:32
  59.8 22.5 %all_gather.6 = bf16[768,640]{1,0:T(8,128)(2,1)} all-gather(bf16[192,640]{1,0:T(8,128)(2,1)S(1)} %fusion.39), channel_id=1, replica_groups=mesh['ctx'=8,'fsdp'=4] {'fsdp'}, dimensions={0}, use_global_device_ids=true | all-gather | bytes 1228800 | tf_op jit(solution)/shard_map/all_gather | solution.py:618
  112.6 32.8 %attend.1 = (bf16[4,192,512]{2,1,0:T(8,128)(2,1)}, f32[192,2048]{1,0:T(8,128)}, f32[8,8,256]{2,1,0:T(8,128)}) custom-call(s32[16]{0:T(128)} %reshape.214.number_ref, s32[4]{0:T(128)} %iota_xor_fusion.order_ref, bf16[576,512]{1,0:T(8,128)(2,1)} %project.4.refs_0_, bf16[576,512]{1,0:T(8,128)(2,1)} %project.5.refs_1_, bf16[576,512]{1,0:T(8,128)(2,1)} %project.6.refs_2_, ...), custom_call_target="tpu_custom_call" | custom-call | flops 19327352832 | bytes 6291456 | tf_op jit(solution)/shard_map/attend/pallas_call | solution.py:183
  149.6 11.9 %all-to-all-done.1 = bf16[4,192,512]{2,1,0:T(8,128)(2,1)} async-done(((bf16[4,192,512]{2,1,0:T(8,128)(2,1)}), bf16[4,192,512]{2,1,0:T(8,128)(2,1)}, u32[]{:S(2)}, u32[]{:S(2)}) %all-to-all-start.1) | async-done | bytes 786464 | tf_op jit(solution)/shard_map/all_to_all | solution.py:36
  161.5 5.5 middle.1
  173.3 31.7 %collective-permute-done.12 = bf16[512,768]{1,0:T(8,128)(2,1)} collective-permute-done((bf16[512,768]{1,0:T(8,128)(2,1)}, bf16[512,768]{1,0:T(8,128)(2,1)}, u32[]{:S(2)}, u32[]{:S(2)}) %collective-permute-start.12) | collective-permute-done | bytes 786464 | tf_op jit(solution)/shard_map/ppermute | solution.py:32
  213.1 17.8 %collective-permute-done.13 = s32[512]{0:T(512)S(1)} collective-permute-done((s32[512]{0:T(512)S(1)}, s32[512]{0:T(512)S(1)}, u32[]{:S(2)}, u32[]{:S(2)}) %collective-permute-start.13) | collective-permute-done | bytes 2080 | tf_op jit(solution)/shard_map/ppermute | solution.py:32
  239.2 19.2 %all-to-all-done.4 = bf16[8,128,768]{2,1,0:T(8,128)(2,1)} async-done(((bf16[8,128,768]{2,1,0:T(8,128)(2,1)}), bf16[8,128,768]{2,1,0:T(8,128)(2,1)}, u32[]{:S(2)}, u32[]{:S(2)}) %all-to-all-start.4) | async-done | bytes 1572896 | tf_op jit(solution)/shard_map/all_to_all | solution.py:36
  266.6 10.2 %expert_step.7 = (bf16[8,4,32,768]{3,2,1,0:T(8,128)(2,1)}, bf16[8,4,32,768]{3,2,1,0:T(8,128)(2,1)}, bf16[8,4,32,768]{3,2,1,0:T(8,128)(2,1)}, bf16[8,4,32,768]{3,2,1,0:T(8,128)(2,1)}) custom-call(bf16[8,4,32,768]{3,2,1,0:T(8,128)(2,1)} %bitcast.28.x_ref.refs_3_, bf16[8,4,32,768]{3,2,1,0:T(8,128)(2,1)} %bitcast.129, bf16[4,768,768]{2,1,0:T(8,128)(2,1)} %first_ref.7, ...), custom_call_target="tpu_custom_call" | custom-call | flops 4831838208 | bytes 18874368 | tf_op jit(solution)/shard_map/expert_step/pallas_call | solution.py:521
  276.7 7.1 %all-to-all-done.3 = bf16[8,128,768]{2,1,0:T(8,128)(2,1)} async-done(((bf16[8,128,768]{2,1,0:T(8,128)(2,1)}), bf16[8,128,768]{2,1,0:T(8,128)(2,1)}, u32[]{:S(2)}, u32[]{:S(2)}) %all-to-all-start.3) | async-done | bytes 1572896 | tf_op jit(solution)/shard_map/all_to_all | solution.py:36
  288.1 10.2 %expert_step.5 = (bf16[8,4,32,768]{3,2,1,0:T(8,128)(2,1)}, bf16[8,4,32,768]{3,2,1,0:T(8,128)(2,1)}, bf16[8,4,32,768]{3,2,1,0:T(8,128)(2,1)}, bf16[8,4,32,768]{3,2,1,0:T(8,128)(2,1)}) custom-call(bf16[8,4,32,768]{3,2,1,0:T(8,128)(2,1)} %collective-permute-done.9.x_ref.refs_1_, bf16[8,4,32,768]{3,2,1,0:T(8,128)(2,1)} %bitcast.127, ...), custom_call_target="tpu_custom_call" | custom-call | flops 4831838208 | bytes 18874368 | tf_op jit(solution)/shard_map/expert_step/pallas_call | solution.py:521
  302.0 10.2 %expert_step.6 = (bf16[8,4,32,768]{3,2,1,0:T(8,128)(2,1)}, bf16[8,4,32,768]{3,2,1,0:T(8,128)(2,1)}, bf16[8,4,32,768]{3,2,1,0:T(8,128)(2,1)}, bf16[8,4,32,768]{3,2,1,0:T(8,128)(2,1)}) custom-call(bf16[8,4,32,768]{3,2,1,0:T(8,128)(2,1)} %bitcast.25.x_ref.refs_2_, bf16[8,4,32,768]{3,2,1,0:T(8,128)(2,1)} %bitcast.133, bf16[4,768,768]{2,1,0:T(8,128)(2,1)} %first_ref.7, ...), custom_call_target="tpu_custom_call" | custom-call | flops 4831838208 | bytes 18874368 | tf_op jit(solution)/shard_map/expert_step/pallas_call | solution.py:521
  320.8 10.1 %expert_step.4 = (bf16[8,4,32,768]{3,2,1,0:T(8,128)(2,1)}, bf16[8,4,32,768]{3,2,1,0:T(8,128)(2,1)}, bf16[8,4,32,768]{3,2,1,0:T(8,128)(2,1)}, bf16[8,4,32,768]{3,2,1,0:T(8,128)(2,1)}) custom-call(bf16[8,4,32,768]{3,2,1,0:T(8,128)(2,1)} %bitcast.21.x_ref.refs_0_, bf16[8,4,32,768]{3,2,1,0:T(8,128)(2,1)} %bitcast.131, bf16[4,768,768]{2,1,0:T(8,128)(2,1)} %first_ref.7, ...), custom_call_target="tpu_custom_call" | custom-call | flops 4831838208 | bytes 18874368 | tf_op jit(solution)/shard_map/expert_step/pallas_call | solution.py:521
  347.0 5.8 collective-permute-done.18
  354.7 17.5 %expert_grads.1 = (f32[4,768,768]{2,1,0:T(8,128)}, f32[4,768,768]{2,1,0:T(8,128)}) custom-call(bf16[8,4,32,768]{3,2,1,0:T(8,128)(2,1)} %bitcast.21.x_ref.refs_0_, bf16[8,4,32,768]{3,2,1,0:T(8,128)(2,1)} %collective-permute-done.9.x_ref.refs_1_, bf16[8,4,32,768]{3,2,1,0:T(8,128)(2,1)} %bitcast.25.x_ref.refs_2_, ...), custom_call_target="tpu_custom_call" | custom-call | flops 9663676416 | bytes 18874368 | tf_op jit(solution)/shard_map/expert_grads/pallas_call | solution.py:553
  372.2 29.7 %collective-permute-done.19.far_ref = bf16[512,768]{1,0:T(8,128)(2,1)S(1)} collective-permute-done((bf16[512,768]{1,0:T(8,128)(2,1)S(1)}, bf16[512,768]{1,0:T(8,128)(2,1)S(1)}, u32[]{:S(2)}, u32[]{:S(2)}) %collective-permute-start.19) | collective-permute-done | bytes 786464 | tf_op jit(solution)/shard_map/ppermute | solution.py:32
  402.8 6.5 %turn.1 = (f32[512,768]{1,0:T(8,128)}, bf16[512,768]{1,0:T(8,128)(2,1)}, bf16[768,512]{1,0:T(8,128)(2,1)}, f32[128,768]{1,0:T(8,128)}) custom-call(bf16[1024,768]{1,0:T(8,128)(2,1)} %bitcast.118, bf16[512,768]{1,0:T(8,128)(2,1)} %copy-done.19, s32[512,1]{1,0:T(8,128)} %copy.63.slot_ref, f32[512,768]{1,0:T(8,128)} %get-tuple-element.53.mid_ref, ...), custom_call_target="tpu_custom_call" | custom-call | flops 1409286144 | bytes 4718592 | tf_op jit(solution)/shard_map/turn/pallas_call | solution.py:367
  430.2 50.3 %attend_back.1 = (bf16[192,2048]{1,0:T(8,128)(2,1)}, bf16[384,2048]{1,0:T(8,128)(2,1)}, bf16[1,384,2048]{2,1,0:T(8,128)(2,1)}) custom-call(s32[16]{0:T(128)} %reshape.214.number_ref, s32[4]{0:T(128)} %iota_xor_fusion.order_ref, bf16[4,192,512]{2,1,0:T(8,128)(2,1)} %copy-done.17, f32[192,2048]{1,0:T(8,128)} %get-tuple-element.78.att_t_ref, ...), custom_call_target="tpu_custom_call" | custom-call | flops 48318382080 | bytes 12582912 | tf_op jit(solution)/shard_map/attend_back/pallas_call | solution.py:289
  499.6 6.9 %rows.1 = (bf16[4,512,768]{2,1,0:T(8,128)(2,1)}, bf16[576,2048]{1,0:T(8,128)(2,1)}) custom-call(bf16[192,2048]{1,0:T(8,128)(2,1)} %get-tuple-element.80.gq_ref, bf16[384,2048]{1,0:T(8,128)(2,1)} %get-tuple-element.81.gown_ref, bf16[1,384,2048]{2,1,0:T(8,128)(2,1)} %bitcast.42.got_ref, bf16[576,768]{1,0:T(8,128)(2,1)} %bitcast.116), custom_call_target="tpu_custom_call" | custom-call | flops 1811939328 | bytes 6291456 | tf_op jit(solution)/shard_map/rows/pallas_call | solution.py:409
  506.5 9.1 %weights.1 = bf16[2,4,96,704]{3,2,1,0:T(8,128)(2,1)} custom-call(bf16[576,2048]{1,0:T(8,128)(2,1)} %get-tuple-element.84.cols_ref, bf16[4,512,768]{2,1,0:T(8,128)(2,1)} %get-tuple-element.83.rows_ref, f32[4,768]{1,0:T(4,128)} %bitcast.146, bf16[512,768]{1,0:T(8,128)(2,1)} %bitcast.111, bf16[512,768]{1,0:T(8,128)(2,1)} %copy-done.8, ...), custom_call_target="tpu_custom_call" | custom-call | flops 1811939328 | bytes 6291456 | tf_op jit(solution)/shard_map/weights/pallas_call | solution.py:460
  539.4 5.0 collective-permute-start.25
  554.0 7.6 %collective-permute-done.23 = bf16[512,768]{1,0:T(8,128)(2,1)S(1)} collective-permute-done((bf16[512,768]{1,0:T(8,128)(2,1)}, bf16[512,768]{1,0:T(8,128)(2,1)S(1)}, u32[]{:S(2)}, u32[]{:S(2)}) %collective-permute-start.23) | collective-permute-done | bytes 786464 | tf_op jit(solution)/shard_map/ppermute | solution.py:32
  561.6 16.0 %collective-permute-done.22 = bf16[512,768]{1,0:T(8,128)(2,1)} collective-permute-done((bf16[512,768]{1,0:T(8,128)(2,1)}, bf16[512,768]{1,0:T(8,128)(2,1)}, u32[]{:S(2)}, u32[]{:S(2)}) %collective-permute-start.22) | collective-permute-done | bytes 786464 | tf_op jit(solution)/shard_map/ppermute | solution.py:32
  581.8 8.9 %all-to-all-done.10.part_ref = bf16[8,96,704]{2,1,0:T(8,128)(2,1)S(1)} async-done(((bf16[8,96,704]{2,1,0:T(8,128)(2,1)}), bf16[8,96,704]{2,1,0:T(8,128)(2,1)S(1)}, u32[]{:S(2)}, u32[]{:S(2)}) %all-to-all-start.10) | async-done | bytes 1081376 | tf_op jit(solution)/shard_map/all_to_all | solution.py:36
  (209 shorter events, 207.3 us)
Async XLA Ops:
  7.2 45.7 %collective-permute-start = (bf16[512,768]{1,0:T(8,128)(2,1)}, bf16[512,768]{1,0:T(8,128)(2,1)S(1)}, u32[]{:S(2)}, u32[]{:S(2)}) collective-permute-start(bf16[512,768]{1,0:T(8,128)(2,1)} %bitcast.106), channel_id=1, source_target_pairs={{0,8},{4,12},{8,0},{12,4},{16,24},{20,28},{24,16},{28,20},{1,9},{5... | collective-permute-start | bytes 2359304 | tf_op jit(solution)/shard_map/ppermute | solution.py:32
  10.2 42.7 %collective-permute-start.1 = (bf16[512,768]{1,0:T(8,128)(2,1)}, bf16[512,768]{1,0:T(8,128)(2,1)S(1)}, u32[]{:S(2)}, u32[]{:S(2)}) collective-permute-start(bf16[512,768]{1,0:T(8,128)(2,1)} %bitcast.107), channel_id=1, source_target_pairs={{0,16},{4,20},{8,24},{12,28},{16,0},{20,4},{24,8},{28,12},{1,17},{... | collective-permute-start | bytes 2359304 | tf_op jit(solution)/shard_map/ppermute | solution.py:32
  11.7 41.2 %collective-permute-start.2 = (bf16[512,768]{1,0:T(8,128)(2,1)}, bf16[512,768]{1,0:T(8,128)(2,1)S(1)}, u32[]{:S(2)}, u32[]{:S(2)}) collective-permute-start(bf16[512,768]{1,0:T(8,128)(2,1)} %bitcast.108), channel_id=1, source_target_pairs={{0,24},{4,28},{8,16},{12,20},{16,8},{20,12},{24,0},{28,4},{1,25},{... | collective-permute-start | bytes 2359304 | tf_op jit(solution)/shard_map/ppermute | solution.py:32
  11.8 37.0 %collective-permute-start.8 = (bf16[512,768]{1,0:T(8,128)(2,1)}, bf16[512,768]{1,0:T(8,128)(2,1)}, u32[]{:S(2)}, u32[]{:S(2)}) collective-permute-start(bf16[512,768]{1,0:T(8,128)(2,1)} %bitcast.138), channel_id=1, source_target_pairs={{0,2},{1,3},{2,0},{3,1},{4,6},{5,7},{6,4},{7,5},{8,10},{9,11},{10,... | collective-permute-start | bytes 2359304 | tf_op jit(solution)/shard_map/ppermute | solution.py:32
  18.9 29.8 %collective-permute-start.7 = (s32[512]{0:T(512)S(1)}, s32[512]{0:T(512)S(1)}, u32[]{:S(2)}, u32[]{:S(2)}) collective-permute-start(s32[512]{0:T(512)S(1)} %multiply_add_fusion), channel_id=1, source_target_pairs={{0,2},{1,3},{2,0},{3,1},{4,6},{5,7},{6,4},{7,5},{8,10},{9,11},{10,... | collective-permute-start | bytes 6152 | tf_op jit(solution)/shard_map/ppermute | solution.py:32
  54.3 57.8 %all-to-all-start = ((bf16[8,2,128,768]{3,2,1,0:T(8,128)(2,1)}), bf16[8,2,128,768]{3,2,1,0:T(8,128)(2,1)S(1)}, u32[]{:S(2)}, u32[]{:S(2)}) async-start(bf16[8,2,128,768]{3,2,1,0:T(8,128)(2,1)} %pad_maximum_fusion), calls=%async_computation | async-start | bytes 6291456 | tf_op jit(solution)/shard_map/all_to_all | solution.py:36
  58.1 91.5 %all-gather.2.cloned.1.call-start = ((), (), s32[]{:S(2)}) async-start(), calls=%async_computation.13 | async-start | bytes 1474560 | tf_op jit(solution)/shard_map/all_gather | solution.py:636
  112.1 95.1 %collective-permute-start.10 = (bf16[8,2,128,768]{3,2,1,0:T(8,128)(2,1)S(1)}, bf16[8,2,128,768]{3,2,1,0:T(8,128)(2,1)}, u32[]{:S(2)}, u32[]{:S(2)}) collective-permute-start(bf16[8,2,128,768]{3,2,1,0:T(8,128)(2,1)S(1)} %all-to-all-done), channel_id=1, source_target_pairs={{0,1},{1,0},{2,3},{3,2},{4,5},{5,4},{6,7},{7,6},{8,9},{9,8},{10,11... | collective-permute-start | bytes 9437192 | tf_op jit(solution)/shard_map/ppermute | solution.py:32
  166.9 38.1 %collective-permute-start.12 = (bf16[512,768]{1,0:T(8,128)(2,1)}, bf16[512,768]{1,0:T(8,128)(2,1)}, u32[]{:S(2)}, u32[]{:S(2)}) collective-permute-start(bf16[512,768]{1,0:T(8,128)(2,1)} %get-tuple-element.57), channel_id=1, source_target_pairs={{0,2},{1,3},{2,0},{3,1},{4,6},{5,7},{6,4},{7,5},{8,10},{9,11},{10,... | collective-permute-start | bytes 2359304 | tf_op jit(solution)/shard_map/ppermute | solution.py:32
  168.8 64.3 %all-to-all-start.2 = ((bf16[8,128,768]{2,1,0:T(8,128)(2,1)}), bf16[8,128,768]{2,1,0:T(8,128)(2,1)}, u32[]{:S(2)}, u32[]{:S(2)}) async-start(bf16[8,128,768]{2,1,0:T(8,128)(2,1)} %bitcast.124), calls=%async_computation.2 | async-start | bytes 3145728 | tf_op jit(solution)/shard_map/all_to_all | solution.py:36
  237.4 50.7 %collective-permute-start.9 = (bf16[8,4,32,768]{3,2,1,0:T(8,128)(2,1)}, bf16[8,4,32,768]{3,2,1,0:T(8,128)(2,1)}, u32[]{:S(2)}, u32[]{:S(2)}) collective-permute-start(bf16[8,4,32,768]{3,2,1,0:T(8,128)(2,1)} %bitcast.21.x_ref.refs_0_), channel_id=1, source_target_pairs={{0,1},{1,0},{2,3},{3,2},{4,5},{5,4},{6,7},{7,6},{8,9},{9,8},{10,11... | collective-permute-start | bytes 4718600 | tf_op jit(solution)/shard_map/ppermute | solution.py:32
  298.4 37.5 %collective-permute-start.17 = (bf16[8,4,32,768]{3,2,1,0:T(8,128)(2,1)}, bf16[8,4,32,768]{3,2,1,0:T(8,128)(2,1)}, u32[]{:S(2)}, u32[]{:S(2)}) collective-permute-start(bf16[8,4,32,768]{3,2,1,0:T(8,128)(2,1)} %get-tuple-element.63), channel_id=1, source_target_pairs={{0,1},{1,0},{2,3},{3,2},{4,5},{5,4},{6,7},{7,6},{8,9},{9,8},{10,11... | collective-permute-start | bytes 4718600 | tf_op jit(solution)/shard_map/ppermute | solution.py:32
  312.2 29.0 %all-to-all-start.7 = ((bf16[8,128,768]{2,1,0:T(8,128)(2,1)}), bf16[8,128,768]{2,1,0:T(8,128)(2,1)S(1)}, u32[]{:S(2)}, u32[]{:S(2)}) async-start(bf16[8,128,768]{2,1,0:T(8,128)(2,1)} %bitcast.123), calls=%async_computation.7 | async-start | bytes 3145728 | tf_op jit(solution)/shard_map/all_to_all | solution.py:36
  320.5 32.2 %collective-permute-start.18 = (bf16[512,768]{1,0:T(8,128)(2,1)}, bf16[512,768]{1,0:T(8,128)(2,1)}, u32[]{:S(2)}, u32[]{:S(2)}) collective-permute-start(bf16[512,768]{1,0:T(8,128)(2,1)} %fusion.24), channel_id=1, source_target_pairs={{0,1},{1,0},{2,3},{3,2},{4,5},{5,4},{6,7},{7,6},{8,9},{9,8},{10,11... | collective-permute-start | bytes 2359304 | tf_op jit(solution)/shard_map/ppermute | solution.py:32
  339.5 75.1 %collective-permute-start.15 = (bf16[8,4,32,768]{3,2,1,0:T(8,128)(2,1)}, bf16[8,4,32,768]{3,2,1,0:T(8,128)(2,1)}, u32[]{:S(2)}, u32[]{:S(2)}) collective-permute-start(bf16[8,4,32,768]{3,2,1,0:T(8,128)(2,1)} %get-tuple-element.61), channel_id=1, source_target_pairs={{0,1},{1,0},{2,3},{3,2},{4,5},{5,4},{6,7},{7,6},{8,9},{9,8},{10,11... | collective-permute-start | bytes 4718600 | tf_op jit(solution)/shard_map/ppermute | solution.py:32
  341.3 31.0 %all-to-all-start.6 = ((bf16[8,128,768]{2,1,0:T(8,128)(2,1)}), bf16[8,128,768]{2,1,0:T(8,128)(2,1)S(1)}, u32[]{:S(2)}, u32[]{:S(2)}) async-start(bf16[8,128,768]{2,1,0:T(8,128)(2,1)} %bitcast.33), calls=%async_computation.6 | async-start | bytes 3145728 | tf_op jit(solution)/shard_map/all_to_all | solution.py:36
  354.1 47.8 %collective-permute-start.19 = (bf16[512,768]{1,0:T(8,128)(2,1)S(1)}, bf16[512,768]{1,0:T(8,128)(2,1)S(1)}, u32[]{:S(2)}, u32[]{:S(2)}) collective-permute-start(bf16[512,768]{1,0:T(8,128)(2,1)S(1)} %add_convert_fusion.3), channel_id=1, source_target_pairs={{0,2},{1,3},{2,0},{3,1},{4,6},{5,7},{6,4},{7,5},{8,10},{9,11},{10,... | collective-permute-start | bytes 2359304 | tf_op jit(solution)/shard_map/ppermute | solution.py:32
  413.3 72.1 %collective-permute-start.11 = (bf16[8,4,32,768]{3,2,1,0:T(8,128)(2,1)}, bf16[8,4,32,768]{3,2,1,0:T(8,128)(2,1)}, u32[]{:S(2)}, u32[]{:S(2)}) collective-permute-start(bf16[8,4,32,768]{3,2,1,0:T(8,128)(2,1)} %get-tuple-element.56), channel_id=1, source_target_pairs={{0,1},{1,0},{2,3},{3,2},{4,5},{5,4},{6,7},{7,6},{8,9},{9,8},{10,11... | collective-permute-start | bytes 4718600 | tf_op jit(solution)/shard_map/ppermute | solution.py:32
  417.7 73.1 %collective-permute-start.16 = (bf16[8,4,32,768]{3,2,1,0:T(8,128)(2,1)}, bf16[8,4,32,768]{3,2,1,0:T(8,128)(2,1)}, u32[]{:S(2)}, u32[]{:S(2)}) collective-permute-start(bf16[8,4,32,768]{3,2,1,0:T(8,128)(2,1)} %add_convert_fusion.2), channel_id=1, source_target_pairs={{0,2},{1,3},{2,0},{3,1},{4,6},{5,7},{6,4},{7,5},{8,10},{9,11},{10,... | collective-permute-start | bytes 4718600 | tf_op jit(solution)/shard_map/ppermute | solution.py:32
  425.7 55.9 %all-to-all-start.11 = ((bf16[8,4,24,896]{3,2,1,0:T(8,128)(2,1)}), bf16[8,4,24,896]{3,2,1,0:T(8,128)(2,1)S(1)}, u32[]{:S(2)}, u32[]{:S(2)}) async-start(bf16[8,4,24,896]{3,2,1,0:T(8,128)(2,1)} %bitcast.104), calls=%async_computation.11 | async-start | bytes 2752512 | tf_op jit(solution)/shard_map/all_to_all | solution.py:36
  525.5 36.1 %collective-permute-start.23 = (bf16[512,768]{1,0:T(8,128)(2,1)}, bf16[512,768]{1,0:T(8,128)(2,1)S(1)}, u32[]{:S(2)}, u32[]{:S(2)}) collective-permute-start(bf16[512,768]{1,0:T(8,128)(2,1)} %get-tuple-element.100), channel_id=1, source_target_pairs={{0,24},{4,28},{8,16},{12,20},{16,8},{20,12},{24,0},{28,4},{1,25},{... | collective-permute-start | bytes 2359304 | tf_op jit(solution)/shard_map/ppermute | solution.py:32
  528.3 49.2 %collective-permute-start.22 = (bf16[512,768]{1,0:T(8,128)(2,1)}, bf16[512,768]{1,0:T(8,128)(2,1)}, u32[]{:S(2)}, u32[]{:S(2)}) collective-permute-start(bf16[512,768]{1,0:T(8,128)(2,1)} %get-tuple-element.101), channel_id=1, source_target_pairs={{0,16},{4,20},{8,24},{12,28},{16,0},{20,4},{24,8},{28,12},{1,17},{... | collective-permute-start | bytes 2359304 | tf_op jit(solution)/shard_map/ppermute | solution.py:32
  528.9 48.7 %collective-permute-start.21 = (bf16[512,768]{1,0:T(8,128)(2,1)}, bf16[512,768]{1,0:T(8,128)(2,1)}, u32[]{:S(2)}, u32[]{:S(2)}) collective-permute-start(bf16[512,768]{1,0:T(8,128)(2,1)} %get-tuple-element.99), channel_id=1, source_target_pairs={{0,8},{4,12},{8,0},{12,4},{16,24},{20,28},{24,16},{28,20},{1,9},{5... | collective-permute-start | bytes 2359304 | tf_op jit(solution)/shard_map/ppermute | solution.py:32
  550.4 40.3 %all-to-all-start.10 = ((bf16[8,96,704]{2,1,0:T(8,128)(2,1)}), bf16[8,96,704]{2,1,0:T(8,128)(2,1)S(1)}, u32[]{:S(2)}, u32[]{:S(2)}) async-start(bf16[8,96,704]{2,1,0:T(8,128)(2,1)} %broadcast_in_dim.10), calls=%async_computation.10 | async-start | bytes 2359296 | tf_op jit(solution)/shard_map/all_to_all | solution.py:36
  (48 other events, 595.5 us)
Sparse Core Ops, SparseCore 0:
  93.1 35.4 all-gather.1

commit v4 on v3

--- a/solution.py
+++ b/solution.py
@@ -13,6 +13,7 @@
 BLK = 256
 TOK_DEV = 512
 CHUNK = 4
+COST = 1000
 epsilon = 1e-05
 masked_value = -1e30
 bf16 = jnp.bfloat16
@@ -32,11 +33,11 @@
     return lax.ppermute(value, axis, [(i, i ^ offset) for i in range(size)])
 
 
-def trade(parts, axis, groups=None):
+def plain_trade(parts, axis, groups=None):
     return lax.all_to_all(parts, axis, 0, 0, tiled=True, axis_index_groups=groups)
 
 
-def share(part, count, axis, groups=None):
+def share(part, count, axis, groups, trade):
     return trade(jnp.broadcast_to(part[None], (count,) + part.shape), axis, groups)
 
 
@@ -74,28 +75,35 @@
 
 
 def cost(flops, moved, exps=0):
-    return pl.CostEstimate(flops=int(flops), bytes_accessed=int(moved), transcendentals=int(exps))
-
-
-def project_kernel(hidden_ref, wt_ref, vec_ref, out_ref):
-    normal, _ = norm_stats(hidden_ref[...].astype(f32))
-    normed = (normal * vec_ref[0:1] + vec_ref[1:2]).astype(bf16)
-    got = dot(wt_ref[...], normed, NT).astype(bf16)
-    span = got.shape[0] // 3
-    out_ref[:span, :] = (got[:span].astype(f32) * HD ** (-0.5)).astype(bf16)
-    out_ref[span:, :] = got[span:]
+    return pl.CostEstimate(flops=int(flops) // COST, bytes_accessed=int(moved) // COST, transcendentals=int(exps) // COST)
+
+
+def project_kernel(pieces, *refs):
+    wt_ref, vec_ref, q_ref, kv_ref = refs[pieces:]
+    span, rows = q_ref.shape[0], refs[0].shape[0]
+    for p, ref in enumerate(refs[:pieces]):
+        normal, _ = norm_stats(ref[...].astype(f32))
+        normed = (normal * vec_ref[0:1] + vec_ref[1:2]).astype(bf16)
+        got = dot(wt_ref[...], normed, NT).astype(bf16)
+        cut = slice(p * rows, (p + 1) * rows)
+        q_ref[:, cut] = (got[:span].astype(f32) * HD ** (-0.5)).astype(bf16)
+        kv_ref[:, cut] = got[span:]
 
 
 def project(hidden, wt, vecs):
-    rows, width = hidden.shape
-    wide = wt.shape[0]
-    return pl.pallas_call(
-        project_kernel,
-        out_shape=jax.ShapeDtypeStruct((wide, rows), bf16),
-        compiler_params=PARAMS,
-        cost_estimate=cost(2 * rows * width * wide, 4 * rows * width),
+    rows, width = hidden[0].shape
+    span = wt.shape[0] // 3
+    total = len(hidden) * rows
+    return pl.pallas_call(
+        partial(project_kernel, len(hidden)),
+        out_shape=[
+            jax.ShapeDtypeStruct((span, total), bf16),
+            jax.ShapeDtypeStruct((2 * span, total), bf16),
+        ],
+        compiler_params=PARAMS,
+        cost_estimate=cost(6 * total * width * span, 4 * total * width),
         name="project",
-    )(hidden, wt, vecs)
+    )(*hidden, wt, vecs)
 
 
 def only_head(block, head):
@@ -106,35 +114,40 @@
     )
 
 
-def key_blocks(number_ref, own_refs, far_refs):
-    span = own_refs[0].shape[0] // 3
-    per = own_refs[0].shape[1] // BLK
-    for p, ref in enumerate(own_refs + far_refs):
-        for i in range(per):
-            at = pl.multiple_of(number_ref[p * per + i] * BLK, BLK)
-            cut = slice(i * BLK, (i + 1) * BLK)
-            yield at, (ref[span:, cut] if p < len(own_refs) else ref[:, cut])
-
-
-def attend_kernel(pieces, sides, number_ref, order_ref, *refs):
-    own_refs, far_refs = refs[:pieces], refs[pieces : pieces * sides]
-    att_ref, att_t_ref, lse_ref, acc_ref, q_all, k_sorted, v_sorted = refs[pieces * sides :]
+def key_blocks(number_ref, kv_refs, high=1):
+    place = 0
+    for ref in kv_refs:
+        for i in range(ref.shape[1] // BLK):
+            if high or i % 2 == 0:
+                at = pl.multiple_of(number_ref[place] * BLK, BLK)
+                yield at, ref[:, i * BLK : (i + 1) * BLK]
+            place += 1
+
+
+def take_queries(q_refs, q_all):
+    at = 0
+    for ref in q_refs:
+        q_all[:, at : at + ref.shape[1]] = ref[...]
+        at += ref.shape[1]
+
+
+def attend_kernel(high, parts, all_parts, number_ref, order_ref, *refs):
+    q_refs, kv_refs = refs[:parts], refs[parts:all_parts]
+    att_ref, att_t_ref, lse_ref, acc_ref, q_all, k_sorted, v_sorted = refs[-7:]
     turn = pl.program_id(0)
     span = acc_ref.shape[0]
     heads = span // HD
-    block = number_ref[turn]
+    block = number_ref[2 * turn + high]
     size = CHUNK * BLK
 
     @pl.when(turn == 0)
     def _():
-        for p, ref in enumerate(own_refs):
-            rows = ref.shape[1]
-            q_all[:, p * rows : (p + 1) * rows] = ref[:span, :]
-        for at, kv in key_blocks(number_ref, own_refs, far_refs):
+        take_queries(q_refs, q_all)
+        for at, kv in key_blocks(number_ref, kv_refs, high):
             k_sorted[pl.ds(at, BLK), :] = jnp.transpose(kv[:span])
             v_sorted[:, pl.ds(at, BLK)] = kv[span:]
 
-    own_queries = q_all[:, pl.ds(pl.multiple_of(turn * BLK, BLK), BLK)]
+    own_queries = q_all[:, pl.ds(pl.multiple_of((2 * turn + high) * BLK, BLK), BLK)]
     queries = [only_head(own_queries, h) for h in range(heads)]
     acc_ref[...] = jnp.zeros_like(acc_ref)
 
@@ -174,28 +187,30 @@
         lse_ref[0, h : h + 1, :] = top[h] + jnp.log(total[h])
 
 
-def attend(numbers, order, own, far):
-    pieces, sides = len(own), 1 + len(far) // len(own)
-    span, piece = own[0].shape[0] // 3, own[0].shape[1]
-    rows = pieces * piece
-    blocks = rows // BLK
-    keys = rows * sides
-    return pl.pallas_call(
-        partial(attend_kernel, pieces, sides),
+def attend(numbers, order, queries, kvs, before):
+    high = 0 if before is None else 1
+    before = () if before is None else tuple(before)
+    pieces, span = order.shape[0], queries[0].shape[0]
+    rows, keys = sum(q.shape[1] for q in queries), sum(kv.shape[1] for kv in kvs)
+    piece, blocks = rows // pieces, rows // BLK
+    sorted_keys = keys if high else keys // 2
+    return pl.pallas_call(
+        partial(attend_kernel, high, len(queries), len(queries + kvs)),
         grid_spec=pltpu.PrefetchScalarGridSpec(
             num_scalar_prefetch=2,
-            grid=(blocks,),
-            in_specs=[whole(a.shape) for a in own + far],
+            grid=(blocks // 2,),
+            in_specs=[whole(a.shape) for a in queries + kvs]
+            + [pl.BlockSpec(memory_space=pl.ANY)] * len(before),
             out_specs=[
-                pl.BlockSpec((1, span, BLK), lambda i, n, o: (o[i // 2], 0, i % 2)),
-                pl.BlockSpec((span, BLK), lambda i, *_: (0, i)),
-                pl.BlockSpec((1, 8, BLK), lambda i, *_: (i, 0, 0)),
+                pl.BlockSpec((1, span, BLK), lambda i, n, o: (o[i], 0, high)),
+                pl.BlockSpec((span, BLK), lambda i, *_: (0, 2 * i + high)),
+                pl.BlockSpec((1, 8, BLK), lambda i, *_: (2 * i + high, 0, 0)),
             ],
             scratch_shapes=[
                 pltpu.VMEM((span, BLK), f32),
                 pltpu.VMEM((span, rows), bf16),
-                pltpu.VMEM((keys, span), bf16),
-                pltpu.VMEM((span, keys), bf16),
+                pltpu.VMEM((sorted_keys, span), bf16),
+                pltpu.VMEM((span, sorted_keys), bf16),
             ],
         ),
         out_shape=[
@@ -205,14 +220,16 @@
         ],
         compiler_params=PARAMS,
         cost_estimate=cost(12 * rows * keys * span, 8 * keys * span, rows * keys * span // 128),
-        name="attend",
-    )(numbers, order, *own, *far)
-
-
-def attend_back_kernel(pieces, sides, number_ref, order_ref, g_ref, att_t_ref, lse_ref, *refs):
-    own_refs, far_refs = refs[:pieces], refs[pieces : pieces * sides]
-    gq_ref, gown_ref, gfar_ref = refs[pieces * sides : pieces * sides + 3]
-    gq_acc, gk_acc, gv_acc, q_all, k_sorted, v_sorted, kt_sorted = refs[pieces * sides + 3 :]
+        input_output_aliases={2 + len(queries + kvs) + i: i for i in range(len(before))},
+        name="attend_high" if high else "attend_low",
+    )(numbers, order, *queries, *kvs, *before)
+
+
+def attend_back_kernel(parts, all_parts, number_ref, order_ref, g_ref, att_t_ref, lse_ref, *refs):
+    q_refs, kv_refs = refs[:parts], refs[parts:all_parts]
+    gq_ref, gown_ref, gfar_ref = refs[all_parts : all_parts + 3]
+    gq_acc, gk_acc, gv_acc, q_all, k_sorted, v_sorted, kt_sorted = refs[all_parts + 3 :]
+    sides = 1 + gfar_ref.shape[0]
     turn = pl.program_id(0)
     span = gq_acc.shape[0]
     heads = span // HD
@@ -223,10 +240,8 @@
     def _():
         gk_acc[...] = jnp.zeros_like(gk_acc)
         gv_acc[...] = jnp.zeros_like(gv_acc)
-        for p, ref in enumerate(own_refs):
-            rows = ref.shape[1]
-            q_all[:, p * rows : (p + 1) * rows] = ref[:span, :]
-        for at, kv in key_blocks(number_ref, own_refs, far_refs):
+        take_queries(q_refs, q_all)
+        for at, kv in key_blocks(number_ref, kv_refs):
             k_sorted[pl.ds(at, BLK), :] = jnp.transpose(kv[:span])
             v_sorted[pl.ds(at, BLK), :] = jnp.transpose(kv[span:])
             kt_sorted[:, pl.ds(at, BLK)] = kv[:span]
@@ -279,15 +294,13 @@
                     gfar_ref[s - 1, :span, cut], gfar_ref[s - 1, span:, cut] = gk, gv
 
 
-def attend_back(numbers, order, own, far, grads, att_t, logs):
-    pieces, sides = len(own), 1 + len(far) // len(own)
-    span, piece = own[0].shape[0] // 3, own[0].shape[1]
-    rows = pieces * piece
-    blocks = rows // BLK
-    keys = rows * sides
+def attend_back(numbers, order, queries, kvs, grads, att_t, logs):
+    span = queries[0].shape[0]
+    rows, keys = sum(q.shape[1] for q in queries), sum(kv.shape[1] for kv in kvs)
+    sides, blocks = keys // rows, rows // BLK
     column = pl.BlockSpec((span, BLK), lambda i, *_: (0, i))
     return pl.pallas_call(
-        partial(attend_back_kernel, pieces, sides),
+        partial(attend_back_kernel, len(queries), len(queries + kvs)),
         grid_spec=pltpu.PrefetchScalarGridSpec(
             num_scalar_prefetch=2,
             grid=(blocks,),
@@ -296,7 +309,7 @@
                 column,
                 pl.BlockSpec((1, 8, BLK), lambda i, *_: (i, 0, 0)),
             ]
-            + [whole(a.shape) for a in own + far],
+            + [whole(a.shape) for a in queries + kvs],
             out_specs=[column, whole((2 * span, rows)), whole((sides - 1, 2 * span, rows))],
             scratch_shapes=[
                 pltpu.VMEM((span, BLK), f32),
@@ -316,7 +329,7 @@
         compiler_params=PARAMS,
         cost_estimate=cost(30 * rows * keys * span, 16 * keys * span, rows * keys * span // 128),
         name="attend_back",
-    )(numbers, order, grads, att_t, logs, *own, *far)
+    )(numbers, order, grads, att_t, logs, *queries, *kvs)
 
 
 def middle_kernel(att_ref, x_ref, w_ref, vec_ref, slot_ref, mid_ref, normed_ref, send_ref):
@@ -378,66 +391,67 @@
     )(got, far, slot[:, None], middle, cot, weight, vecs)
 
 
-def out_grad_kernel(att_ref, gbr_ref, sum_ref, out_ref):
-    width = gbr_ref.shape[1]
-    out_ref[:, :width] = dot(att_ref[...], gbr_ref[...]).astype(bf16)
-    out_ref[:, width:] = jnp.transpose(sum_ref[...]).astype(bf16)
-
-
-def out_grad_step(att_t, gbr, sums):
-    return pl.pallas_call(
-        out_grad_kernel,
-        out_shape=jax.ShapeDtypeStruct((att_t.shape[0], gbr.shape[1] + 128), bf16),
+def out_grad_kernel(planes, att_ref, gbr_ref, sum_ref, out_ref):
+    count = out_ref.shape[0]
+    weights = dot(att_ref[...], gbr_ref[...])
+    step = weights.shape[0] // (planes * count)
+    for c in range(count):
+        at = [(z * count + c) * step for z in range(planes)]
+        pieces = [weights[a : a + step] for a in at] + [sum_ref[:16]]
+        out_ref[c] = jnp.concatenate(pieces, axis=0).astype(bf16)
+
+
+def out_grad_step(att_t, gbr, sums, planes, devices):
+    rows = att_t.shape[0] // devices + 16
+    return pl.pallas_call(
+        partial(out_grad_kernel, planes),
+        out_shape=jax.ShapeDtypeStruct((devices, rows, gbr.shape[1]), bf16),
         compiler_params=PARAMS,
         cost_estimate=cost(2 * att_t.size * gbr.shape[1], 6 * gbr.size),
         name="out_grad",
     )(att_t, gbr, sums)
 
 
-def rows_kernel(gq_ref, gown_ref, got_ref, wt_ref, rows_ref, cols_ref):
-    gkv = gown_ref[...].astype(f32)
-    for k in range(got_ref.shape[0]):
-        gkv = gkv + got_ref[k].astype(f32)
-    columns = jnp.concatenate([gq_ref[...], gkv.astype(bf16)], axis=0)
-    cols_ref[...] = columns
-    rows_ref[0] = dot(columns, wt_ref[...], TN).astype(bf16)
-
-
-def rows_step(gq, gown, got, wt, rows):
+def rows_kernel(order_ref, gq_ref, gown_ref, got_ref, wt_ref, cols_ref, out_ref):
+    rows = out_ref.shape[1]
+    for j in range(out_ref.shape[0]):
+        cut = slice(j * rows, (j + 1) * rows)
+        gkv = gown_ref[:, cut].astype(f32)
+        for k in range(got_ref.shape[0]):
+            gkv = gkv + got_ref[k, :, cut].astype(f32)
+        columns = jnp.concatenate([gq_ref[:, cut], gkv.astype(bf16)], axis=0)
+        cols_ref[:, cut] = columns
+        out_ref[order_ref[j]] = dot(columns, wt_ref[...], TN).astype(bf16)
+
+
+SCALARS = pl.BlockSpec(memory_space=pltpu.SMEM)
+ARRAY = pl.BlockSpec(memory_space=pltpu.VMEM)
+
+
+def rows_step(order, gq, gown, got, wt, rows):
     sources = gq.shape[1] // rows
     wide, width = wt.shape
     return pl.pallas_call(
         rows_kernel,
-        grid=(sources,),
-        in_specs=[
-            pl.BlockSpec((gq.shape[0], rows), lambda i: (0, i)),
-            pl.BlockSpec((gown.shape[0], rows), lambda i: (0, i)),
-            pl.BlockSpec((got.shape[0], gown.shape[0], rows), lambda i: (0, 0, i)),
-            whole(wt.shape),
-        ],
-        out_specs=[
-            pl.BlockSpec((1, rows, width), lambda i: (i, 0, 0)),
-            pl.BlockSpec((wide, rows), lambda i: (0, i)),
-        ],
+        in_specs=[SCALARS] + [ARRAY] * 4,
         out_shape=[
+            jax.ShapeDtypeStruct((wide, sources * rows), bf16),
             jax.ShapeDtypeStruct((sources, rows, width), bf16),
-            jax.ShapeDtypeStruct((wide, sources * rows), bf16),
         ],
         compiler_params=PARAMS,
         cost_estimate=cost(2 * sources * rows * width * wide, 4 * sources * rows * width),
         name="rows",
-    )(gq, gown, got, wt)
-
-
-def weights_kernel(cols_ref, rows_ref, vec_ref, *refs):
-    sources = rows_ref.shape[0]
-    hidden_refs, mixed_ref = refs[:sources], refs[sources]
+    )(order, gq, gown, got, wt)
+
+
+def weights_kernel(order_ref, cols_ref, vec_ref, rows_ref, *refs):
+    hidden_refs, mixed_ref = refs[:-1], refs[-1]
     piece = rows_ref.shape[1]
     total, gains, biases = None, 0.0, 0.0
     for j, ref in enumerate(hidden_refs):
         normal, _ = norm_stats(ref[...].astype(f32))
         normed = (normal * vec_ref[0:1] + vec_ref[1:2]).astype(bf16)
-        rows = rows_ref[j].astype(f32)
+        rows = rows_ref[order_ref[j]].astype(f32)
         gains += jnp.sum(rows * normal, axis=0, keepdims=True)
         biases += jnp.sum(rows, axis=0, keepdims=True)
         part = dot(cols_ref[:, j * piece : (j + 1) * piece], normed)
@@ -451,41 +465,44 @@
         for s in range(cores):
             at = (z * cores + s) * count
             mixed_ref[s, z, :, :wide] = weights[at : at + count]
-            mixed_ref[s, z, :, wide:] = sums[at : at + count]
-
-
-def weights_step(cols, rows, vecs, hidden, cores, planes):
+            mixed_ref[s, z, :, wide : wide + 128] = sums[at : at + count]
+            rest = mixed_ref.shape[3] - wide - 128
+            mixed_ref[s, z, :, wide + 128 :] = jnp.zeros((count, rest), bf16)
+
+
+def weights_step(order, cols, rows, vecs, hidden, cores, planes):
     wide, width = cols.shape[0], rows.shape[2]
-    shape = (cores, planes, width // (cores * planes), wide + 128)
+    shape = (cores, planes, width // (cores * planes), width)
     return pl.pallas_call(
         weights_kernel,
+        in_specs=[SCALARS] + [ARRAY] * (3 + len(hidden)),
         out_shape=jax.ShapeDtypeStruct(shape, bf16),
         compiler_params=PARAMS,
-        cost_estimate=cost(2 * cols.size * width, 4 * rows.size),
+        cost_estimate=cost(2 * cols.size * width, 4 * cols.size),
         name="weights",
-    )(cols, rows, vecs, *hidden)
+    )(order, cols, vecs, rows, *hidden)
 
 
 def assemble_kernel(span, groups, part_ref, out_ref, sum_ref):
-    count, rows, _ = part_ref.shape
+    count, rows = part_ref.shape[0], out_ref.shape[0] // (part_ref.shape[0] // groups)
     cores = count // groups
     for s in range(cores):
         at = slice(s * rows, (s + 1) * rows)
-        pieces = [part_ref[g * cores + s].astype(f32) for g in range(groups)]
+        pieces = [part_ref[g * cores + s, :rows].astype(f32) for g in range(groups)]
         out_ref[at, :] = jnp.concatenate(
             [p[:, t * span : (t + 1) * span] for t in range(3) for p in pieces], axis=1
         )
-        sum_ref[at, :] = sum(p[:, 3 * span :] for p in pieces)
-
-
-def assemble(part, span, groups):
-    count, rows, wide = part.shape
+        sum_ref[at, :] = sum(p[:, 3 * span : 3 * span + 128] for p in pieces)
+
+
+def assemble(part, rows, span, groups):
+    count = part.shape[0]
     total = rows * (count // groups)
     return pl.pallas_call(
         partial(assemble_kernel, span, groups),
         out_shape=[
             jax.ShapeDtypeStruct((total, 3 * span * groups), f32),
-            jax.ShapeDtypeStruct((total, wide - 3 * span), f32),
+            jax.ShapeDtypeStruct((total, 128), f32),
         ],
         compiler_params=PARAMS,
         cost_estimate=cost(part.size, 6 * part.size),
@@ -525,11 +542,7 @@
         out_specs=[hidden_spec, hidden_spec, token_spec, token_spec],
         out_shape=[like(hidden), like(hidden), like(width), like(width)],
         compiler_params=PARAMS,
-        cost_estimate=pl.CostEstimate(
-            flops=8 * sources * experts * room * width * hidden,
-            bytes_accessed=4 * first.size + 12 * tokens.size,
-            transcendentals=sources * experts * room * hidden,
-        ),
+        cost_estimate=cost(8 * sources * experts * room * width * hidden, 4 * first.size + 12 * tokens.size, sources * experts * room * hidden),
         name="expert_step",
     )(tokens, grads, first, second)
 
@@ -557,11 +570,7 @@
         out_specs=[out_spec, out_spec],
         out_shape=[out, out],
         compiler_params=PARAMS,
-        cost_estimate=pl.CostEstimate(
-            flops=4 * parts * sources * experts * room * width * hidden,
-            bytes_accessed=8 * experts * width * hidden,
-            transcendentals=0,
-        ),
+        cost_estimate=cost(4 * parts * sources * experts * room * width * hidden, 8 * experts * width * hidden, 0),
         name="expert_grads",
     )(*tokens, *grads, *acts, *gpres)
 
@@ -587,110 +596,135 @@
 
     own_hidden = hidden_in[0]
     out_cot = out_grad[0]
+    evens = range(2, planes, 2)
+    packed = (devices, local_experts * room, width)
+    shaped = (devices, local_experts, room, width)
+    latest = []
+
+    def trade(parts, *args):
+        got = plain_trade(after(parts, *latest), *args)
+        latest[:] = [got]
+        return got
+
+    exchange = lambda rows: trade(rows.reshape(packed), "ctx").reshape(shaped)
 
     expert_of = hash_table[token_ids[0]]
     same = expert_of[:, None] == expert_of[None, :]
     shape = (TOK_DEV, TOK_DEV)
     before = lax.broadcasted_iota(jnp.int32, shape, 1) < lax.broadcasted_iota(jnp.int32, shape, 0)
     slot = expert_of * room + jnp.sum((same & before).astype(jnp.int32), axis=1)
-
-    def spread(value):
-        far = [None, None]
-        for k in range(2, planes):
-            far.append(swap(far[k - 1], "fsdp", 1) if k % 2 else swap(value, "fsdp", k))
-        return far
-
     counter = lambda axis: lax.broadcasted_iota(
         jnp.int32, (all_slots, TOK_DEV) if axis == 0 else (TOK_DEV, all_slots), axis
     )
     place = lambda s, rows: dot((counter(0) == s[None, :]).astype(bf16), rows).astype(bf16)
-    fetch = lambda s, rows: dot((counter(1) == s[:, None]).astype(bf16), rows)
-    packed = (devices, local_experts * room, width)
-    shaped = (devices, local_experts, room, width)
-    exchange = lambda rows: trade(rows.reshape(packed), "ctx").reshape(shaped)
-    evens = range(2, planes, 2)
+    fetch = lambda s, rows: dot(
+        (counter(1) == s[:, None]).astype(bf16), rows.reshape(all_slots, width)
+    )
+    sent = place(slot, out_cot)
 
     cut = lambda part: lax.dynamic_slice_in_dim(qkv_weight, part * width + group * span, span, 1)
     vecs = jnp.stack([norm1_gain, norm1_bias, norm2_gain, norm2_bias], axis=1)
+    lines = width // planes
+    codes = jnp.stack([slot // room, slot % room]).astype(bf16).reshape(-1)
+    across_lines = -(-codes.shape[0] // lines)
+    codes = jnp.pad(codes, (0, across_lines * lines - codes.shape[0])).reshape(lines, across_lines)
     own_cols = jnp.concatenate(
-        [cut(0), cut(1), cut(2), jnp.pad(vecs, ((0, 0), (0, 60)))], axis=1
+        [cut(0), cut(1), cut(2), vecs, jnp.pad(codes, ((0, 0), (0, 60 - codes.shape[1])))], axis=1
     )
     full = lax.all_gather(own_cols, "fsdp", axis=0, tiled=True)
     wt, vecs = full[:, : 3 * span].T, full[:, 3 * span : 3 * span + 4].T.astype(f32)
+    codes = full[:, 3 * span + 4 : 3 * span + 4 + across_lines].reshape(planes, -1)
+    codes = codes[:, : 2 * TOK_DEV].astype(jnp.int32)
+    all_slot = codes[:, :TOK_DEV] * room + codes[:, TOK_DEV:]
+    far_slots = {
+        k: lax.dynamic_index_in_dim(all_slot, plane ^ k, 0, False) for k in range(1, planes)
+    }
     hidden = [own_hidden] + [swap(own_hidden, "ctx", j * cores) for j in range(1, groups)]
-    far_cots = {k: swap(out_cot, "fsdp", k) for k in evens}
-    far_slots = spread(slot)
-
-    near_first = [place(slot, out_cot)] + [place(far_slots[k], far_cots[k]) for k in evens]
-    sides = len(near_first)
-    stacked = after(jnp.stack([p.reshape(packed) for p in near_first], axis=1), *hidden)
-    got_near = trade(stacked, "ctx")
-    got_far = swap(got_near, "fsdp", 1)
+    far_cots = {k: swap(after(out_cot, full), "fsdp", k) for k in evens}
+
     gys = [None] * planes
-    for i, k in enumerate([0, *evens]):
-        gys[k] = got_near[:, i].reshape(shaped)
-        gys[k + 1] = got_far[:, i].reshape(shaped)
-
-    own = [project(h, wt, vecs) for h in hidden]
-    far = [swap(o[span:], "ctx", k) for k in range(1, cores) for o in own]
-    out_full = lax.all_gather(out_weight, "fsdp", axis=0, tiled=True)
+    gys[0] = exchange(after(sent, *hidden))
+    queries, kvs = zip(project(hidden[:1], wt, vecs), project(hidden[1:], wt, vecs))
+    kvs = kvs + tuple(swap(kv, "ctx", k) for k in range(1, cores) for kv in kvs)
     table = deal_order.reshape(groups, cores)
     order = group ^ jnp.arange(groups, dtype=jnp.int32)
     low = jnp.stack(
         [lax.dynamic_index_in_dim(table, core ^ s, 1, False)[order] for s in range(cores)]
     )
     numbers = jnp.stack([low, 2 * devices - 1 - low], axis=2).reshape(-1)
-    att, att_f, logs = attend(numbers, order, own, far)
-    att = after(att, got_near)
+    part = lax.dynamic_index_in_dim(out_weight.reshape(cores, -1, width), core, 0, False)
+    part = after(part, full)
+    part = [part] + [swap(part, "fsdp", k) for k in range(1, planes)]
+    half = list(attend(numbers, order, queries, kvs, None))
+    sends = [place(far_slots[k], after(far_cots[k], half[0], *part)) for k in evens]
+    half[0] = after(half[0], gys[0], *sends)
+    att, att_f, logs = attend(numbers, order, queries, kvs, half)
+    part = jnp.stack(in_order(part, plane))
+    part = in_order([part] + [swap(part, "ctx", k) for k in range(1, cores)], core)
+    out_full = jnp.stack(part, axis=1).reshape(width, width)
+    for k, send in zip(evens, sends):
+        gys[k] = exchange(send)
     att_t = trade(att, "ctx", across).reshape(width, TOK_DEV)
+    gys[1] = swap(after(gys[0], *sends), "fsdp", 1)
+    att_t = after(att_t, gys[1])
     middle, normed, sent = middle_step(att_t, own_hidden, out_full, vecs, slot, all_slots)
 
-    tokens = [exchange(sent)]
-    tokens.append(swap(tokens[0], "fsdp", 1))
+    tokens, acts, gpres, gns, eys = ([None] * planes for _ in range(5))
+
+    def run(k, *earlier):
+        acts[k], gpres[k], gns[k], eys[k] = expert_step(
+            after(tokens[k], *earlier), gys[k], expert_in, expert_out
+        )
+
+    tokens[0] = exchange(sent)
+    run(0)
+    done = [acts[0]]
     for k in evens:
+        gys[k + 1] = swap(after(gys[k], normed), "fsdp", 1)
         rows = swap(normed, "fsdp", k)
-        send = place(far_slots[k], after(rows, got_far))
-        tokens.append(exchange(send))
+        send = place(far_slots[k], after(rows, *done))
+        tokens[k] = exchange(send)
         rows = swap(after(rows, send), "fsdp", 1)
-        tokens.append(exchange(place(far_slots[k + 1], rows)))
-    acts, gpres, gns, eys = [], [], [], []
-    for k in range(planes):
-        act, gpre, gn, ey = expert_step(tokens[k], gys[k], expert_in, expert_out)
-        acts.append(act)
-        gpres.append(gpre)
-        gns.append(gn)
-        eys.append(ey)
-    grad_expert_in, grad_expert_out = expert_grads(tokens, gys, acts, gpres)
-
-    far_grad = jnp.zeros((TOK_DEV, width), f32)
+        tokens[k + 1] = exchange(place(far_slots[k + 1], after(rows, gys[k + 1])))
+        tokens[1] = swap(after(tokens[0], send), "fsdp", 1)
+        run(k)
+        run(k + 1, acts[k])
+        done = [acts[k + 1]]
+
+    gns[planes - 1] = after(gns[planes - 1], tokens[1])
+
+    far_grad, far_ys = jnp.zeros((TOK_DEV, width), f32), []
     for k in evens:
-        last = fetch(far_slots[k + 1], exchange(gns[k + 1]).reshape(all_slots, width)).astype(bf16)
-        back = fetch(far_slots[k], exchange(gns[k]).reshape(all_slots, width))
+        last = fetch(far_slots[k + 1], exchange(gns[k + 1])).astype(bf16)
+        far_y = swap(eys[k + 1], "fsdp", 1)
+        tokens[1] = after(tokens[1], last, far_y)
+        far_ys.append((eys[k].astype(f32) + far_y.astype(f32)).astype(bf16))
+        back = fetch(far_slots[k], exchange(gns[k]))
         back = (back + swap(last, "fsdp", 1).astype(f32)).astype(bf16)
         far_grad = far_grad + swap(back, "fsdp", k).astype(f32)
-    near = (gns[0].astype(f32) + swap(gns[1], "fsdp", 1).astype(f32)).astype(bf16)
-    near = exchange(near).reshape(all_slots, width)
-    far_grad = after(far_grad.astype(bf16), near, grad_expert_in)
+    run(1)
+    grad_expert_in, grad_expert_out = expert_grads(tokens, gys, acts, gpres)
+    near = fetch(far_slots[1], after(exchange(gns[1]), back)).astype(bf16)
+    near = swap(near, "fsdp", 1)
+    far_grad = (far_grad + near.astype(f32)).astype(bf16)
+    got = exchange(gns[0]).reshape(all_slots, width)
+    stacked = [p.reshape(packed) for p in [eys[0], eys[1]] + far_ys]
+    far_grad = after(far_grad, got, grad_expert_in, *stacked)
     grad_middle, branch, gatt, sums_two = turn_step(
-        near, far_grad, slot, middle, out_cot, out_full, vecs
+        got, far_grad, slot, middle, out_cot, out_full, vecs
     )
     gatt = trade(gatt.reshape(groups, span, TOK_DEV), "ctx", across)
-    outs = out_grad_step(att_t, branch, sums_two)
-
-    total_y = eys[0].astype(f32) + swap(eys[1], "fsdp", 1).astype(f32)
-    for k in evens:
-        back = (eys[k].astype(f32) + swap(eys[k + 1], "fsdp", 1).astype(f32)).astype(bf16)
-        total_y = total_y + swap(back, "fsdp", k).astype(f32)
-    token_y = fetch(slot, exchange(total_y.astype(bf16)).reshape(all_slots, width))
-    layer_out = (middle + token_y).astype(bf16)
-
-    gq, gown, gfar = attend_back(numbers, order, own, far, gatt, att_f, logs)
+    outs = out_grad_step(att_t, branch, sums_two, planes, devices)
+    stacked = jnp.concatenate(stacked + [outs], axis=1)
+    gatt = after(gatt, stacked)
+    returned = trade(after(stacked, gatt), "ctx")
+
+    gq, gown, gfar = attend_back(numbers, order, queries, kvs, gatt, att_f, logs)
     got = jnp.stack([swap(gfar[k - 1], "ctx", k) for k in range(1, cores)])
-    grad_rows, grad_cols = rows_step(gq, gown, got, wt, TOK_DEV)
-    grad_normed = grad_rows[0].astype(f32)
-    for j in range(1, groups):
-        grad_normed = grad_normed + swap(grad_rows[j], "ctx", j * cores).astype(f32)
-    mixed = weights_step(grad_cols, grad_rows, vecs, hidden, cores, planes)
+    grad_cols, grad_rows = rows_step(order, gq, gown, got, wt, TOK_DEV)
+    came = trade(grad_rows, "ctx", across)
+    grad_normed = jnp.sum(came.astype(f32), axis=0)
+    mixed = weights_step(order, grad_cols, grad_rows, vecs, hidden, cores, planes)
     own_normal, own_scale = norm_stats(own_hidden.astype(f32))
     grad_hidden = grad_middle + norm_back(own_normal, own_scale, vecs[0], grad_normed)
 
@@ -701,24 +735,38 @@
             total = total + swap(pick(k), axis, k * stride).astype(f32)
         return total.astype(bf16)
 
-    part = keep(keep(mixed, core, "ctx", 1), plane, "fsdp", 1)
-    grad_qkv, vec_one = assemble(share(part, devices, "ctx"), span, groups)
-
+    size = local_experts * room
     rows = width // planes
-    wide = outs.shape[1]
-    part = jnp.moveaxis(outs.reshape(planes, devices, rows // devices, wide), 1, 0)
-    part = jnp.sum(trade(part, "ctx").astype(f32), axis=0).astype(bf16)
-    part = keep(part, plane, "fsdp", 1)
-    part = share(part, devices, "ctx").reshape(rows, wide).astype(f32)
+    outs = returned[:, (len(evens) + 2) * size :].astype(f32)
+    outs = jnp.sum(outs, axis=0).astype(bf16)
+    outs, sums = outs[:-16].reshape(planes, rows // devices, width), outs[-16:]
+    sums = jnp.broadcast_to(sums[None], (planes,) + sums.shape)
+    part = keep(mixed, core, "ctx", 1)
+    part = keep(jnp.concatenate([part, outs, sums], axis=1), plane, "fsdp", 1)
+    part, sums = part[:-16], part[-16:]
+    vec_two = lax.dynamic_slice_in_dim(sums, plane * rows, rows, 1).astype(f32)
+
+    returned = after(returned, part)
+    token_y = fetch(slot, returned[:, :size])
+    for i, k in enumerate(evens):
+        back = fetch(far_slots[k], returned[:, (i + 2) * size : (i + 3) * size]).astype(bf16)
+        token_y = token_y + swap(back, "fsdp", k).astype(f32)
+    back = fetch(far_slots[1], returned[:, size : 2 * size]).astype(bf16)
+    token_y = token_y + swap(back, "fsdp", 1).astype(f32)
+    layer_out = (middle + token_y).astype(bf16)
+
+    part = share(part, devices, "ctx", None, trade)
+    grad_qkv, vec_one = assemble(part, rows // cores, span, groups)
+    part = part[:, rows // cores :].reshape(rows, width).astype(f32)
     return (
         layer_out[None],
         grad_hidden[None],
         grad_qkv,
-        part[:, :width],
+        part,
         vec_one[:, 0],
         vec_one[:, 1],
-        part[:, width],
-        part[:, width + 1],
+        vec_two[0],
+        vec_two[1],
         grad_expert_in,
         grad_expert_out,
     )

time: 609 us -> 587 us (0.964)
  between operations: 14.9 us -> 1.85 us
  matrix products: 16.6 us -> 27.4 us
  starting transfers between devices: 95.3 us -> 86.2 us
  local copies, waits for them, and re-layouts: 41.1 us -> 33.3 us
    ppermute x31 -> x26, waiting for transfers between devices: 152 us -> 112 us  [swap(): return lax.ppermute(value, axis, [(i, i ^ offset) for i in range(size)])]
    all_to_all x13 -> x14, waiting for transfers between devices: 47.5 us -> 85 us  [plain_trade(): lax.all_to_all(parts, axis, 0, 0, tiled=True, axis_index_groups=groups)]
    ppermute x31 -> x26, starting transfers between devices: 40.6 us -> 29.7 us  [swap(): return lax.ppermute(value, axis, [(i, i ^ offset) for i in range(size)])]
    dot_general x7 -> x10, matrix products: 16.6 us -> 27.4 us  [dot(): return lax.dot_general(a, b, dims, preferred_element_type=f32)]
    slice x8, local copies, waits for them, and re-layouts: 14.4 us -> 4.62 us  [the longest x1 3.88 us: local(): token_y = fetch(slot, returned[:, :size])]
    convert_element_type x5, other arithmetic: 12 us -> 5.56 us  [the longest x1 2.49 us: local(): far_grad = (far_grad + near.astype(f32)).astype(bf16)]
    pallas_call x9 -> x8, Pallas kernels: 116 us -> 114 us  [the longest x1 49.7 us: attend_back(): pl.pallas_call(partial(attend_back_kernel, len(queries), len(queries + kv...]
    all_to_all x13 -> x14, starting transfers between devices: 54.7 us -> 56.5 us  [plain_trade(): lax.all_to_all(parts, axis, 0, 0, tiled=True, axis_index_groups=groups)]
  transfers between devices with their start and end apart: 45 -> 40, of which waited for: 17 -> 21; matrix products, arithmetic and copies ran while one was open for 13% -> 12% of each run, Pallas kernels for 31% -> 30%
where the time goes in v4:
time: 587 us; the launch traced here: 578 us
  waiting for transfers between devices  197 us (34%)
  Pallas kernels  187 us (32%)
  starting transfers between devices  86.2 us (15%)
  local copies, waits for them, and re-layouts  33.3 us (6%)
  matrix products  27.4 us (5%)
  other arithmetic  23 us (4%)
  blocking collectives  22.6 us (4%)
    ppermute x26, waiting for transfers between devices, swap(): return lax.ppermute(value, axis, [(i, i ^ offset) for i in range(size)])  112 us
    all_to_all x14, waiting for transfers between devices, plain_trade(): lax.all_to_all(parts, axis, 0, 0, tiled=True, axis_index_groups=groups)  85 us
    all_to_all x14, starting transfers between devices, plain_trade(): lax.all_to_all(parts, axis, 0, 0, tiled=True, axis_index_groups=groups)  56.5 us
    pallas_call x1, Pallas kernels, attend_back(): pl.pallas_call(partial(attend_back_kernel, len(queries), len(queries + kv...  49.7 us
    pallas_call x4, Pallas kernels, expert_step(): pl.pallas_call(expert_kernel, grid=(experts,), in_specs=[token_spec, toke...  40.7 us
    pallas_call x2, Pallas kernels, attend(): pl.pallas_call(partial(attend_kernel, high, len(queries), len(queries + k...  36 us
    ppermute x26, starting transfers between devices, swap(): return lax.ppermute(value, axis, [(i, i ^ offset) for i in range(size)])  29.7 us
    dot_general x10, matrix products, dot(): return lax.dot_general(a, b, dims, preferred_element_type=f32)  27.4 us
  transfers between devices with their start and end apart: 40, of which 21 were waited for; matrix products, arithmetic and copies ran while one was open for 12% of the time, Pallas kernels for 30%

profile of v4, /device:TPU:0, one launch (start us, length us, event | category | flops | bytes accessed | tf_op | source)
XLA Modules:
  0.0 577.8 jit_solution(5403072329246175865)
XLA Ops:
  14.8 22.6 %all_gather.3 = bf16[768,640]{1,0:T(8,128)(2,1)S(1)} all-gather(bf16[192,640]{1,0:T(8,128)(2,1)S(1)} %concatenate.16), channel_id=1, replica_groups=mesh['ctx'=8,'fsdp'=4] {'fsdp'}, dimensions={0}, use_global_device_ids=true | all-gather | bytes 1228800 | tf_op jit(solution)/shard_map/all_gather | solution.py:634
  65.5 12.6 %attend_low.1 = (bf16[4,192,512]{2,1,0:T(8,128)(2,1)}, f32[192,2048]{1,0:T(8,128)}, f32[8,8,256]{2,1,0:T(8,128)}) custom-call(s32[16]{0:T(128)} %reshape.343.number_ref, s32[4]{0:T(128)} %iota_xor_fusion.order_ref, bf16[192,512]{1,0:T(8,128)(2,1)} %get-tuple-element.85.refs_0_, bf16[192,1536]{1,0:T(8,128)(2,1)} %get-tuple-element.86.refs_1_, ...), custom_call_target="tpu_custom_call" | custom-call | flops 19327352 | bytes 6291 | tf_op jit(solution)/shard_map/attend_low/pallas_call | solution.py:197
  78.1 12.0 %collective-permute-done.5 = bf16[512,768]{1,0:T(8,128)(2,1)} collective-permute-done((bf16[512,768]{1,0:T(8,128)(2,1)}, bf16[512,768]{1,0:T(8,128)(2,1)}, u32[]{:S(2)}, u32[]{:S(2)}) %collective-permute-start.5) | collective-permute-done | bytes 786464 | tf_op jit(solution)/shard_map/ppermute | solution.py:33
  103.6 23.4 %attend_high.1 = (bf16[4,192,512]{2,1,0:T(8,128)(2,1)}, f32[192,2048]{1,0:T(8,128)}, f32[8,8,256]{2,1,0:T(8,128)}) custom-call(s32[16]{0:T(128)} %reshape.343.number_ref, s32[4]{0:T(128)} %iota_xor_fusion.order_ref, bf16[192,512]{1,0:T(8,128)(2,1)} %get-tuple-element.85.refs_0_, ...), custom_call_target="tpu_custom_call", output_to_operand_aliasing={{0}: (8, {}), {1}: (9, {}), {2}: (10, {})} | custom-call | flops 19327352 | bytes 6291 | tf_op jit(solution)/shard_map/attend_high/pallas_call | solution.py:197
  135.9 7.3 %all-to-all-done.2 = bf16[4,192,512]{2,1,0:T(8,128)(2,1)} async-done(((bf16[4,192,512]{2,1,0:T(8,128)(2,1)}), bf16[4,192,512]{2,1,0:T(8,128)(2,1)}, u32[]{:S(2)}, u32[]{:S(2)}) %all-to-all-start.2) | async-done | bytes 786464 | tf_op jit(solution)/shard_map/all_to_all | solution.py:37
  154.8 18.3 %all-to-all-done.3 = bf16[8,128,768]{2,1,0:T(8,128)(2,1)S(1)} async-done(((bf16[8,128,768]{2,1,0:T(8,128)(2,1)}), bf16[8,128,768]{2,1,0:T(8,128)(2,1)S(1)}, u32[]{:S(2)}, u32[]{:S(2)}) %all-to-all-start.3) | async-done | bytes 1572896 | tf_op jit(solution)/shard_map/all_to_all | solution.py:37
  174.4 10.2 %expert_step.4 = (bf16[8,4,32,768]{3,2,1,0:T(8,128)(2,1)}, bf16[8,4,32,768]{3,2,1,0:T(8,128)(2,1)}, bf16[8,4,32,768]{3,2,1,0:T(8,128)(2,1)}, bf16[8,4,32,768]{3,2,1,0:T(8,128)(2,1)}) custom-call(bf16[8,4,32,768]{3,2,1,0:T(8,128)(2,1)} %bitcast.127, bf16[8,4,32,768]{3,2,1,0:T(8,128)(2,1)} %bitcast.122, bf16[4,768,768]{2,1,0:T(8,128)(2,1)} %first_ref.7, ...), custom_call_target="tpu_custom_call" | custom-call | flops 4831838 | bytes 18874 | tf_op jit(solution)/shard_map/expert_step/pallas_call | solution.py:538
  199.5 7.5 %collective-permute-done.14.gy_ref.refs_7_ = bf16[8,4,32,768]{3,2,1,0:T(8,128)(2,1)} collective-permute-done((bf16[8,4,32,768]{3,2,1,0:T(8,128)(2,1)S(1)}, bf16[8,4,32,768]{3,2,1,0:T(8,128)(2,1)}, u32[]{:S(2)}, u32[]{:S(2)}) %collective-permute-start.14) | collective-permute-done | bytes 1572896 | tf_op jit(solution)/shard_map/ppermute | solution.py:33
  207.0 16.7 %collective-permute-done.13 = bf16[512,768]{1,0:T(8,128)(2,1)S(1)} collective-permute-done((bf16[512,768]{1,0:T(8,128)(2,1)}, bf16[512,768]{1,0:T(8,128)(2,1)S(1)}, u32[]{:S(2)}, u32[]{:S(2)}) %collective-permute-start.13) | collective-permute-done | bytes 786464 | tf_op jit(solution)/shard_map/ppermute | solution.py:33
  230.5 10.2 %expert_step.5 = (bf16[8,4,32,768]{3,2,1,0:T(8,128)(2,1)}, bf16[8,4,32,768]{3,2,1,0:T(8,128)(2,1)}, bf16[8,4,32,768]{3,2,1,0:T(8,128)(2,1)}, bf16[8,4,32,768]{3,2,1,0:T(8,128)(2,1)}) custom-call(bf16[8,4,32,768]{3,2,1,0:T(8,128)(2,1)} %bitcast.38.x_ref.refs_2_, bf16[8,4,32,768]{3,2,1,0:T(8,128)(2,1)} %bitcast.125, bf16[4,768,768]{2,1,0:T(8,128)(2,1)} %first_ref.7, ...), custom_call_target="tpu_custom_call" | custom-call | flops 4831838 | bytes 18874 | tf_op jit(solution)/shard_map/expert_step/pallas_call | solution.py:538
  240.6 10.8 %all-to-all-done.5 = bf16[8,128,768]{2,1,0:T(8,128)(2,1)S(1)} async-done(((bf16[8,128,768]{2,1,0:T(8,128)(2,1)}), bf16[8,128,768]{2,1,0:T(8,128)(2,1)S(1)}, u32[]{:S(2)}, u32[]{:S(2)}) %all-to-all-start.5) | async-done | bytes 1572896 | tf_op jit(solution)/shard_map/all_to_all | solution.py:37
  252.6 10.1 %expert_step.6 = (bf16[8,4,32,768]{3,2,1,0:T(8,128)(2,1)}, bf16[8,4,32,768]{3,2,1,0:T(8,128)(2,1)}, bf16[8,4,32,768]{3,2,1,0:T(8,128)(2,1)}, bf16[8,4,32,768]{3,2,1,0:T(8,128)(2,1)}) custom-call(bf16[8,4,32,768]{3,2,1,0:T(8,128)(2,1)} %bitcast.130, bf16[8,4,32,768]{3,2,1,0:T(8,128)(2,1)} %collective-permute-done.14.gy_ref.refs_7_, ...), custom_call_target="tpu_custom_call" | custom-call | flops 4831838 | bytes 18874 | tf_op jit(solution)/shard_map/expert_step/pallas_call | solution.py:538
  266.7 20.6 %all-to-all-done.6 = bf16[8,128,768]{2,1,0:T(8,128)(2,1)S(1)} async-done(((bf16[8,128,768]{2,1,0:T(8,128)(2,1)}), bf16[8,128,768]{2,1,0:T(8,128)(2,1)S(1)}, u32[]{:S(2)}, u32[]{:S(2)}) %all-to-all-start.6) | async-done | bytes 1572896 | tf_op jit(solution)/shard_map/all_to_all | solution.py:37
  292.9 10.5 %collective-permute-done.15 = bf16[8,4,32,768]{3,2,1,0:T(8,128)(2,1)} collective-permute-done((bf16[8,4,32,768]{3,2,1,0:T(8,128)(2,1)}, bf16[8,4,32,768]{3,2,1,0:T(8,128)(2,1)}, u32[]{:S(2)}, u32[]{:S(2)}) %collective-permute-start.15) | collective-permute-done | bytes 1572896 | tf_op jit(solution)/shard_map/ppermute | solution.py:33
  303.4 10.2 %expert_step.7 = (bf16[8,4,32,768]{3,2,1,0:T(8,128)(2,1)}, bf16[8,4,32,768]{3,2,1,0:T(8,128)(2,1)}, bf16[8,4,32,768]{3,2,1,0:T(8,128)(2,1)}, bf16[8,4,32,768]{3,2,1,0:T(8,128)(2,1)}) custom-call(bf16[8,4,32,768]{3,2,1,0:T(8,128)(2,1)} %collective-permute-done.12.x_ref.refs_1_, bf16[8,4,32,768]{3,2,1,0:T(8,128)(2,1)} %collective-permute-done.9.gy_ref.refs_5_, ...), custom_call_target="tpu_custom_call" | custom-call | flops 4831838 | bytes 18874 | tf_op jit(solution)/shard_map/expert_step/pallas_call | solution.py:538
  317.7 20.7 %all-to-all-done.8 = bf16[8,128,768]{2,1,0:T(8,128)(2,1)S(1)} async-done(((bf16[8,128,768]{2,1,0:T(8,128)(2,1)}), bf16[8,128,768]{2,1,0:T(8,128)(2,1)S(1)}, u32[]{:S(2)}, u32[]{:S(2)}) %all-to-all-start.8) | async-done | bytes 1572896 | tf_op jit(solution)/shard_map/all_to_all | solution.py:37
  351.9 17.6 %expert_grads.1 = (f32[4,768,768]{2,1,0:T(8,128)}, f32[4,768,768]{2,1,0:T(8,128)}) custom-call(bf16[8,4,32,768]{3,2,1,0:T(8,128)(2,1)} %bitcast.128, bf16[8,4,32,768]{3,2,1,0:T(8,128)(2,1)} %collective-permute-done.12.x_ref.refs_1_, bf16[8,4,32,768]{3,2,1,0:T(8,128)(2,1)} %bitcast.38.x_ref.refs_2_, bf16[8,4,32,768]{3,2,1,0:T(8,128)(2,1)} %bitcast.131, ...), custom_call_target="tpu_custom_call" | custom-call | flops 9663676 | bytes 18874 | tf_op jit(solution)/shard_map/expert_grads/pallas_call | solution.py:566
  371.5 12.9 %collective-permute-done.17 = bf16[512,768]{1,0:T(8,128)(2,1)} collective-permute-done((bf16[512,768]{1,0:T(8,128)(2,1)}, bf16[512,768]{1,0:T(8,128)(2,1)}, u32[]{:S(2)}, u32[]{:S(2)}) %collective-permute-start.17) | collective-permute-done | bytes 786464 | tf_op jit(solution)/shard_map/ppermute | solution.py:33
  389.6 6.5 %turn.1 = (f32[512,768]{1,0:T(8,128)}, bf16[512,768]{1,0:T(8,128)(2,1)}, bf16[768,512]{1,0:T(8,128)(2,1)}, f32[128,768]{1,0:T(8,128)}) custom-call(bf16[1024,768]{1,0:T(8,128)(2,1)} %bitcast.138, bf16[512,768]{1,0:T(8,128)(2,1)} %add_convert_fusion.2.far_ref, s32[512,1]{1,0:T(8,128)} %copy.71.slot_ref, f32[512,768]{1,0:T(8,128)} %get-tuple-element.102.mid_ref, ...), custom_call_target="tpu_custom_call" | custom-call | flops 1409286 | bytes 4718 | tf_op jit(solution)/shard_map/turn/pallas_call | solution.py:380
  416.1 49.7 %attend_back.1 = (bf16[192,2048]{1,0:T(8,128)(2,1)}, bf16[384,2048]{1,0:T(8,128)(2,1)}, bf16[1,384,2048]{2,1,0:T(8,128)(2,1)}) custom-call(s32[16]{0:T(128)} %reshape.343.number_ref, s32[4]{0:T(128)} %iota_xor_fusion.order_ref, bf16[4,192,512]{2,1,0:T(8,128)(2,1)} %copy-done.14, f32[192,2048]{1,0:T(8,128)} %get-tuple-element.146.att_t_ref, ...), custom_call_target="tpu_custom_call" | custom-call | flops 48318384 | bytes 12582 | tf_op jit(solution)/shard_map/attend_back/pallas_call | solution.py:302
  470.6 6.9 %rows.1 = (bf16[576,2048]{1,0:T(8,128)(2,1)}, bf16[4,512,768]{2,1,0:T(8,128)(2,1)}) custom-call(s32[4]{0:T(128)} %iota_xor_fusion.order_ref, bf16[192,2048]{1,0:T(8,128)(2,1)} %get-tuple-element.148.gq_ref, bf16[384,2048]{1,0:T(8,128)(2,1)} %get-tuple-element.149.gown_ref, bf16[1,384,2048]{2,1,0:T(8,128)(2,1)} %bitcast.144, bf16[576,768]{1,0:T(8,128)(2,1)} %bitcast.134), custom_call_target="tpu_custom_call" | custom-call | flops 1811939 | bytes 6291 | tf_op jit(solution)/shard_map/rows/pallas_call | solution.py:434
  477.5 9.1 %weights.1 = bf16[2,4,96,768]{3,2,1,0:T(8,128)(2,1)} custom-call(s32[4]{0:T(128)} %iota_xor_fusion.order_ref, bf16[576,2048]{1,0:T(8,128)(2,1)} %get-tuple-element.151.cols_ref, f32[4,768]{1,0:T(4,128)} %bitcast.162, bf16[4,512,768]{2,1,0:T(8,128)(2,1)} %get-tuple-element.155.rows_ref, bf16[512,768]{1,0:T(8,128)(2,1)} %bitcast.120, ...), custom_call_target="tpu_custom_call" | custom-call | flops 1811939 | bytes 4718 | tf_op jit(solution)/shard_map/weights/pallas_call | solution.py:476
  506.5 9.8 %collective-permute-done.22 = bf16[136,768]{1,0:T(8,128)(2,1)S(1)} collective-permute-done((bf16[136,768]{1,0:T(8,128)(2,1)S(1)}, bf16[136,768]{1,0:T(8,128)(2,1)S(1)}, u32[]{:S(2)}, u32[]{:S(2)}) %collective-permute-start.22) | collective-permute-done | bytes 208928 | tf_op jit(solution)/shard_map/ppermute | solution.py:33
  538.4 17.5 %collective-permute-done.25 = bf16[512,768]{1,0:T(8,128)(2,1)S(1)} collective-permute-done((bf16[512,768]{1,0:T(8,128)(2,1)}, bf16[512,768]{1,0:T(8,128)(2,1)S(1)}, u32[]{:S(2)}, u32[]{:S(2)}) %collective-permute-start.25) | collective-permute-done | bytes 786464 | tf_op jit(solution)/shard_map/ppermute | solution.py:33
  (217 shorter events, 222.2 us)
Async XLA Ops:
  0.7 47.7 %collective-permute-start = (bf16[512,768]{1,0:T(8,128)(2,1)}, bf16[512,768]{1,0:T(8,128)(2,1)S(1)}, u32[]{:S(2)}, u32[]{:S(2)}) collective-permute-start(bf16[512,768]{1,0:T(8,128)(2,1)} %bitcast.115), channel_id=1, source_target_pairs={{0,8},{4,12},{8,0},{12,4},{16,24},{20,28},{24,16},{28,20},{1,9},{5... | collective-permute-start | bytes 2359304 | tf_op jit(solution)/shard_map/ppermute | solution.py:33
  3.7 44.8 %collective-permute-start.1 = (bf16[512,768]{1,0:T(8,128)(2,1)}, bf16[512,768]{1,0:T(8,128)(2,1)S(1)}, u32[]{:S(2)}, u32[]{:S(2)}) collective-permute-start(bf16[512,768]{1,0:T(8,128)(2,1)} %bitcast.116), channel_id=1, source_target_pairs={{0,16},{4,20},{8,24},{12,28},{16,0},{20,4},{24,8},{28,12},{1,17},{... | collective-permute-start | bytes 2359304 | tf_op jit(solution)/shard_map/ppermute | solution.py:33
  5.2 44.5 %collective-permute-start.2 = (bf16[512,768]{1,0:T(8,128)(2,1)}, bf16[512,768]{1,0:T(8,128)(2,1)}, u32[]{:S(2)}, u32[]{:S(2)}) collective-permute-start(bf16[512,768]{1,0:T(8,128)(2,1)} %bitcast.117), channel_id=1, source_target_pairs={{0,24},{4,28},{8,16},{12,20},{16,8},{20,12},{24,0},{28,4},{1,25},{... | collective-permute-start | bytes 2359304 | tf_op jit(solution)/shard_map/ppermute | solution.py:33
  37.4 40.7 %collective-permute-start.6 = (bf16[96,768]{1,0:T(8,128)(2,1)}, bf16[96,768]{1,0:T(8,128)(2,1)}, u32[]{:S(2)}, u32[]{:S(2)}) collective-permute-start(bf16[96,768]{1,0:T(8,128)(2,1)} %dynamic-slice_bitcast_fusion.4), channel_id=1, source_target_pairs={{0,1},{1,0},{2,3},{3,2},{4,5},{5,4},{6,7},{7,6},{8,9},{9,8},{10,11... | collective-permute-start | bytes 442376 | tf_op jit(solution)/shard_map/ppermute | solution.py:33
  37.4 40.7 %collective-permute-start.7 = (bf16[96,768]{1,0:T(8,128)(2,1)}, bf16[96,768]{1,0:T(8,128)(2,1)}, u32[]{:S(2)}, u32[]{:S(2)}) collective-permute-start(bf16[96,768]{1,0:T(8,128)(2,1)} %dynamic-slice_bitcast_fusion.4), channel_id=1, source_target_pairs={{0,2},{1,3},{2,0},{3,1},{4,6},{5,7},{6,4},{7,5},{8,10},{9,11},{10,... | collective-permute-start | bytes 442376 | tf_op jit(solution)/shard_map/ppermute | solution.py:33
  48.5 41.6 %collective-permute-start.5 = (bf16[512,768]{1,0:T(8,128)(2,1)}, bf16[512,768]{1,0:T(8,128)(2,1)}, u32[]{:S(2)}, u32[]{:S(2)}) collective-permute-start(bf16[512,768]{1,0:T(8,128)(2,1)} %bitcast.14.cot_ref), channel_id=1, source_target_pairs={{0,2},{1,3},{2,0},{3,1},{4,6},{5,7},{6,4},{7,5},{8,10},{9,11},{10,... | collective-permute-start | bytes 2359304 | tf_op jit(solution)/shard_map/ppermute | solution.py:33
  55.2 38.2 %all-to-all-start = ((bf16[8,128,768]{2,1,0:T(8,128)(2,1)}), bf16[8,128,768]{2,1,0:T(8,128)(2,1)S(1)}, u32[]{:S(2)}, u32[]{:S(2)}) async-start(bf16[8,128,768]{2,1,0:T(8,128)(2,1)} %bitcast.146), calls=%async_computation | async-start | bytes 3145728 | tf_op jit(solution)/shard_map/all_to_all | solution.py:37
  93.4 33.6 %all-to-all-start.1 = ((bf16[8,128,768]{2,1,0:T(8,128)(2,1)}), bf16[8,128,768]{2,1,0:T(8,128)(2,1)S(1)}, u32[]{:S(2)}, u32[]{:S(2)}) async-start(bf16[8,128,768]{2,1,0:T(8,128)(2,1)} %bitcast.147), calls=%async_computation.1 | async-start | bytes 3145728 | tf_op jit(solution)/shard_map/all_to_all | solution.py:37
  97.4 38.5 %collective-permute-start.9 = (bf16[8,4,32,768]{3,2,1,0:T(8,128)(2,1)S(1)}, bf16[8,4,32,768]{3,2,1,0:T(8,128)(2,1)}, u32[]{:S(2)}, u32[]{:S(2)}) collective-permute-start(bf16[8,4,32,768]{3,2,1,0:T(8,128)(2,1)S(1)} %bitcast.121), channel_id=1, source_target_pairs={{0,1},{1,0},{2,3},{3,2},{4,5},{5,4},{6,7},{7,6},{8,9},{9,8},{10,11... | collective-permute-start | bytes 4718600 | tf_op jit(solution)/shard_map/ppermute | solution.py:33
  103.4 27.8 %collective-permute-start.10 = (bf16[4,96,768]{2,1,0:T(8,128)(2,1)}, bf16[4,96,768]{2,1,0:T(8,128)(2,1)}, u32[]{:S(2)}, u32[]{:S(2)}) collective-permute-start(bf16[4,96,768]{2,1,0:T(8,128)(2,1)} %pad_maximum_fusion.3), channel_id=1, source_target_pairs={{0,4},{4,0},{8,12},{12,8},{16,20},{20,16},{24,28},{28,24},{1,5},{5... | collective-permute-start | bytes 1769480 | tf_op jit(solution)/shard_map/ppermute | solution.py:33
  152.2 37.5 %collective-permute-start.11 = (bf16[512,768]{1,0:T(8,128)(2,1)}, bf16[512,768]{1,0:T(8,128)(2,1)}, u32[]{:S(2)}, u32[]{:S(2)}) collective-permute-start(bf16[512,768]{1,0:T(8,128)(2,1)} %get-tuple-element.106), channel_id=1, source_target_pairs={{0,2},{1,3},{2,0},{3,1},{4,6},{5,7},{6,4},{7,5},{8,10},{9,11},{10,... | collective-permute-start | bytes 2359304 | tf_op jit(solution)/shard_map/ppermute | solution.py:33
  152.8 54.2 %collective-permute-start.14 = (bf16[8,4,32,768]{3,2,1,0:T(8,128)(2,1)S(1)}, bf16[8,4,32,768]{3,2,1,0:T(8,128)(2,1)}, u32[]{:S(2)}, u32[]{:S(2)}) collective-permute-start(bf16[8,4,32,768]{3,2,1,0:T(8,128)(2,1)S(1)} %bitcast.124), channel_id=1, source_target_pairs={{0,1},{1,0},{2,3},{3,2},{4,5},{5,4},{6,7},{7,6},{8,9},{9,8},{10,11... | collective-permute-start | bytes 4718600 | tf_op jit(solution)/shard_map/ppermute | solution.py:33
  193.0 33.0 %all-to-all-start.4 = ((bf16[8,128,768]{2,1,0:T(8,128)(2,1)}), bf16[8,128,768]{2,1,0:T(8,128)(2,1)}, u32[]{:S(2)}, u32[]{:S(2)}) async-start(bf16[8,128,768]{2,1,0:T(8,128)(2,1)} %bitcast.150), calls=%async_computation.4 | async-start | bytes 3145728 | tf_op jit(solution)/shard_map/all_to_all | solution.py:37
  197.4 26.4 %collective-permute-start.13 = (bf16[512,768]{1,0:T(8,128)(2,1)}, bf16[512,768]{1,0:T(8,128)(2,1)S(1)}, u32[]{:S(2)}, u32[]{:S(2)}) collective-permute-start(bf16[512,768]{1,0:T(8,128)(2,1)} %collective-permute-done.11), channel_id=1, source_target_pairs={{0,1},{1,0},{2,3},{3,2},{4,5},{5,4},{6,7},{7,6},{8,9},{9,8},{10,11... | collective-permute-start | bytes 2359304 | tf_op jit(solution)/shard_map/ppermute | solution.py:33
  197.5 65.2 %collective-permute-start.12 = (bf16[8,4,32,768]{3,2,1,0:T(8,128)(2,1)S(1)}, bf16[8,4,32,768]{3,2,1,0:T(8,128)(2,1)}, u32[]{:S(2)}, u32[]{:S(2)}) collective-permute-start(bf16[8,4,32,768]{3,2,1,0:T(8,128)(2,1)S(1)} %bitcast.129), channel_id=1, source_target_pairs={{0,1},{1,0},{2,3},{3,2},{4,5},{5,4},{6,7},{7,6},{8,9},{9,8},{10,11... | collective-permute-start | bytes 4718600 | tf_op jit(solution)/shard_map/ppermute | solution.py:33
  266.3 37.0 %collective-permute-start.15 = (bf16[8,4,32,768]{3,2,1,0:T(8,128)(2,1)}, bf16[8,4,32,768]{3,2,1,0:T(8,128)(2,1)}, u32[]{:S(2)}, u32[]{:S(2)}) collective-permute-start(bf16[8,4,32,768]{3,2,1,0:T(8,128)(2,1)} %get-tuple-element.120), channel_id=1, source_target_pairs={{0,1},{1,0},{2,3},{3,2},{4,5},{5,4},{6,7},{7,6},{8,9},{9,8},{10,11... | collective-permute-start | bytes 4718600 | tf_op jit(solution)/shard_map/ppermute | solution.py:33
  339.6 48.8 %all-to-all-start.9 = ((bf16[8,128,768]{2,1,0:T(8,128)(2,1)}), bf16[8,128,768]{2,1,0:T(8,128)(2,1)S(1)}, u32[]{:S(2)}, u32[]{:S(2)}) async-start(bf16[8,128,768]{2,1,0:T(8,128)(2,1)} %bitcast.43), calls=%async_computation.9 | async-start | bytes 3145728 | tf_op jit(solution)/shard_map/all_to_all | solution.py:37
  346.6 37.8 %collective-permute-start.17 = (bf16[512,768]{1,0:T(8,128)(2,1)}, bf16[512,768]{1,0:T(8,128)(2,1)}, u32[]{:S(2)}, u32[]{:S(2)}) collective-permute-start(bf16[512,768]{1,0:T(8,128)(2,1)} %add_convert_fusion.3), channel_id=1, source_target_pairs={{0,2},{1,3},{2,0},{3,1},{4,6},{5,7},{6,4},{7,5},{8,10},{9,11},{10,... | collective-permute-start | bytes 2359304 | tf_op jit(solution)/shard_map/ppermute | solution.py:33
  349.3 36.7 %collective-permute-start.18 = (bf16[512,768]{1,0:T(8,128)(2,1)}, bf16[512,768]{1,0:T(8,128)(2,1)}, u32[]{:S(2)}, u32[]{:S(2)}) collective-permute-start(bf16[512,768]{1,0:T(8,128)(2,1)} %fusion.26), channel_id=1, source_target_pairs={{0,1},{1,0},{2,3},{3,2},{4,5},{5,4},{6,7},{7,6},{8,9},{9,8},{10,11... | collective-permute-start | bytes 2359304 | tf_op jit(solution)/shard_map/ppermute | solution.py:33
  411.1 78.9 %all-to-all-start.11 = ((bf16[8,496,768]{2,1,0:T(8,128)(2,1)}), bf16[8,496,768]{2,1,0:T(8,128)(2,1)}, u32[]{:S(2)}, u32[]{:S(2)}) async-start(bf16[8,496,768]{2,1,0:T(8,128)(2,1)} %pad_maximum_fusion), calls=%async_computation.11 | async-start | bytes 12189696 | tf_op jit(solution)/shard_map/all_to_all | solution.py:37
  491.6 41.7 %all-to-all-start.12 = ((bf16[4,512,768]{2,1,0:T(8,128)(2,1)}), bf16[4,512,768]{2,1,0:T(8,128)(2,1)}, u32[]{:S(2)}, u32[]{:S(2)}) async-start(bf16[4,512,768]{2,1,0:T(8,128)(2,1)} %get-tuple-element.155.rows_ref), calls=%async_computation.12 | async-start | bytes 6291456 | tf_op jit(solution)/shard_map/all_to_all | solution.py:37
  522.3 33.7 %collective-permute-start.25 = (bf16[512,768]{1,0:T(8,128)(2,1)}, bf16[512,768]{1,0:T(8,128)(2,1)S(1)}, u32[]{:S(2)}, u32[]{:S(2)}) collective-permute-start(bf16[512,768]{1,0:T(8,128)(2,1)} %fusion.27), channel_id=1, source_target_pairs={{0,1},{1,0},{2,3},{3,2},{4,5},{5,4},{6,7},{7,6},{8,9},{9,8},{10,11... | collective-permute-start | bytes 2359304 | tf_op jit(solution)/shard_map/ppermute | solution.py:33
  524.3 37.2 %collective-permute-start.24 = (bf16[512,768]{1,0:T(8,128)(2,1)}, bf16[512,768]{1,0:T(8,128)(2,1)}, u32[]{:S(2)}, u32[]{:S(2)}) collective-permute-start(bf16[512,768]{1,0:T(8,128)(2,1)} %fusion.25), channel_id=1, source_target_pairs={{0,2},{1,3},{2,0},{3,1},{4,6},{5,7},{6,4},{7,5},{8,10},{9,11},{10,... | collective-permute-start | bytes 2359304 | tf_op jit(solution)/shard_map/ppermute | solution.py:33
  534.6 36.7 %all-to-all-start.13 = ((bf16[8,120,768]{2,1,0:T(8,128)(2,1)}), bf16[8,120,768]{2,1,0:T(8,128)(2,1)S(1)}, u32[]{:S(2)}, u32[]{:S(2)}) async-start(bf16[8,120,768]{2,1,0:T(8,128)(2,1)} %broadcast_in_dim.11), calls=%async_computation.13 | async-start | bytes 2949120 | tf_op jit(solution)/shard_map/all_to_all | solution.py:37
  (46 other events, 442.7 us)

commit v5 on v4

--- a/solution.py
+++ b/solution.py
@@ -750,9 +750,9 @@
     token_y = fetch(slot, returned[:, :size])
     for i, k in enumerate(evens):
         back = fetch(far_slots[k], returned[:, (i + 2) * size : (i + 3) * size]).astype(bf16)
-        token_y = token_y + swap(back, "fsdp", k).astype(f32)
+        token_y = token_y + after(swap(back, "fsdp", k), grad_hidden).astype(f32)
     back = fetch(far_slots[1], returned[:, size : 2 * size]).astype(bf16)
-    token_y = token_y + swap(back, "fsdp", 1).astype(f32)
+    token_y = token_y + after(swap(back, "fsdp", 1), grad_hidden).astype(f32)
     layer_out = (middle + token_y).astype(bf16)
 
     part = share(part, devices, "ctx", None, trade)

time: 587 us -> 578 us (0.985)
  waiting for transfers between devices: 197 us -> 188 us
    unnamed x63 -> x69, local copies, waits for them, and re-layouts: 11.8 us -> 11.7 us
where the time goes in v5:
time: 578 us; the launch traced here: 568 us
  waiting for transfers between devices  188 us (33%)
  Pallas kernels  186 us (32%)
  starting transfers between devices  86.2 us (15%)
  local copies, waits for them, and re-layouts  32 us (6%)
  other arithmetic  25.5 us (4%)
  matrix products  25.5 us (4%)
  blocking collectives  22.6 us (4%)
    ppermute x26, waiting for transfers between devices, swap(): return lax.ppermute(value, axis, [(i, i ^ offset) for i in range(size)])  106 us
    all_to_all x14, waiting for transfers between devices, plain_trade(): lax.all_to_all(parts, axis, 0, 0, tiled=True, axis_index_groups=groups)  82.3 us
    all_to_all x14, starting transfers between devices, plain_trade(): lax.all_to_all(parts, axis, 0, 0, tiled=True, axis_index_groups=groups)  56.6 us
    pallas_call x1, Pallas kernels, attend_back(): pl.pallas_call(partial(attend_back_kernel, len(queries), len(queries + kv...  49.6 us
    pallas_call x4, Pallas kernels, expert_step(): pl.pallas_call(expert_kernel, grid=(experts,), in_specs=[token_spec, toke...  40.7 us
    pallas_call x2, Pallas kernels, attend(): pl.pallas_call(partial(attend_kernel, high, len(queries), len(queries + k...  35.8 us
    ppermute x26, starting transfers between devices, swap(): return lax.ppermute(value, axis, [(i, i ^ offset) for i in range(size)])  29.7 us
    dot_general x10, matrix products, dot(): return lax.dot_general(a, b, dims, preferred_element_type=f32)  25.5 us
  transfers between devices with their start and end apart: 40, of which 21 were waited for; matrix products, arithmetic and copies ran while one was open for 12% of the time, Pallas kernels for 30%

profile of v5, /device:TPU:0, one launch (start us, length us, event | category | flops | bytes accessed | tf_op | source)
XLA Modules:
  0.0 568.4 jit_solution(2352608892819488247)
XLA Ops:
  14.7 22.6 %all_gather.3 = bf16[768,640]{1,0:T(8,128)(2,1)S(1)} all-gather(bf16[192,640]{1,0:T(8,128)(2,1)S(1)} %concatenate.16), channel_id=1, replica_groups=mesh['ctx'=8,'fsdp'=4] {'fsdp'}, dimensions={0}, use_global_device_ids=true | all-gather | bytes 1228800 | tf_op jit(solution)/shard_map/all_gather | solution.py:634
  65.4 11.3 %attend_low.1 = (bf16[4,192,512]{2,1,0:T(8,128)(2,1)}, f32[192,2048]{1,0:T(8,128)}, f32[8,8,256]{2,1,0:T(8,128)}) custom-call(s32[16]{0:T(128)} %reshape.343.number_ref, s32[4]{0:T(128)} %iota_xor_fusion.order_ref, bf16[192,512]{1,0:T(8,128)(2,1)} %get-tuple-element.87.refs_0_, bf16[192,1536]{1,0:T(8,128)(2,1)} %get-tuple-element.88.refs_1_, ...), custom_call_target="tpu_custom_call" | custom-call | flops 19327352 | bytes 6291 | tf_op jit(solution)/shard_map/attend_low/pallas_call | solution.py:197
  76.7 13.4 %collective-permute-done.5 = bf16[512,768]{1,0:T(8,128)(2,1)} collective-permute-done((bf16[512,768]{1,0:T(8,128)(2,1)}, bf16[512,768]{1,0:T(8,128)(2,1)}, u32[]{:S(2)}, u32[]{:S(2)}) %collective-permute-start.5) | collective-permute-done | bytes 786464 | tf_op jit(solution)/shard_map/ppermute | solution.py:33
  103.6 24.5 %attend_high.1 = (bf16[4,192,512]{2,1,0:T(8,128)(2,1)}, f32[192,2048]{1,0:T(8,128)}, f32[8,8,256]{2,1,0:T(8,128)}) custom-call(s32[16]{0:T(128)} %reshape.343.number_ref, s32[4]{0:T(128)} %iota_xor_fusion.order_ref, bf16[192,512]{1,0:T(8,128)(2,1)} %get-tuple-element.87.refs_0_, ...), custom_call_target="tpu_custom_call", output_to_operand_aliasing={{0}: (8, {}), {1}: (9, {}), {2}: (10, {})} | custom-call | flops 19327352 | bytes 6291 | tf_op jit(solution)/shard_map/attend_high/pallas_call | solution.py:197
  135.8 6.1 %all-to-all-done.2 = bf16[4,192,512]{2,1,0:T(8,128)(2,1)} async-done(((bf16[4,192,512]{2,1,0:T(8,128)(2,1)}), bf16[4,192,512]{2,1,0:T(8,128)(2,1)}, u32[]{:S(2)}, u32[]{:S(2)}) %all-to-all-start.2) | async-done | bytes 786464 | tf_op jit(solution)/shard_map/all_to_all | solution.py:37
  153.6 18.3 %all-to-all-done.3 = bf16[8,128,768]{2,1,0:T(8,128)(2,1)S(1)} async-done(((bf16[8,128,768]{2,1,0:T(8,128)(2,1)}), bf16[8,128,768]{2,1,0:T(8,128)(2,1)S(1)}, u32[]{:S(2)}, u32[]{:S(2)}) %all-to-all-start.3) | async-done | bytes 1572896 | tf_op jit(solution)/shard_map/all_to_all | solution.py:37
  173.1 10.3 %expert_step.4 = (bf16[8,4,32,768]{3,2,1,0:T(8,128)(2,1)}, bf16[8,4,32,768]{3,2,1,0:T(8,128)(2,1)}, bf16[8,4,32,768]{3,2,1,0:T(8,128)(2,1)}, bf16[8,4,32,768]{3,2,1,0:T(8,128)(2,1)}) custom-call(bf16[8,4,32,768]{3,2,1,0:T(8,128)(2,1)} %bitcast.126, bf16[8,4,32,768]{3,2,1,0:T(8,128)(2,1)} %bitcast.121, bf16[4,768,768]{2,1,0:T(8,128)(2,1)} %first_ref.7, ...), custom_call_target="tpu_custom_call" | custom-call | flops 4831838 | bytes 18874 | tf_op jit(solution)/shard_map/expert_step/pallas_call | solution.py:538
  198.3 7.4 %collective-permute-done.14.gy_ref.refs_7_ = bf16[8,4,32,768]{3,2,1,0:T(8,128)(2,1)} collective-permute-done((bf16[8,4,32,768]{3,2,1,0:T(8,128)(2,1)S(1)}, bf16[8,4,32,768]{3,2,1,0:T(8,128)(2,1)}, u32[]{:S(2)}, u32[]{:S(2)}) %collective-permute-start.14) | collective-permute-done | bytes 1572896 | tf_op jit(solution)/shard_map/ppermute | solution.py:33
  205.8 16.7 %collective-permute-done.13 = bf16[512,768]{1,0:T(8,128)(2,1)S(1)} collective-permute-done((bf16[512,768]{1,0:T(8,128)(2,1)}, bf16[512,768]{1,0:T(8,128)(2,1)S(1)}, u32[]{:S(2)}, u32[]{:S(2)}) %collective-permute-start.13) | collective-permute-done | bytes 786464 | tf_op jit(solution)/shard_map/ppermute | solution.py:33
  229.2 10.2 %expert_step.5 = (bf16[8,4,32,768]{3,2,1,0:T(8,128)(2,1)}, bf16[8,4,32,768]{3,2,1,0:T(8,128)(2,1)}, bf16[8,4,32,768]{3,2,1,0:T(8,128)(2,1)}, bf16[8,4,32,768]{3,2,1,0:T(8,128)(2,1)}) custom-call(bf16[8,4,32,768]{3,2,1,0:T(8,128)(2,1)} %bitcast.38.x_ref.refs_2_, bf16[8,4,32,768]{3,2,1,0:T(8,128)(2,1)} %bitcast.124, bf16[4,768,768]{2,1,0:T(8,128)(2,1)} %first_ref.7, ...), custom_call_target="tpu_custom_call" | custom-call | flops 4831838 | bytes 18874 | tf_op jit(solution)/shard_map/expert_step/pallas_call | solution.py:538
  239.4 10.8 %all-to-all-done.5 = bf16[8,128,768]{2,1,0:T(8,128)(2,1)S(1)} async-done(((bf16[8,128,768]{2,1,0:T(8,128)(2,1)}), bf16[8,128,768]{2,1,0:T(8,128)(2,1)S(1)}, u32[]{:S(2)}, u32[]{:S(2)}) %all-to-all-start.5) | async-done | bytes 1572896 | tf_op jit(solution)/shard_map/all_to_all | solution.py:37
  251.3 10.1 %expert_step.6 = (bf16[8,4,32,768]{3,2,1,0:T(8,128)(2,1)}, bf16[8,4,32,768]{3,2,1,0:T(8,128)(2,1)}, bf16[8,4,32,768]{3,2,1,0:T(8,128)(2,1)}, bf16[8,4,32,768]{3,2,1,0:T(8,128)(2,1)}) custom-call(bf16[8,4,32,768]{3,2,1,0:T(8,128)(2,1)} %bitcast.129, bf16[8,4,32,768]{3,2,1,0:T(8,128)(2,1)} %collective-permute-done.14.gy_ref.refs_7_, ...), custom_call_target="tpu_custom_call" | custom-call | flops 4831838 | bytes 18874 | tf_op jit(solution)/shard_map/expert_step/pallas_call | solution.py:538
  265.4 20.6 %all-to-all-done.6 = bf16[8,128,768]{2,1,0:T(8,128)(2,1)S(1)} async-done(((bf16[8,128,768]{2,1,0:T(8,128)(2,1)}), bf16[8,128,768]{2,1,0:T(8,128)(2,1)S(1)}, u32[]{:S(2)}, u32[]{:S(2)}) %all-to-all-start.6) | async-done | bytes 1572896 | tf_op jit(solution)/shard_map/all_to_all | solution.py:37
  291.6 10.5 %collective-permute-done.15 = bf16[8,4,32,768]{3,2,1,0:T(8,128)(2,1)} collective-permute-done((bf16[8,4,32,768]{3,2,1,0:T(8,128)(2,1)}, bf16[8,4,32,768]{3,2,1,0:T(8,128)(2,1)}, u32[]{:S(2)}, u32[]{:S(2)}) %collective-permute-start.15) | collective-permute-done | bytes 1572896 | tf_op jit(solution)/shard_map/ppermute | solution.py:33
  302.1 10.2 %expert_step.7 = (bf16[8,4,32,768]{3,2,1,0:T(8,128)(2,1)}, bf16[8,4,32,768]{3,2,1,0:T(8,128)(2,1)}, bf16[8,4,32,768]{3,2,1,0:T(8,128)(2,1)}, bf16[8,4,32,768]{3,2,1,0:T(8,128)(2,1)}) custom-call(bf16[8,4,32,768]{3,2,1,0:T(8,128)(2,1)} %collective-permute-done.12.x_ref.refs_1_, bf16[8,4,32,768]{3,2,1,0:T(8,128)(2,1)} %collective-permute-done.9.gy_ref.refs_5_, ...), custom_call_target="tpu_custom_call" | custom-call | flops 4831838 | bytes 18874 | tf_op jit(solution)/shard_map/expert_step/pallas_call | solution.py:538
  316.4 20.7 %all-to-all-done.8 = bf16[8,128,768]{2,1,0:T(8,128)(2,1)S(1)} async-done(((bf16[8,128,768]{2,1,0:T(8,128)(2,1)}), bf16[8,128,768]{2,1,0:T(8,128)(2,1)S(1)}, u32[]{:S(2)}, u32[]{:S(2)}) %all-to-all-start.8) | async-done | bytes 1572896 | tf_op jit(solution)/shard_map/all_to_all | solution.py:37
  350.6 17.6 %expert_grads.1 = (f32[4,768,768]{2,1,0:T(8,128)}, f32[4,768,768]{2,1,0:T(8,128)}) custom-call(bf16[8,4,32,768]{3,2,1,0:T(8,128)(2,1)} %bitcast.127, bf16[8,4,32,768]{3,2,1,0:T(8,128)(2,1)} %collective-permute-done.12.x_ref.refs_1_, bf16[8,4,32,768]{3,2,1,0:T(8,128)(2,1)} %bitcast.38.x_ref.refs_2_, bf16[8,4,32,768]{3,2,1,0:T(8,128)(2,1)} %bitcast.130, ...), custom_call_target="tpu_custom_call" | custom-call | flops 9663676 | bytes 18874 | tf_op jit(solution)/shard_map/expert_grads/pallas_call | solution.py:566
  370.2 12.9 %collective-permute-done.17 = bf16[512,768]{1,0:T(8,128)(2,1)} collective-permute-done((bf16[512,768]{1,0:T(8,128)(2,1)}, bf16[512,768]{1,0:T(8,128)(2,1)}, u32[]{:S(2)}, u32[]{:S(2)}) %collective-permute-start.17) | collective-permute-done | bytes 786464 | tf_op jit(solution)/shard_map/ppermute | solution.py:33
  388.3 6.5 %turn.1 = (f32[512,768]{1,0:T(8,128)}, bf16[512,768]{1,0:T(8,128)(2,1)}, bf16[768,512]{1,0:T(8,128)(2,1)}, f32[128,768]{1,0:T(8,128)}) custom-call(bf16[1024,768]{1,0:T(8,128)(2,1)} %bitcast.137, bf16[512,768]{1,0:T(8,128)(2,1)} %add_convert_fusion.2.far_ref, s32[512,1]{1,0:T(8,128)} %copy.71.slot_ref, f32[512,768]{1,0:T(8,128)} %get-tuple-element.104.mid_ref, ...), custom_call_target="tpu_custom_call" | custom-call | flops 1409286 | bytes 4718 | tf_op jit(solution)/shard_map/turn/pallas_call | solution.py:380
  414.7 49.6 %attend_back.1 = (bf16[192,2048]{1,0:T(8,128)(2,1)}, bf16[384,2048]{1,0:T(8,128)(2,1)}, bf16[1,384,2048]{2,1,0:T(8,128)(2,1)}) custom-call(s32[16]{0:T(128)} %reshape.343.number_ref, s32[4]{0:T(128)} %iota_xor_fusion.order_ref, bf16[4,192,512]{2,1,0:T(8,128)(2,1)} %copy-done.15, f32[192,2048]{1,0:T(8,128)} %get-tuple-element.148.att_t_ref, ...), custom_call_target="tpu_custom_call" | custom-call | flops 48318384 | bytes 12582 | tf_op jit(solution)/shard_map/attend_back/pallas_call | solution.py:302
  469.2 6.8 %rows.1 = (bf16[576,2048]{1,0:T(8,128)(2,1)}, bf16[4,512,768]{2,1,0:T(8,128)(2,1)}) custom-call(s32[4]{0:T(128)} %iota_xor_fusion.order_ref, bf16[192,2048]{1,0:T(8,128)(2,1)} %get-tuple-element.150.gq_ref, bf16[384,2048]{1,0:T(8,128)(2,1)} %get-tuple-element.151.gown_ref, bf16[1,384,2048]{2,1,0:T(8,128)(2,1)} %bitcast.143, bf16[576,768]{1,0:T(8,128)(2,1)} %bitcast.133), custom_call_target="tpu_custom_call" | custom-call | flops 1811939 | bytes 6291 | tf_op jit(solution)/shard_map/rows/pallas_call | solution.py:434
  476.1 9.1 %weights.1 = bf16[2,4,96,768]{3,2,1,0:T(8,128)(2,1)} custom-call(s32[4]{0:T(128)} %iota_xor_fusion.order_ref, bf16[576,2048]{1,0:T(8,128)(2,1)} %get-tuple-element.153.cols_ref, f32[4,768]{1,0:T(4,128)} %bitcast.162, bf16[4,512,768]{2,1,0:T(8,128)(2,1)} %get-tuple-element.157.rows_ref, bf16[512,768]{1,0:T(8,128)(2,1)} %bitcast.119, ...), custom_call_target="tpu_custom_call" | custom-call | flops 1811939 | bytes 4718 | tf_op jit(solution)/shard_map/weights/pallas_call | solution.py:476
  505.3 9.9 %collective-permute-done.22 = bf16[136,768]{1,0:T(8,128)(2,1)S(1)} collective-permute-done((bf16[136,768]{1,0:T(8,128)(2,1)S(1)}, bf16[136,768]{1,0:T(8,128)(2,1)S(1)}, u32[]{:S(2)}, u32[]{:S(2)}) %collective-permute-start.22) | collective-permute-done | bytes 208928 | tf_op jit(solution)/shard_map/ppermute | solution.py:33
  541.1 12.6 %collective-permute-done.25 = bf16[512,768]{1,0:T(8,128)(2,1)S(1)} collective-permute-done((bf16[512,768]{1,0:T(8,128)(2,1)}, bf16[512,768]{1,0:T(8,128)(2,1)S(1)}, u32[]{:S(2)}, u32[]{:S(2)}) %collective-permute-start.25) | collective-permute-done | bytes 786464 | tf_op jit(solution)/shard_map/ppermute | solution.py:33
  (226 shorter events, 217.6 us)
Async XLA Ops:
  0.7 47.6 %collective-permute-start = (bf16[512,768]{1,0:T(8,128)(2,1)}, bf16[512,768]{1,0:T(8,128)(2,1)S(1)}, u32[]{:S(2)}, u32[]{:S(2)}) collective-permute-start(bf16[512,768]{1,0:T(8,128)(2,1)} %bitcast.114), channel_id=1, source_target_pairs={{0,8},{4,12},{8,0},{12,4},{16,24},{20,28},{24,16},{28,20},{1,9},{5... | collective-permute-start | bytes 2359304 | tf_op jit(solution)/shard_map/ppermute | solution.py:33
  3.7 44.7 %collective-permute-start.1 = (bf16[512,768]{1,0:T(8,128)(2,1)}, bf16[512,768]{1,0:T(8,128)(2,1)S(1)}, u32[]{:S(2)}, u32[]{:S(2)}) collective-permute-start(bf16[512,768]{1,0:T(8,128)(2,1)} %bitcast.115), channel_id=1, source_target_pairs={{0,16},{4,20},{8,24},{12,28},{16,0},{20,4},{24,8},{28,12},{1,17},{... | collective-permute-start | bytes 2359304 | tf_op jit(solution)/shard_map/ppermute | solution.py:33
  5.2 44.4 %collective-permute-start.2 = (bf16[512,768]{1,0:T(8,128)(2,1)}, bf16[512,768]{1,0:T(8,128)(2,1)}, u32[]{:S(2)}, u32[]{:S(2)}) collective-permute-start(bf16[512,768]{1,0:T(8,128)(2,1)} %bitcast.116), channel_id=1, source_target_pairs={{0,24},{4,28},{8,16},{12,20},{16,8},{20,12},{24,0},{28,4},{1,25},{... | collective-permute-start | bytes 2359304 | tf_op jit(solution)/shard_map/ppermute | solution.py:33
  37.4 39.3 %collective-permute-start.6 = (bf16[96,768]{1,0:T(8,128)(2,1)}, bf16[96,768]{1,0:T(8,128)(2,1)}, u32[]{:S(2)}, u32[]{:S(2)}) collective-permute-start(bf16[96,768]{1,0:T(8,128)(2,1)} %dynamic-slice_bitcast_fusion.4), channel_id=1, source_target_pairs={{0,1},{1,0},{2,3},{3,2},{4,5},{5,4},{6,7},{7,6},{8,9},{9,8},{10,11... | collective-permute-start | bytes 442376 | tf_op jit(solution)/shard_map/ppermute | solution.py:33
  37.4 39.3 %collective-permute-start.7 = (bf16[96,768]{1,0:T(8,128)(2,1)}, bf16[96,768]{1,0:T(8,128)(2,1)}, u32[]{:S(2)}, u32[]{:S(2)}) collective-permute-start(bf16[96,768]{1,0:T(8,128)(2,1)} %dynamic-slice_bitcast_fusion.4), channel_id=1, source_target_pairs={{0,2},{1,3},{2,0},{3,1},{4,6},{5,7},{6,4},{7,5},{8,10},{9,11},{10,... | collective-permute-start | bytes 442376 | tf_op jit(solution)/shard_map/ppermute | solution.py:33
  48.4 41.6 %collective-permute-start.5 = (bf16[512,768]{1,0:T(8,128)(2,1)}, bf16[512,768]{1,0:T(8,128)(2,1)}, u32[]{:S(2)}, u32[]{:S(2)}) collective-permute-start(bf16[512,768]{1,0:T(8,128)(2,1)} %bitcast.14.cot_ref), channel_id=1, source_target_pairs={{0,2},{1,3},{2,0},{3,1},{4,6},{5,7},{6,4},{7,5},{8,10},{9,11},{10,... | collective-permute-start | bytes 2359304 | tf_op jit(solution)/shard_map/ppermute | solution.py:33
  55.1 38.2 %all-to-all-start = ((bf16[8,128,768]{2,1,0:T(8,128)(2,1)}), bf16[8,128,768]{2,1,0:T(8,128)(2,1)S(1)}, u32[]{:S(2)}, u32[]{:S(2)}) async-start(bf16[8,128,768]{2,1,0:T(8,128)(2,1)} %bitcast.145), calls=%async_computation | async-start | bytes 3145728 | tf_op jit(solution)/shard_map/all_to_all | solution.py:37
  93.4 34.8 %all-to-all-start.1 = ((bf16[8,128,768]{2,1,0:T(8,128)(2,1)}), bf16[8,128,768]{2,1,0:T(8,128)(2,1)S(1)}, u32[]{:S(2)}, u32[]{:S(2)}) async-start(bf16[8,128,768]{2,1,0:T(8,128)(2,1)} %bitcast.146), calls=%async_computation.1 | async-start | bytes 3145728 | tf_op jit(solution)/shard_map/all_to_all | solution.py:37
  97.3 38.5 %collective-permute-start.9 = (bf16[8,4,32,768]{3,2,1,0:T(8,128)(2,1)S(1)}, bf16[8,4,32,768]{3,2,1,0:T(8,128)(2,1)}, u32[]{:S(2)}, u32[]{:S(2)}) collective-permute-start(bf16[8,4,32,768]{3,2,1,0:T(8,128)(2,1)S(1)} %bitcast.120), channel_id=1, source_target_pairs={{0,1},{1,0},{2,3},{3,2},{4,5},{5,4},{6,7},{7,6},{8,9},{9,8},{10,11... | collective-permute-start | bytes 4718600 | tf_op jit(solution)/shard_map/ppermute | solution.py:33
  103.4 29.0 %collective-permute-start.10 = (bf16[4,96,768]{2,1,0:T(8,128)(2,1)}, bf16[4,96,768]{2,1,0:T(8,128)(2,1)}, u32[]{:S(2)}, u32[]{:S(2)}) collective-permute-start(bf16[4,96,768]{2,1,0:T(8,128)(2,1)} %pad_maximum_fusion.3), channel_id=1, source_target_pairs={{0,4},{4,0},{8,12},{12,8},{16,20},{20,16},{24,28},{28,24},{1,5},{5... | collective-permute-start | bytes 1769480 | tf_op jit(solution)/shard_map/ppermute | solution.py:33
  151.0 37.5 %collective-permute-start.11 = (bf16[512,768]{1,0:T(8,128)(2,1)}, bf16[512,768]{1,0:T(8,128)(2,1)}, u32[]{:S(2)}, u32[]{:S(2)}) collective-permute-start(bf16[512,768]{1,0:T(8,128)(2,1)} %get-tuple-element.108), channel_id=1, source_target_pairs={{0,2},{1,3},{2,0},{3,1},{4,6},{5,7},{6,4},{7,5},{8,10},{9,11},{10,... | collective-permute-start | bytes 2359304 | tf_op jit(solution)/shard_map/ppermute | solution.py:33
  151.6 54.2 %collective-permute-start.14 = (bf16[8,4,32,768]{3,2,1,0:T(8,128)(2,1)S(1)}, bf16[8,4,32,768]{3,2,1,0:T(8,128)(2,1)}, u32[]{:S(2)}, u32[]{:S(2)}) collective-permute-start(bf16[8,4,32,768]{3,2,1,0:T(8,128)(2,1)S(1)} %bitcast.123), channel_id=1, source_target_pairs={{0,1},{1,0},{2,3},{3,2},{4,5},{5,4},{6,7},{7,6},{8,9},{9,8},{10,11... | collective-permute-start | bytes 4718600 | tf_op jit(solution)/shard_map/ppermute | solution.py:33
  191.8 32.9 %all-to-all-start.4 = ((bf16[8,128,768]{2,1,0:T(8,128)(2,1)}), bf16[8,128,768]{2,1,0:T(8,128)(2,1)}, u32[]{:S(2)}, u32[]{:S(2)}) async-start(bf16[8,128,768]{2,1,0:T(8,128)(2,1)} %bitcast.149), calls=%async_computation.4 | async-start | bytes 3145728 | tf_op jit(solution)/shard_map/all_to_all | solution.py:37
  196.2 26.3 %collective-permute-start.13 = (bf16[512,768]{1,0:T(8,128)(2,1)}, bf16[512,768]{1,0:T(8,128)(2,1)S(1)}, u32[]{:S(2)}, u32[]{:S(2)}) collective-permute-start(bf16[512,768]{1,0:T(8,128)(2,1)} %collective-permute-done.11), channel_id=1, source_target_pairs={{0,1},{1,0},{2,3},{3,2},{4,5},{5,4},{6,7},{7,6},{8,9},{9,8},{10,11... | collective-permute-start | bytes 2359304 | tf_op jit(solution)/shard_map/ppermute | solution.py:33
  196.3 65.2 %collective-permute-start.12 = (bf16[8,4,32,768]{3,2,1,0:T(8,128)(2,1)S(1)}, bf16[8,4,32,768]{3,2,1,0:T(8,128)(2,1)}, u32[]{:S(2)}, u32[]{:S(2)}) collective-permute-start(bf16[8,4,32,768]{3,2,1,0:T(8,128)(2,1)S(1)} %bitcast.128), channel_id=1, source_target_pairs={{0,1},{1,0},{2,3},{3,2},{4,5},{5,4},{6,7},{7,6},{8,9},{9,8},{10,11... | collective-permute-start | bytes 4718600 | tf_op jit(solution)/shard_map/ppermute | solution.py:33
  265.1 37.0 %collective-permute-start.15 = (bf16[8,4,32,768]{3,2,1,0:T(8,128)(2,1)}, bf16[8,4,32,768]{3,2,1,0:T(8,128)(2,1)}, u32[]{:S(2)}, u32[]{:S(2)}) collective-permute-start(bf16[8,4,32,768]{3,2,1,0:T(8,128)(2,1)} %get-tuple-element.122), channel_id=1, source_target_pairs={{0,1},{1,0},{2,3},{3,2},{4,5},{5,4},{6,7},{7,6},{8,9},{9,8},{10,11... | collective-permute-start | bytes 4718600 | tf_op jit(solution)/shard_map/ppermute | solution.py:33
  338.3 48.8 %all-to-all-start.9 = ((bf16[8,128,768]{2,1,0:T(8,128)(2,1)}), bf16[8,128,768]{2,1,0:T(8,128)(2,1)S(1)}, u32[]{:S(2)}, u32[]{:S(2)}) async-start(bf16[8,128,768]{2,1,0:T(8,128)(2,1)} %bitcast.43), calls=%async_computation.9 | async-start | bytes 3145728 | tf_op jit(solution)/shard_map/all_to_all | solution.py:37
  345.3 37.8 %collective-permute-start.17 = (bf16[512,768]{1,0:T(8,128)(2,1)}, bf16[512,768]{1,0:T(8,128)(2,1)}, u32[]{:S(2)}, u32[]{:S(2)}) collective-permute-start(bf16[512,768]{1,0:T(8,128)(2,1)} %add_convert_fusion.3), channel_id=1, source_target_pairs={{0,2},{1,3},{2,0},{3,1},{4,6},{5,7},{6,4},{7,5},{8,10},{9,11},{10,... | collective-permute-start | bytes 2359304 | tf_op jit(solution)/shard_map/ppermute | solution.py:33
  348.0 36.7 %collective-permute-start.18 = (bf16[512,768]{1,0:T(8,128)(2,1)}, bf16[512,768]{1,0:T(8,128)(2,1)}, u32[]{:S(2)}, u32[]{:S(2)}) collective-permute-start(bf16[512,768]{1,0:T(8,128)(2,1)} %fusion.25), channel_id=1, source_target_pairs={{0,1},{1,0},{2,3},{3,2},{4,5},{5,4},{6,7},{7,6},{8,9},{9,8},{10,11... | collective-permute-start | bytes 2359304 | tf_op jit(solution)/shard_map/ppermute | solution.py:33
  409.8 78.8 %all-to-all-start.11 = ((bf16[8,496,768]{2,1,0:T(8,128)(2,1)}), bf16[8,496,768]{2,1,0:T(8,128)(2,1)}, u32[]{:S(2)}, u32[]{:S(2)}) async-start(bf16[8,496,768]{2,1,0:T(8,128)(2,1)} %pad_maximum_fusion), calls=%async_computation.11 | async-start | bytes 12189696 | tf_op jit(solution)/shard_map/all_to_all | solution.py:37
  488.6 42.0 %all-to-all-start.12 = ((bf16[4,512,768]{2,1,0:T(8,128)(2,1)}), bf16[4,512,768]{2,1,0:T(8,128)(2,1)}, u32[]{:S(2)}, u32[]{:S(2)}) async-start(bf16[4,512,768]{2,1,0:T(8,128)(2,1)} %get-tuple-element.157.rows_ref), calls=%async_computation.12 | async-start | bytes 6291456 | tf_op jit(solution)/shard_map/all_to_all | solution.py:37
  520.1 33.6 %collective-permute-start.25 = (bf16[512,768]{1,0:T(8,128)(2,1)}, bf16[512,768]{1,0:T(8,128)(2,1)S(1)}, u32[]{:S(2)}, u32[]{:S(2)}) collective-permute-start(bf16[512,768]{1,0:T(8,128)(2,1)} %fusion.26), channel_id=1, source_target_pairs={{0,1},{1,0},{2,3},{3,2},{4,5},{5,4},{6,7},{7,6},{8,9},{9,8},{10,11... | collective-permute-start | bytes 2359304 | tf_op jit(solution)/shard_map/ppermute | solution.py:33
  522.1 37.2 %collective-permute-start.24 = (bf16[512,768]{1,0:T(8,128)(2,1)}, bf16[512,768]{1,0:T(8,128)(2,1)}, u32[]{:S(2)}, u32[]{:S(2)}) collective-permute-start(bf16[512,768]{1,0:T(8,128)(2,1)} %fusion.24), channel_id=1, source_target_pairs={{0,2},{1,3},{2,0},{3,1},{4,6},{5,7},{6,4},{7,5},{8,10},{9,11},{10,... | collective-permute-start | bytes 2359304 | tf_op jit(solution)/shard_map/ppermute | solution.py:33
  531.8 30.0 %all-to-all-start.13 = ((bf16[8,120,768]{2,1,0:T(8,128)(2,1)}), bf16[8,120,768]{2,1,0:T(8,128)(2,1)S(1)}, u32[]{:S(2)}, u32[]{:S(2)}) async-start(bf16[8,120,768]{2,1,0:T(8,128)(2,1)} %broadcast_in_dim.11), calls=%async_computation.13 | async-start | bytes 2949120 | tf_op jit(solution)/shard_map/all_to_all | solution.py:37
  (51 other events, 492.2 us)
